TPU v7x, 128 devices: a whole 4x4x4 slice. The times are simulated.
128 devices in a mesh: grp: 4 (over z), sub: 32 (over x, y, core).
Axes of the slice: x: 4, y: 4, z: 4, core: 2. Of those that a mesh axis runs over, the one named last changes fastest.
Arguments:
- three_centre: bfloat16 [64, 8192, 512], P('grp', 'sub'), may hold values from -6 to 6
- pair_blocks: int32 [32, 2], P('sub'), may hold values from 0 to 31, all different within a row
- green_occ: bfloat16 [8192, 1024], P('sub', 'grp'), may hold values from -0.25 to 0.25
- occ_mask: int32 [32, 4], P('sub', 'grp'), may hold values 0 or 1
- green_virt: bfloat16 [1024, 8192], P('grp', 'sub'), may hold values from -0.0625 to 0.0625
- virt_mask: int32 [4, 32], P('grp', 'sub'), may hold values 0 or 1
- owner: int32 [64, 1], replicated, may hold values from 0 to 31; in each aligned block of 64 rows (0 to 63, 64 to 127, ...) at most 3 rows name the same one
Outputs:
- products: float32 [4, 96, 256, 256], P('grp', 'sub')
Inputs may be any that keep to these rules, and one draw needn't show every extreme that they name: `pair_blocks`: the 2 partner blocks of a basis block are distinct, and every basis block is some block's partner. No index is the owner of more than 3 RI functions of the slab, and one owns exactly 3.
All inputs are finite; a program needn't handle non-finite values. No bound on the sum of `occ_mask` or of `virt_mask` on one device may be relied on, other than what follows from the above.
Results may differ from a plain program's by a relative error of at most 0.0029.
Values may be sent and summed in bfloat16 or wider, within the bound.
No kernel may reach another device: no remote copies, remote signals or barrier semaphores. Data moves between devices by JAX's collectives and lax.ppermute only.
A program may use at most 128 MiB of HBM per device.

v0:
```python
import jax
import jax.numpy as jnp
from jax import lax
from jax.sharding import PartitionSpec as P

CAP = 3


def per_device(three_centre, pair_blocks, green_occ, occ_mask, green_virt, virt_mask, owner):
    block_size = green_occ.shape[1]
    partners = pair_blocks.shape[1]
    sub_count = lax.axis_size("sub")
    slab_total = owner.shape[0]
    slot_total = sub_count * CAP
    occ_local = green_occ * occ_mask[0, 0].astype(green_occ.dtype)
    occ_whole = lax.all_gather(occ_local, "sub", axis=0, tiled=True)
    picked = jnp.concatenate(
        [
            lax.dynamic_slice_in_dim(occ_whole, pair_blocks[0, part] * block_size, block_size, 0)
            for part in range(partners)
        ],
        axis=0,
    )
    piece = lax.all_gather(three_centre, "grp", axis=0, tiled=True)
    count = piece.shape[0]
    flat = piece.reshape(count * block_size, partners * block_size)
    result = jnp.dot(flat, picked, preferred_element_type=jnp.float32)
    half = result.astype(jnp.bfloat16).reshape(count, block_size, block_size)
    owner_flat = owner[:, 0]
    numbers = jnp.arange(slab_total, dtype=jnp.int32)
    earlier = (owner_flat[None, :] == owner_flat[:, None]) & (numbers[None, :] < numbers[:, None])
    position = jnp.sum(earlier.astype(jnp.int32), axis=1)
    slots = owner_flat * CAP + position
    match = (slots[None, :] == jnp.arange(slot_total, dtype=jnp.int32)[:, None]).astype(jnp.int32)
    filled = jnp.sum(match, axis=1) > 0
    source = jnp.sum(match * numbers[None, :], axis=1)
    virt_local = green_virt * virt_mask[0, 0].astype(green_virt.dtype)
    outgoing = jnp.where(filled[:, None, None], half[source], jnp.zeros((), jnp.bfloat16))
    outgoing = outgoing.reshape(sub_count, CAP, block_size, block_size)
    virt_whole = lax.all_gather(virt_local, "sub", axis=1, tiled=True)
    virt_split = virt_whole.reshape(block_size, sub_count, block_size)
    owned = jnp.einsum(
        "sjm,jkml->ksl",
        virt_split,
        lax.all_to_all(outgoing, "sub", split_axis=0, concat_axis=0, tiled=True),
        preferred_element_type=jnp.float32,
    )
    return owned.reshape(1, CAP, block_size, block_size)


def solution(mesh):
    in_specs = (
        P("grp", "sub", None),
        P("sub", None),
        P("sub", "grp"),
        P("sub", "grp"),
        P("grp", "sub"),
        P("grp", "sub"),
        P(),
    )
    out_specs = P("grp", "sub", None, None)
    return jax.shard_map(
        per_device, mesh=mesh, in_specs=in_specs, out_specs=out_specs, check_vma=False
    )
```

profile of v0, /device:TPU:12, one launch (start us, length us, event | category | flops | bytes accessed | tf_op | source)
XLA Modules:
  0.0 494.7 jit_solution(17360266964634942005)
XLA Ops:
  6.5 0.0 all-gather.4.cloned.1.call-start
  7.2 1.6 broadcast_multiply_fusion.1
  8.8 0.0 all-gather.4.cloned.1.call-update
  8.8 0.0 all-gather.6.cloned.1.call-start
  8.8 0.7 all-gather.6.cloned.1.call-update
  9.5 1.3 fusion.7
  12.1 0.9 convert_reduce_fusion.1
  13.1 0.7 multiply_add_fusion
  13.7 0.1 convert_reduce_fusion
  13.8 0.1 gt.11
  14.0 42.0 %all-gather.4.cloned.1.call-done = bf16[8192,256]{1,0:T(8,128)(2,1)} async-done(((bf16[256,256]{1,0:T(8,128)(2,1)}), bf16[8192,256]{1,0:T(8,128)(2,1)}) %all-gather.4.cloned.1.call-update) | async-done | bytes 4194320 | tf_op jit(solution)/shard_map/all_gather | solution.py:16
  56.0 1.0 constant_dynamic-slice_fusion.1
  57.0 156.1 %all-gather.6.cloned.1.call-done = bf16[64,256,512]{2,1,0:T(8,128)(2,1)} async-done(((bf16[16,256,512]{2,1,0:T(8,128)(2,1)}), bf16[64,256,512]{2,1,0:T(8,128)(2,1)}) %all-gather.6.cloned.1.call-update) | async-done | bytes 16777232 | tf_op jit(solution)/shard_map/all_gather | solution.py:24
  213.1 10.2 %fusion = bf16[16384,256]{0,1:T(8,128)(2,1)} fusion(bf16[16384,512]{1,0:T(8,128)(2,1)} %bitcast.31, bf16[256,256]{1,0:T(8,128)(2,1)S(1)} %get-tuple-element.8, bf16[256,256]{1,0:T(8,128)(2,1)S(1)} %get-tuple-element.7), kind=kOutput, calls=%fused_computation.2 | convolution fusion | flops 4299685888 | bytes 25427968 | tf_op jit(solution)/shard_map/dot_general | solution.py:27
  223.3 11.9 %copy.28 = bf16[16384,256]{1,0:T(8,128)(2,1)} copy(bf16[16384,256]{0,1:T(8,128)(2,1)} %fusion) | data formatting | bytes 16777216 | tf_op jit(solution)/shard_map/reshape | solution.py:28
  235.2 10.2 %gather_fusion = bf16[96,256,256]{2,1,0:T(8,128)(2,1)} fusion(bf16[64,256,256]{2,1,0:T(8,128)(2,1)} %bitcast.29, s32[1024]{0:T(1024)S(1)} %pad_clamp_fusion), kind=kCustom, calls=%fused_computation | custom fusion | bytes 25166208 | tf_op jit(solution)/shard_map/gather | solution.py:38
  245.4 10.6 %broadcast_select_fusion = bf16[32,3,256,256]{3,2,1,0:T(8,128)(2,1)} fusion(bf16[32,3,256,256]{3,2,1,0:T(8,128)(2,1)} %bitcast.30, pred[32,3]{1,0:T(8,128)(4,1)S(1)} %gt.11), kind=kLoop, calls=%fused_computation.3 | loop fusion | flops 6291456 | bytes 25165920 | tf_op jit(solution)/shard_map/jit(_where)/select_n | solution.py:38
  256.0 16.6 %copy.23 = bf16[32,3,256,256]{2,3,1,0:T(8,128)(2,1)} copy(bf16[32,3,256,256]{3,2,1,0:T(8,128)(2,1)} %broadcast_select_fusion) | data formatting | bytes 25165824 | tf_op jit(solution)/shard_map/jit(_where)/select_n | solution.py:38
  272.7 0.0 copy-start
  272.7 7.6 %all-to-all-start = ((bf16[32,3,256,256]{2,3,1,0:T(8,128)(2,1)}), bf16[32,3,256,256]{2,3,1,0:T(8,128)(2,1)}, u32[]{:S(2)}, u32[]{:S(2)}) async-start(bf16[32,3,256,256]{2,3,1,0:T(8,128)(2,1)} %copy.23), calls=%async_computation | async-start | bytes 25165824 | tf_op jit(solution)/shard_map/all_to_all | solution.py:45
  280.2 0.0 all-gather.8.cloned.1.call-start
  280.3 0.0 copy-done
  280.3 0.1 copy.24
  281.1 0.7 broadcast_multiply_fusion
  281.7 0.0 all-gather.8.cloned.1.call-update
  281.8 149.8 %all-gather.8.cloned.1.call-done = bf16[256,8192]{0,1:T(8,128)(2,1)} async-done(((bf16[256,256]{0,1:T(8,128)(2,1)}), bf16[256,8192]{0,1:T(8,128)(2,1)}) %all-gather.8.cloned.1.call-update) | async-done | bytes 4194320 | tf_op jit(solution)/shard_map/all_gather | solution.py:40
  431.5 47.9 %all-to-all-done = bf16[32,3,256,256]{2,3,1,0:T(8,128)(2,1)} async-done(((bf16[32,3,256,256]{2,3,1,0:T(8,128)(2,1)}), bf16[32,3,256,256]{2,3,1,0:T(8,128)(2,1)}, u32[]{:S(2)}, u32[]{:S(2)}) %all-to-all-start) | async-done | bytes 12582944 | tf_op jit(solution)/shard_map/all_to_all | solution.py:45
  479.4 7.6 %convolution_bitcast_fusion = f32[1,3,256,256]{2,3,1,0:T(8,128)S(1)} fusion(bf16[32,3,256,256]{2,3,1,0:T(8,128)(2,1)} %all-to-all-done, bf16[256,32,256,1]{0,2,3,1:T(8,128)(2,1)} %bitcast.32), kind=kOutput, calls=%fused_computation.4 | convolution fusion | flops 3221225472 | bytes 17563648 | tf_op jit(solution)/shard_map/sjm,jkml->ksl/dot_general | solution.py:42
  487.0 1.1 copy.26
  (3 shorter events, 0.0 us)
Async XLA Ops:
  6.5 49.4 %all-gather.4.cloned.1.call-start = ((), (), s32[]{:S(2)}) async-start(), calls=%async_computation.1 | async-start | bytes 4325376 | tf_op jit(solution)/shard_map/all_gather | solution.py:16
  8.8 204.3 %all-gather.6.cloned.1.call-start = ((), (), s32[]{:S(2)}) async-start(), calls=%async_computation.2 | async-start | bytes 20971520 | tf_op jit(solution)/shard_map/all_gather | solution.py:24
  272.7 7.6 %copy-start = (bf16[256,256]{1,0:T(8,128)(2,1)S(1)}, bf16[256,256]{1,0:T(8,128)(2,1)}, u32[]{:S(2)}) copy-start(bf16[256,256]{1,0:T(8,128)(2,1)} %param.11) | copy-start | bytes 393220
  272.7 206.7 %all-to-all-start = ((bf16[32,3,256,256]{2,3,1,0:T(8,128)(2,1)}), bf16[32,3,256,256]{2,3,1,0:T(8,128)(2,1)}, u32[]{:S(2)}, u32[]{:S(2)}) async-start(bf16[32,3,256,256]{2,3,1,0:T(8,128)(2,1)} %copy.23), calls=%async_computation | async-start | bytes 25165824 | tf_op jit(solution)/shard_map/all_to_all | solution.py:45
  280.2 151.3 %all-gather.8.cloned.1.call-start = ((), (), s32[]{:S(2)}) async-start(), calls=%async_computation.3 | async-start | bytes 4325376 | tf_op jit(solution)/shard_map/all_gather | solution.py:40
Sparse Core Ops, SparseCore 0:
  9.6 46.3 all-gather.3
  57.6 155.4 all-gather.5
  283.3 148.1 all-gather.7
where the time goes:
time: 496 us; the launch traced here: 495 us
  waiting for transfers between devices  397 us (80%)
  local copies, waits for them, and re-layouts  42.4 us (9%)
  matrix products  17.8 us (4%)
  between operations  15.7 us (3%)
  other arithmetic  14.6 us (3%)
  starting transfers between devices  7.66 us (2%)
    all_gather x1, waiting for transfers between devices, per_device(): piece = lax.all_gather(three_centre, 'grp', axis=0, tiled=True)  156 us
    all_gather x1, waiting for transfers between devices, per_device(): virt_whole = lax.all_gather(virt_local, 'sub', axis=1, tiled=True)  150 us
    all_to_all x1, waiting for transfers between devices, per_device(): lax.all_to_all(outgoing, 'sub', split_axis=0, concat_axis=0, tiled=True)  47.9 us
    all_gather x1, waiting for transfers between devices, per_device(): occ_whole = lax.all_gather(occ_local, 'sub', axis=0, tiled=True)  42 us
    select_n x1, local copies, waits for them, and re-layouts, per_device(): jnp.where(filled[:, None, None], half[source], jnp.zeros((), jnp.bfloat16))  16.6 us
    reshape x1, local copies, waits for them, and re-layouts, per_device(): half = result.astype(jnp.bfloat16).reshape(count, block_size, block_size)  11.9 us
    select_n x1, other arithmetic, per_device(): jnp.where(filled[:, None, None], half[source], jnp.zeros((), jnp.bfloat16))  10.6 us
    gather x1, local copies, waits for them, and re-layouts, per_device(): half[source]  10.2 us
  transfers between devices with their start and end apart: 4, of which 4 were waited for; matrix products, arithmetic and copies ran while one was open for 1% of the time, Pallas kernels for 0%

commit v1 on v0

v1 whole, which is shorter than its diff:
```python
import functools

import jax
import jax.numpy as jnp
from jax import lax
from jax.experimental import pallas as pl
from jax.experimental.pallas import tpu as pltpu
from jax.sharding import PartitionSpec as P

CAP = 3
AXES = ("grp", "sub")
BF = jnp.bfloat16
F32 = jnp.float32
SWAP = (0, 2, 1, 3)


def pairs(target):
    out = []
    for z in range(4):
        for x in range(4):
            for y in range(4):
                for c in range(2):
                    tz, tx, ty, tc = target(z, x, y, c)
                    out.append((z * 32 + (x * 4 + y) * 2 + c, tz * 32 + (tx * 4 + ty) * 2 + tc))
    return out


def first(c):
    return 1 if c == 0 else 3


CORE = pairs(lambda z, x, y, c: (z, x, y, 1 - c))
Z1 = pairs(lambda z, x, y, c: (z ^ first(c), x, y, c))
Z2 = pairs(lambda z, x, y, c: (z ^ first(1 - c), x, y, c))
X_A = pairs(lambda z, x, y, c: (z, x ^ first(c), y, c))
X_B = pairs(lambda z, x, y, c: (z, x ^ first(1 - c), y, c))
Y_A = pairs(lambda z, x, y, c: (z, x, y ^ first(c), c))
Y_B = pairs(lambda z, x, y, c: (z, x, y ^ first(1 - c), c))


def on(axis0, e):
    def target(z, x, y, c):
        return (z, x ^ e, y, c) if (c == axis0) else (z, x, y ^ e, c)

    return pairs(target)


def move(value, permutation):
    return lax.ppermute(value, AXES, permutation)


def place(d, e):
    return jnp.where(d == 0, 0, jnp.where(d == 2, 3, jnp.where(d == e, 1, 2)))


def ring_order(q, e):
    return [q ^ 2, q ^ e, q ^ (4 - e), q]


def products_body(sc, t_own, t_oth, go_own, go_oth, gv_own, gv_oth, send, keep, gvp, half):
    @pl.when(pl.program_id(0) == 0)
    def _():
        for k in range(16):
            rows = pl.ds(pl.multiple_of(sc[1 + k] * 16, 16), 16)
            for g in range(4):
                gvp[g, k * 16 : (k + 1) * 16, 0:256] = gv_own[g, rows, :]
                gvp[g, k * 16 : (k + 1) * 16, 256:512] = gv_oth[SWAP[g], rows, :]

    for g in range(4):
        half[0:256, :] = jnp.dot(t_own[0], go_own[g], preferred_element_type=F32).astype(BF)
        half[256:512, :] = jnp.dot(t_oth[0], go_oth[SWAP[g]], preferred_element_type=F32).astype(BF)
        out = jnp.dot(gvp[g], half[...], preferred_element_type=F32)
        send[0, g] = out[0:128].astype(BF)
        keep[0, g] = out[128:256]


def products_of(part, scalars, t_own, t_oth, go_own, go_oth, gv_own, gv_oth):
    whole = lambda shape: pl.BlockSpec(shape, lambda p, sc: (0,) * len(shape))
    return pl.pallas_call(
        products_body,
        grid_spec=pltpu.PrefetchScalarGridSpec(
            num_scalar_prefetch=1,
            grid=(4,),
            in_specs=[
                pl.BlockSpec((1, 256, 512), lambda p, sc: (sc[0] * 8 + part * 4 + p, 0, 0)),
                pl.BlockSpec((1, 256, 512), lambda p, sc: (part * 4 + p, 0, 0)),
                whole((4, 512, 256)),
                whole((4, 512, 256)),
                whole((4, 256, 256)),
                whole((4, 256, 256)),
            ],
            out_specs=[
                pl.BlockSpec((1, 4, 128, 256), lambda p, sc: (p, 0, 0, 0)),
                pl.BlockSpec((1, 4, 128, 256), lambda p, sc: (p, 0, 0, 0)),
            ],
            scratch_shapes=[pltpu.VMEM((4, 256, 512), BF), pltpu.VMEM((512, 256), BF)],
        ),
        out_shape=[
            jax.ShapeDtypeStruct((4, 4, 128, 256), BF),
            jax.ShapeDtypeStruct((4, 4, 128, 256), F32),
        ],
        compiler_params=pltpu.CompilerParams(vmem_limit_bytes=32 * 1024 * 1024),
        cost_estimate=pl.CostEstimate(flops=3_300_000_000, bytes_accessed=12_000_000, transcendentals=0),
    )(scalars, t_own, t_oth, go_own, go_oth, gv_own, gv_oth)


def slots_body(sc, mine, other, out):
    for s in range(32 * CAP):
        at = sc[s]

        @pl.when(at < 0)
        def _():
            out[s] = jnp.zeros_like(out[s])

        @pl.when((at >= 0) & (at < 32))
        def _():
            out[s] = mine[jnp.clip(at, 0, 31)]

        @pl.when(at >= 32)
        def _():
            out[s] = other[jnp.clip(at - 32, 0, 31)]


def fill_slots(source, mine, other):
    whole = lambda shape: pl.BlockSpec(shape, lambda i, sc: (0,) * len(shape))
    return pl.pallas_call(
        slots_body,
        grid_spec=pltpu.PrefetchScalarGridSpec(
            num_scalar_prefetch=1,
            grid=(1,),
            in_specs=[whole((32, 8, 256)), whole((32, 8, 256))],
            out_specs=whole((32 * CAP, 8, 256)),
        ),
        out_shape=jax.ShapeDtypeStruct((32 * CAP, 8, 256), F32),
    )(source, mine, other)


def reduce_steps(send, keep, steps):
    got = []
    begin = 0
    for number, step in enumerate(steps):
        if number:
            size = 128 >> number
            total = keep[:, :, begin : begin + size]
            offset = begin
            for level, part in enumerate(got):
                total = total + part[:, :, offset : offset + size].astype(F32)
                offset -= 64 >> level
            send = total.astype(BF)
            begin += size
        got.append(move(send, step))
    total = keep[:, :, begin : begin + 16]
    offset = begin
    for level, part in enumerate(got):
        total = total + part[:, :, offset : offset + 16].astype(F32)
        offset -= 64 >> level
    return total


def per_device(three_centre, pair_blocks, green_occ, occ_mask, green_virt, virt_mask, owner):
    z = lax.axis_index("grp")
    sub = lax.axis_index("sub")
    x, y, c = sub // 8, (sub // 2) % 4, sub % 2
    e = 1 + 2 * c

    t_oth = move(lax.dynamic_slice_in_dim(three_centre, (1 - c) * 8, 8, 0), CORE)
    pair_oth = move(pair_blocks, CORE)

    gv = green_virt * virt_mask[0, 0].astype(BF)
    gv1 = move(gv, Z1)
    gv = jnp.stack([gv, gv1])
    gv2 = move(gv, Z2)
    gv = jnp.concatenate([gv, gv2])
    gv_oth = move(gv, CORE)

    go = green_occ * occ_mask[0, 0].astype(BF)
    set1 = jnp.stack([go, move(go, on(0, 1))])
    set2 = move(set1, on(0, 3))
    a1 = jnp.stack([set1, move(set1, on(1, 1))])
    b1 = jnp.stack([set2, move(set2, on(1, 3))])
    a2 = jnp.concatenate([a1, move(a1, on(1, 3))])
    b2 = jnp.concatenate([b1, move(b1, on(1, 1))])

    def block_from(target):
        tx, ty = target // 8, (target // 2) % 4
        d1 = jnp.where(c == 0, x ^ tx, y ^ ty)
        d2 = jnp.where(c == 0, y ^ ty, x ^ tx)
        p1 = place(d1, 1)
        in_a = lax.dynamic_slice(a2, (place(d2, 1), p1 % 2, 0, 0), (1, 1, 256, 256))
        in_b = lax.dynamic_slice(b2, (place(d2, 3), p1 % 2, 0, 0), (1, 1, 256, 256))
        return jnp.where(p1 < 2, in_a, in_b).reshape(256, 256)

    for_oth = move(jnp.concatenate([block_from(pair_oth[0, k]) for k in range(2)]), CORE)
    go = jnp.concatenate(
        [
            jnp.where(
                pair_blocks[0, k] % 2 == c,
                block_from(pair_blocks[0, k]),
                for_oth[k * 256 : (k + 1) * 256],
            )
            for k in range(2)
        ]
    )
    go = jnp.stack([go, move(go, Z1)])
    go = jnp.concatenate([go, move(go, Z2)])
    go_oth = move(go, CORE)

    order_x, order_y = ring_order(x, e), ring_order(y, e)
    strips_a = [i * 4 + j for i in order_x for j in order_y]
    strips_b = [i * 4 + j for j in order_y for i in order_x]
    operands = (three_centre, t_oth, go, go_oth, gv, gv_oth)
    send_a, keep_a = products_of(0, jnp.stack([c] + strips_a).astype(jnp.int32), *operands)
    send_b, keep_b = products_of(1, jnp.stack([c] + strips_b).astype(jnp.int32), *operands)
    sum_a = reduce_steps(send_a, keep_a, (X_A, X_B, Y_A, Y_B))
    sum_b = reduce_steps(send_b, keep_b, (Y_A, Y_B, X_A, X_B))
    total = jnp.concatenate([sum_a, sum_b]).transpose(1, 0, 2, 3)

    got1 = move(jnp.stack([total[1], total[3]]), Z1)
    got2 = move(jnp.stack([total[2], got1[1]]), Z2)
    whole = jnp.concatenate([total[0:1], got1[0:1], got2])

    mine = lax.dynamic_slice_in_dim(whole, c * 8, 8, 2)
    other = move(lax.dynamic_slice_in_dim(whole, (1 - c) * 8, 8, 2), CORE)

    owner_flat = owner[:, 0]
    slab = owner_flat.shape[0]
    numbers = jnp.arange(slab, dtype=jnp.int32)
    earlier = (owner_flat[None, :] == owner_flat[:, None]) & (numbers[None, :] < numbers[:, None])
    position = jnp.sum(earlier.astype(jnp.int32), axis=1)
    slots = owner_flat * CAP + position
    d = (numbers // 16) ^ z
    core = (numbers // 8) % 2
    at = jnp.where(core == c, 0, 32) + place(d, 1 + 2 * core) * 8 + numbers % 8
    match = slots[None, :] == jnp.arange(32 * CAP, dtype=jnp.int32)[:, None]
    source = jnp.max(jnp.where(match, at[None, :], -1), axis=1)
    outgoing = fill_slots(source, mine.reshape(32, 8, 256), other.reshape(32, 8, 256))
    arrived = lax.all_to_all(
        outgoing.reshape(32, CAP, 8, 256), "sub", split_axis=0, concat_axis=0, tiled=True
    )
    return arrived.transpose(1, 0, 2, 3).reshape(1, CAP, 256, 256)


def solution(mesh):
    in_specs = (
        P("grp", "sub", None),
        P("sub", None),
        P("sub", "grp"),
        P("sub", "grp"),
        P("grp", "sub"),
        P("grp", "sub"),
        P(),
    )
    out_specs = P("grp", "sub", None, None)
    return jax.shard_map(
        per_device, mesh=mesh, in_specs=in_specs, out_specs=out_specs, check_vma=False
    )
```

time: 496 us -> 173 us (0.35)
  the two profiles are of different devices: /device:TPU:12 before, /device:TPU:1 now
where the time goes in v1:
time: 173 us; the launch traced here: 172 us
  waiting for transfers between devices  60.6 us (35%)
  starting transfers between devices  42.6 us (25%)
  blocking collectives  21.4 us (12%)
  Pallas kernels  19.9 us (12%)
  between operations  12 us (7%)
  local copies, waits for them, and re-layouts  9.21 us (5%)
  other arithmetic  6.57 us (4%)
    ppermute x26, waiting for transfers between devices, move(): return lax.ppermute(value, AXES, permutation)  60.6 us
    ppermute x26, starting transfers between devices, move(): return lax.ppermute(value, AXES, permutation)  42.6 us
    all_to_all x1, blocking collectives, per_device(): lax.all_to_all(outgoing.reshape(32, CAP, 8, 256), 'sub', split_axis=0, co...  21.4 us
    pallas_call x2, Pallas kernels, products_of(): pl.pallas_call(products_body, grid_spec=pltpu.PrefetchScalarGridSpec(num_...  15.8 us
    pallas_call x1, Pallas kernels, fill_slots(): pl.pallas_call(slots_body, grid_spec=pltpu.PrefetchScalarGridSpec(num_sca...  4.06 us
  transfers between devices with their start and end apart: 26, of which 15 were waited for; matrix products, arithmetic and copies ran while one was open for 5% of the time, Pallas kernels for 5%

profile of v1, /device:TPU:1, one launch (start us, length us, event | category | flops | bytes accessed | tf_op | source)
XLA Modules:
  0.0 172.4 jit_solution(8225234260951902661)
XLA Ops:
  1.6 2.2 %collective-permute-start.1 = (bf16[256,256]{1,0:T(8,128)(2,1)S(1)}, bf16[256,256]{1,0:T(8,128)(2,1)S(1)}, u32[]{:S(2)}, u32[]{:S(2)}) collective-permute-start(bf16[256,256]{1,0:T(8,128)(2,1)S(1)} %broadcast_multiply_fusion.1), channel_id=1, source_target_pairs={{0,8},{1,3},{2,10},{3,1},{4,12},{5,7},{6,14},{7,5},{8,0},{9,11},{1... | collective-permute-start | bytes 393224 | tf_op jit(solution)/shard_map/ppermute | solution.py:49
  4.7 1.7 %collective-permute-done.1 = bf16[256,256]{1,0:T(8,128)(2,1)S(1)} collective-permute-done((bf16[256,256]{1,0:T(8,128)(2,1)S(1)}, bf16[256,256]{1,0:T(8,128)(2,1)S(1)}, u32[]{:S(2)}, u32[]{:S(2)}) %collective-permute-start.1) | collective-permute-done | bytes 131104 | tf_op jit(solution)/shard_map/ppermute | solution.py:49
  6.5 3.0 %collective-permute-start.4 = (bf16[2,256,256]{2,1,0:T(8,128)(2,1)S(1)}, bf16[2,256,256]{2,1,0:T(8,128)(2,1)S(1)}, u32[]{:S(2)}, u32[]{:S(2)}) collective-permute-start(bf16[2,256,256]{2,1,0:T(8,128)(2,1)S(1)} %get-tuple-element.28), channel_id=1, source_target_pairs={{0,24},{1,7},{2,26},{3,5},{4,28},{5,3},{6,30},{7,1},{8,16},{9,15},... | collective-permute-start | bytes 786440 | tf_op jit(solution)/shard_map/ppermute | solution.py:49
  10.7 2.8 %collective-permute-done.4 = bf16[2,256,256]{2,1,0:T(8,128)(2,1)S(1)} collective-permute-done((bf16[2,256,256]{2,1,0:T(8,128)(2,1)S(1)}, bf16[2,256,256]{2,1,0:T(8,128)(2,1)S(1)}, u32[]{:S(2)}, u32[]{:S(2)}) %collective-permute-start.4) | collective-permute-done | bytes 262176 | tf_op jit(solution)/shard_map/ppermute | solution.py:49
  13.5 2.5 %collective-permute-start.5 = (bf16[2,256,256]{2,1,0:T(8,128)(2,1)S(1)}, bf16[2,256,256]{2,1,0:T(8,128)(2,1)S(1)}, u32[]{:S(2)}, u32[]{:S(2)}) collective-permute-start(bf16[2,256,256]{2,1,0:T(8,128)(2,1)S(1)} %collective-permute-done.4), channel_id=1, source_target_pairs={{0,6},{1,25},{2,4},{3,27},{4,2},{5,29},{6,0},{7,31},{8,14},{9,17},... | collective-permute-start | bytes 786440 | tf_op jit(solution)/shard_map/ppermute | solution.py:49
  16.1 1.5 collective-permute-start.3
  17.6 2.7 %collective-permute-done.5 = bf16[2,256,256]{2,1,0:T(8,128)(2,1)S(1)} collective-permute-done((bf16[2,256,256]{2,1,0:T(8,128)(2,1)S(1)}, bf16[2,256,256]{2,1,0:T(8,128)(2,1)S(1)}, u32[]{:S(2)}, u32[]{:S(2)}) %collective-permute-start.5) | collective-permute-done | bytes 262176 | tf_op jit(solution)/shard_map/ppermute | solution.py:49
  20.4 3.5 %collective-permute-start.7 = (s32[1,2]{1,0:T(1,128)S(1)}, s32[1,2]{1,0:T(1,128)S(1)}, u32[]{:S(2)}, u32[]{:S(2)}) collective-permute-start(s32[1,2]{1,0:T(1,128)S(1)} %copy-done.3), channel_id=1, source_target_pairs={{0,1},{1,0},{2,3},{3,2},{4,5},{5,4},{6,7},{7,6},{8,9},{9,8},{10,11... | collective-permute-start | bytes 32 | tf_op jit(solution)/shard_map/ppermute | solution.py:49
  39.9 3.9 %collective-permute-start.9 = (bf16[512,256]{1,0:T(8,128)(2,1)S(1)}, bf16[512,256]{1,0:T(8,128)(2,1)S(1)}, u32[]{:S(2)}, u32[]{:S(2)}) collective-permute-start(bf16[512,256]{1,0:T(8,128)(2,1)S(1)} %get-tuple-element.26), channel_id=1, source_target_pairs={{0,32},{1,97},{2,34},{3,99},{4,36},{5,101},{6,38},{7,103},{8,40},{... | collective-permute-start | bytes 786440 | tf_op jit(solution)/shard_map/ppermute | solution.py:49
  43.9 3.1 %constant_dynamic-slice_fusion.2 = bf16[8,256,512]{2,1,0:T(8,128)(2,1)} fusion(bf16[16,256,512]{2,1,0:T(8,128)(2,1)} %t_own.3, s32[]{:T(128)S(6)} %select_n.383), kind=kLoop, calls=%fused_computation.37 | loop fusion | bytes 4194308 | tf_op jit(solution)/shard_map/dynamic_slice | solution.py:166
  48.5 2.7 %collective-permute-start.12 = (bf16[256,256]{1,0:T(8,128)(2,1)S(1)}, bf16[256,256]{1,0:T(8,128)(2,1)S(1)}, u32[]{:S(2)}, u32[]{:S(2)}) collective-permute-start(bf16[256,256]{1,0:T(8,128)(2,1)S(1)} %broadcast_multiply_fusion), channel_id=1, source_target_pairs={{0,32},{1,97},{2,34},{3,99},{4,36},{5,101},{6,38},{7,103},{8,40},{... | collective-permute-start | bytes 393224 | tf_op jit(solution)/shard_map/ppermute | solution.py:49
  51.2 6.3 %collective-permute-done.10 = bf16[2,512,256]{2,1,0:T(8,128)(2,1)S(1)} collective-permute-done((bf16[2,512,256]{2,1,0:T(8,128)(2,1)S(1)}, bf16[2,512,256]{2,1,0:T(8,128)(2,1)S(1)}, u32[]{:S(2)}, u32[]{:S(2)}) %collective-permute-start.10) | collective-permute-done | bytes 524320 | tf_op jit(solution)/shard_map/ppermute | solution.py:49
  57.6 2.0 %collective-permute-start.11 = (bf16[4,512,256]{2,1,0:T(8,128)(2,1)S(1)}, bf16[4,512,256]{2,1,0:T(8,128)(2,1)S(1)}, u32[]{:S(2)}, u32[]{:S(2)}) collective-permute-start(bf16[4,512,256]{2,1,0:T(8,128)(2,1)S(1)} %pad_maximum_fusion.2.go_own), channel_id=1, source_target_pairs={{0,1},{1,0},{2,3},{3,2},{4,5},{5,4},{6,7},{7,6},{8,9},{9,8},{10,11... | collective-permute-start | bytes 3145736 | tf_op jit(solution)/shard_map/ppermute | solution.py:49
  59.8 5.5 %collective-permute-done.13 = bf16[2,256,256]{2,1,0:T(8,128)(2,1)S(1)} collective-permute-done((bf16[2,256,256]{2,1,0:T(8,128)(2,1)S(1)}, bf16[2,256,256]{2,1,0:T(8,128)(2,1)S(1)}, u32[]{:S(2)}, u32[]{:S(2)}) %collective-permute-start.13) | collective-permute-done | bytes 262176 | tf_op jit(solution)/shard_map/ppermute | solution.py:49
  65.3 2.2 %collective-permute-start.14 = (bf16[4,256,256]{2,1,0:T(8,128)(2,1)S(1)}, bf16[4,256,256]{2,1,0:T(8,128)(2,1)S(1)}, u32[]{:S(2)}, u32[]{:S(2)}) collective-permute-start(bf16[4,256,256]{2,1,0:T(8,128)(2,1)S(1)} %pad_maximum_fusion.6.gv_own), channel_id=1, source_target_pairs={{0,1},{1,0},{2,3},{3,2},{4,5},{5,4},{6,7},{7,6},{8,9},{9,8},{10,11... | collective-permute-start | bytes 1572872 | tf_op jit(solution)/shard_map/ppermute | solution.py:49
  69.0 2.2 %copy-done = bf16[16,256,512]{2,1,0:T(8,128)(2,1)S(1)} copy-done((bf16[16,256,512]{2,1,0:T(8,128)(2,1)S(1)}, bf16[16,256,512]{2,1,0:T(8,128)(2,1)}, u32[]{:S(2)}) %copy-start) | copy-done | bytes 4194328
  71.2 8.0 %shard_map.73 = (bf16[4,4,128,256]{3,2,1,0:T(8,128)(2,1)S(1)}, f32[4,4,128,256]{3,2,1,0:T(8,128)S(1)}) custom-call(s32[17]{0:T(128)S(1)} %stack.142.sc, bf16[16,256,512]{2,1,0:T(8,128)(2,1)S(1)} %copy-done, bf16[8,256,512]{2,1,0:T(8,128)(2,1)} %collective-permute-done.t_oth, bf16[4,512,256]{2,1,0:T(8,128)(2,1)S(1)} %pad_maximum_fusion.2.go_own, ...), custom_call_target="tpu_custom_call" | custom-call | flops 3300000000 | bytes 12000000 | tf_op jit(solution)/shard_map/pallas_call | solution.py:79
  79.3 2.6 %collective-permute-start.15 = (bf16[4,4,128,256]{3,2,1,0:T(8,128)(2,1)S(1)}, bf16[4,4,128,256]{3,2,1,0:T(8,128)(2,1)S(1)}, u32[]{:S(2)}, u32[]{:S(2)}) collective-permute-start(bf16[4,4,128,256]{3,2,1,0:T(8,128)(2,1)S(1)} %get-tuple-element.10), channel_id=1, source_target_pairs={{0,8},{1,25},{2,10},{3,27},{4,12},{5,29},{6,14},{7,31},{8,0},{9,17... | collective-permute-start | bytes 3145736 | tf_op jit(solution)/shard_map/ppermute | solution.py:49
  81.8 7.8 %shard_map.74 = (bf16[4,4,128,256]{3,2,1,0:T(8,128)(2,1)S(1)}, f32[4,4,128,256]{3,2,1,0:T(8,128)S(1)}) custom-call(s32[17]{0:T(128)S(1)} %stack.158.sc, bf16[16,256,512]{2,1,0:T(8,128)(2,1)S(1)} %copy-done.1, bf16[8,256,512]{2,1,0:T(8,128)(2,1)} %collective-permute-done.t_oth, bf16[4,512,256]{2,1,0:T(8,128)(2,1)S(1)} %pad_maximum_fusion.2.go_own, ...), custom_call_target="tpu_custom_call" | custom-call | flops 3300000000 | bytes 12000000 | tf_op jit(solution)/shard_map/pallas_call | solution.py:79
  89.7 2.8 %collective-permute-start.19 = (bf16[4,4,128,256]{3,2,1,0:T(8,128)(2,1)S(1)}, bf16[4,4,128,256]{3,2,1,0:T(8,128)(2,1)S(1)}, u32[]{:S(2)}, u32[]{:S(2)}) collective-permute-start(bf16[4,4,128,256]{3,2,1,0:T(8,128)(2,1)S(1)} %get-tuple-element.12), channel_id=1, source_target_pairs={{0,2},{1,7},{2,0},{3,5},{4,6},{5,3},{6,4},{7,1},{8,10},{9,15},{10,... | collective-permute-start | bytes 3145736 | tf_op jit(solution)/shard_map/ppermute | solution.py:49
  92.5 1.8 %collective-permute-done.15 = bf16[4,4,128,256]{3,2,1,0:T(8,128)(2,1)S(1)} collective-permute-done((bf16[4,4,128,256]{3,2,1,0:T(8,128)(2,1)S(1)}, bf16[4,4,128,256]{3,2,1,0:T(8,128)(2,1)S(1)}, u32[]{:S(2)}, u32[]{:S(2)}) %collective-permute-start.15) | collective-permute-done | bytes 1048608 | tf_op jit(solution)/shard_map/ppermute | solution.py:49
  94.5 10.3 %collective-permute-done.19 = bf16[4,4,128,256]{3,2,1,0:T(8,128)(2,1)S(1)} collective-permute-done((bf16[4,4,128,256]{3,2,1,0:T(8,128)(2,1)S(1)}, bf16[4,4,128,256]{3,2,1,0:T(8,128)(2,1)S(1)}, u32[]{:S(2)}, u32[]{:S(2)}) %collective-permute-start.19) | collective-permute-done | bytes 1048608 | tf_op jit(solution)/shard_map/ppermute | solution.py:49
  105.3 2.7 %collective-permute-start.17 = (bf16[4,4,32,256]{3,2,1,0:T(8,128)(2,1)S(1)}, bf16[4,4,32,256]{3,2,1,0:T(8,128)(2,1)S(1)}, u32[]{:S(2)}, u32[]{:S(2)}) collective-permute-start(bf16[4,4,32,256]{3,2,1,0:T(8,128)(2,1)S(1)} %add_convert_fusion.3), channel_id=1, source_target_pairs={{0,2},{1,7},{2,0},{3,5},{4,6},{5,3},{6,4},{7,1},{8,10},{9,15},{10,... | collective-permute-start | bytes 786440 | tf_op jit(solution)/shard_map/ppermute | solution.py:49
  107.9 7.9 %collective-permute-done.20 = bf16[4,4,64,256]{3,2,1,0:T(8,128)(2,1)S(1)} collective-permute-done((bf16[4,4,64,256]{3,2,1,0:T(8,128)(2,1)S(1)}, bf16[4,4,64,256]{3,2,1,0:T(8,128)(2,1)S(1)}, u32[]{:S(2)}, u32[]{:S(2)}) %collective-permute-start.20) | collective-permute-done | bytes 524320 | tf_op jit(solution)/shard_map/ppermute | solution.py:49
  116.4 6.4 %collective-permute-done.21 = bf16[4,4,32,256]{3,2,1,0:T(8,128)(2,1)S(1)} collective-permute-done((bf16[4,4,32,256]{3,2,1,0:T(8,128)(2,1)S(1)}, bf16[4,4,32,256]{3,2,1,0:T(8,128)(2,1)S(1)}, u32[]{:S(2)}, u32[]{:S(2)}) %collective-permute-start.21) | collective-permute-done | bytes 262176 | tf_op jit(solution)/shard_map/ppermute | solution.py:49
  123.1 3.7 %collective-permute-done.22 = bf16[4,4,16,256]{3,2,1,0:T(8,128)(2,1)S(1)} collective-permute-done((bf16[4,4,16,256]{3,2,1,0:T(8,128)(2,1)S(1)}, bf16[4,4,16,256]{3,2,1,0:T(8,128)(2,1)S(1)}, u32[]{:S(2)}, u32[]{:S(2)}) %collective-permute-start.22) | collective-permute-done | bytes 131104 | tf_op jit(solution)/shard_map/ppermute | solution.py:49
  127.0 2.8 %collective-permute-start.23 = (f32[2,8,16,256]{3,2,0,1:T(8,128)S(1)}, f32[2,8,16,256]{3,2,0,1:T(8,128)S(1)}, u32[]{:S(2)}, u32[]{:S(2)}) collective-permute-start(f32[2,8,16,256]{3,2,0,1:T(8,128)S(1)} %pad_maximum_fusion.12), channel_id=1, source_target_pairs={{0,32},{1,97},{2,34},{3,99},{4,36},{5,101},{6,38},{7,103},{8,40},{... | collective-permute-start | bytes 786440 | tf_op jit(solution)/shard_map/ppermute | solution.py:49
  129.8 3.8 %collective-permute-done.23 = f32[2,8,16,256]{3,2,0,1:T(8,128)S(1)} collective-permute-done((f32[2,8,16,256]{3,2,0,1:T(8,128)S(1)}, f32[2,8,16,256]{3,2,0,1:T(8,128)S(1)}, u32[]{:S(2)}, u32[]{:S(2)}) %collective-permute-start.23) | collective-permute-done | bytes 262176 | tf_op jit(solution)/shard_map/ppermute | solution.py:49
  134.1 5.0 %collective-permute-done.24 = f32[2,8,16,256]{3,2,0,1:T(8,128)S(1)} collective-permute-done((f32[2,8,16,256]{3,2,0,1:T(8,128)S(1)}, f32[2,8,16,256]{3,2,0,1:T(8,128)S(1)}, u32[]{:S(2)}, u32[]{:S(2)}) %collective-permute-start.24) | collective-permute-done | bytes 262176 | tf_op jit(solution)/shard_map/ppermute | solution.py:49
  139.2 4.6 %collective-permute-start.25 = (f32[4,8,8,256]{3,2,0,1:T(8,128)S(1)}, f32[4,8,8,256]{3,2,0,1:T(8,128)S(1)}, u32[]{:S(2)}, u32[]{:S(2)}) collective-permute-start(f32[4,8,8,256]{3,2,0,1:T(8,128)S(1)} %get-tuple-element.17), channel_id=1, source_target_pairs={{0,1},{1,0},{2,3},{3,2},{4,5},{5,4},{6,7},{7,6},{8,9},{9,8},{10,11... | collective-permute-start | bytes 786440 | tf_op jit(solution)/shard_map/ppermute | solution.py:49
  145.9 4.1 %shard_map.75 = f32[96,8,256]{2,1,0:T(8,128)} custom-call(s32[96]{0:T(128)} %select_reduce_fusion.sc, f32[32,8,256]{2,1,0:T(8,128)} %bitcast.58, f32[32,8,256]{2,1,0:T(8,128)} %bitcast.59), custom_call_target="tpu_custom_call" | custom-call | tf_op jit(solution)/shard_map/pallas_call | solution.py:126
  150.0 21.4 %all_to_all.5 = f32[32,3,8,256]{3,2,1,0:T(8,128)S(1)} all-to-all(f32[32,3,8,256]{3,2,1,0:T(8,128)} %bitcast.57), channel_id=1, replica_groups=mesh['grp'=4,'sub'=32] {'sub'}, dimensions={0} | all-to-all | bytes 1572864 | tf_op jit(solution)/shard_map/all_to_all | solution.py:237
  (77 shorter events, 16.9 us)
Async XLA Ops:
  0.0 20.4 %copy-start.3 = (s32[1,2]{1,0:T(1,128)S(1)}, s32[1,2]{1,0:T(1,128)}, u32[]{:S(2)}) copy-start(s32[1,2]{1,0:T(1,128)} %param.8) | copy-start | bytes 28
  1.6 4.9 %collective-permute-start.1 = (bf16[256,256]{1,0:T(8,128)(2,1)S(1)}, bf16[256,256]{1,0:T(8,128)(2,1)S(1)}, u32[]{:S(2)}, u32[]{:S(2)}) collective-permute-start(bf16[256,256]{1,0:T(8,128)(2,1)S(1)} %broadcast_multiply_fusion.1), channel_id=1, source_target_pairs={{0,8},{1,3},{2,10},{3,1},{4,12},{5,7},{6,14},{7,5},{8,0},{9,11},{1... | collective-permute-start | bytes 393224 | tf_op jit(solution)/shard_map/ppermute | solution.py:49
  6.5 7.0 %collective-permute-start.4 = (bf16[2,256,256]{2,1,0:T(8,128)(2,1)S(1)}, bf16[2,256,256]{2,1,0:T(8,128)(2,1)S(1)}, u32[]{:S(2)}, u32[]{:S(2)}) collective-permute-start(bf16[2,256,256]{2,1,0:T(8,128)(2,1)S(1)} %get-tuple-element.28), channel_id=1, source_target_pairs={{0,24},{1,7},{2,26},{3,5},{4,28},{5,3},{6,30},{7,1},{8,16},{9,15},... | collective-permute-start | bytes 786440 | tf_op jit(solution)/shard_map/ppermute | solution.py:49
  9.5 6.5 %collective-permute-start.2 = (bf16[2,256,256]{2,1,0:T(8,128)(2,1)S(1)}, bf16[2,256,256]{2,1,0:T(8,128)(2,1)S(1)}, u32[]{:S(2)}, u32[]{:S(2)}) collective-permute-start(bf16[2,256,256]{2,1,0:T(8,128)(2,1)S(1)} %get-tuple-element.28), channel_id=1, source_target_pairs={{0,2},{1,9},{2,0},{3,11},{4,6},{5,13},{6,4},{7,15},{8,10},{9,1},{1... | collective-permute-start | bytes 786440 | tf_op jit(solution)/shard_map/ppermute | solution.py:49
  13.5 6.7 %collective-permute-start.5 = (bf16[2,256,256]{2,1,0:T(8,128)(2,1)S(1)}, bf16[2,256,256]{2,1,0:T(8,128)(2,1)S(1)}, u32[]{:S(2)}, u32[]{:S(2)}) collective-permute-start(bf16[2,256,256]{2,1,0:T(8,128)(2,1)S(1)} %collective-permute-done.4), channel_id=1, source_target_pairs={{0,6},{1,25},{2,4},{3,27},{4,2},{5,29},{6,0},{7,31},{8,14},{9,17},... | collective-permute-start | bytes 786440 | tf_op jit(solution)/shard_map/ppermute | solution.py:49
  16.1 14.5 %collective-permute-start.3 = (bf16[2,2,256,256]{3,2,1,0:T(8,128)(2,1)S(1)}, bf16[2,2,256,256]{3,2,1,0:T(8,128)(2,1)}, u32[]{:S(2)}, u32[]{:S(2)}) collective-permute-start(bf16[2,2,256,256]{3,2,1,0:T(8,128)(2,1)S(1)} %pad_maximum_fusion.3), channel_id=1, source_target_pairs={{0,6},{1,25},{2,4},{3,27},{4,2},{5,29},{6,0},{7,31},{8,14},{9,17},... | collective-permute-start | bytes 1572872 | tf_op jit(solution)/shard_map/ppermute | solution.py:49
  20.3 11.4 %collective-permute-start.6 = (bf16[2,2,256,256]{3,2,1,0:T(8,128)(2,1)S(1)}, bf16[2,2,256,256]{3,2,1,0:T(8,128)(2,1)}, u32[]{:S(2)}, u32[]{:S(2)}) collective-permute-start(bf16[2,2,256,256]{3,2,1,0:T(8,128)(2,1)S(1)} %pad_maximum_fusion.4), channel_id=1, source_target_pairs={{0,2},{1,9},{2,0},{3,11},{4,6},{5,13},{6,4},{7,15},{8,10},{9,1},{1... | collective-permute-start | bytes 1572872 | tf_op jit(solution)/shard_map/ppermute | solution.py:49
  20.4 4.3 %collective-permute-start.7 = (s32[1,2]{1,0:T(1,128)S(1)}, s32[1,2]{1,0:T(1,128)S(1)}, u32[]{:S(2)}, u32[]{:S(2)}) collective-permute-start(s32[1,2]{1,0:T(1,128)S(1)} %copy-done.3), channel_id=1, source_target_pairs={{0,1},{1,0},{2,3},{3,2},{4,5},{5,4},{6,7},{7,6},{8,9},{9,8},{10,11... | collective-permute-start | bytes 32 | tf_op jit(solution)/shard_map/ppermute | solution.py:49
  33.0 6.8 %collective-permute-start.8 = (bf16[512,256]{1,0:T(8,128)(2,1)S(1)}, bf16[512,256]{1,0:T(8,128)(2,1)S(1)}, u32[]{:S(2)}, u32[]{:S(2)}) collective-permute-start(bf16[512,256]{1,0:T(8,128)(2,1)S(1)} %pad_maximum_fusion.9), channel_id=1, source_target_pairs={{0,1},{1,0},{2,3},{3,2},{4,5},{5,4},{6,7},{7,6},{8,9},{9,8},{10,11... | collective-permute-start | bytes 786440 | tf_op jit(solution)/shard_map/ppermute | solution.py:49
  39.9 7.7 %collective-permute-start.9 = (bf16[512,256]{1,0:T(8,128)(2,1)S(1)}, bf16[512,256]{1,0:T(8,128)(2,1)S(1)}, u32[]{:S(2)}, u32[]{:S(2)}) collective-permute-start(bf16[512,256]{1,0:T(8,128)(2,1)S(1)} %get-tuple-element.26), channel_id=1, source_target_pairs={{0,32},{1,97},{2,34},{3,99},{4,36},{5,101},{6,38},{7,103},{8,40},{... | collective-permute-start | bytes 786440 | tf_op jit(solution)/shard_map/ppermute | solution.py:49
  43.9 4.6 %copy-start.2 = (bf16[256,256]{1,0:T(8,128)(2,1)S(1)}, bf16[256,256]{1,0:T(8,128)(2,1)}, u32[]{:S(2)}) copy-start(bf16[256,256]{1,0:T(8,128)(2,1)} %param.11) | copy-start | bytes 393220
  47.0 22.1 %collective-permute-start = (bf16[8,256,512]{2,1,0:T(8,128)(2,1)}, bf16[8,256,512]{2,1,0:T(8,128)(2,1)}, u32[]{:S(2)}, u32[]{:S(2)}) collective-permute-start(bf16[8,256,512]{2,1,0:T(8,128)(2,1)} %constant_dynamic-slice_fusion.2), channel_id=1, source_target_pairs={{0,1},{1,0},{2,3},{3,2},{4,5},{5,4},{6,7},{7,6},{8,9},{9,8},{10,11... | collective-permute-start | bytes 6291464 | tf_op jit(solution)/shard_map/ppermute | solution.py:49
  47.7 9.8 %collective-permute-start.10 = (bf16[2,512,256]{2,1,0:T(8,128)(2,1)S(1)}, bf16[2,512,256]{2,1,0:T(8,128)(2,1)S(1)}, u32[]{:S(2)}, u32[]{:S(2)}) collective-permute-start(bf16[2,512,256]{2,1,0:T(8,128)(2,1)S(1)} %pad_maximum_fusion.5), channel_id=1, source_target_pairs={{0,96},{1,33},{2,98},{3,35},{4,100},{5,37},{6,102},{7,39},{8,104},... | collective-permute-start | bytes 1572872 | tf_op jit(solution)/shard_map/ppermute | solution.py:49
  48.5 11.2 %collective-permute-start.12 = (bf16[256,256]{1,0:T(8,128)(2,1)S(1)}, bf16[256,256]{1,0:T(8,128)(2,1)S(1)}, u32[]{:S(2)}, u32[]{:S(2)}) collective-permute-start(bf16[256,256]{1,0:T(8,128)(2,1)S(1)} %broadcast_multiply_fusion), channel_id=1, source_target_pairs={{0,32},{1,97},{2,34},{3,99},{4,36},{5,101},{6,38},{7,103},{8,40},{... | collective-permute-start | bytes 393224 | tf_op jit(solution)/shard_map/ppermute | solution.py:49
  57.6 11.4 %collective-permute-start.11 = (bf16[4,512,256]{2,1,0:T(8,128)(2,1)S(1)}, bf16[4,512,256]{2,1,0:T(8,128)(2,1)S(1)}, u32[]{:S(2)}, u32[]{:S(2)}) collective-permute-start(bf16[4,512,256]{2,1,0:T(8,128)(2,1)S(1)} %pad_maximum_fusion.2.go_own), channel_id=1, source_target_pairs={{0,1},{1,0},{2,3},{3,2},{4,5},{5,4},{6,7},{7,6},{8,9},{9,8},{10,11... | collective-permute-start | bytes 3145736 | tf_op jit(solution)/shard_map/ppermute | solution.py:49
  59.7 5.6 %collective-permute-start.13 = (bf16[2,256,256]{2,1,0:T(8,128)(2,1)S(1)}, bf16[2,256,256]{2,1,0:T(8,128)(2,1)S(1)}, u32[]{:S(2)}, u32[]{:S(2)}) collective-permute-start(bf16[2,256,256]{2,1,0:T(8,128)(2,1)S(1)} %pad_maximum_fusion.11), channel_id=1, source_target_pairs={{0,96},{1,33},{2,98},{3,35},{4,100},{5,37},{6,102},{7,39},{8,104},... | collective-permute-start | bytes 786440 | tf_op jit(solution)/shard_map/ppermute | solution.py:49
  65.3 3.7 %collective-permute-start.14 = (bf16[4,256,256]{2,1,0:T(8,128)(2,1)S(1)}, bf16[4,256,256]{2,1,0:T(8,128)(2,1)S(1)}, u32[]{:S(2)}, u32[]{:S(2)}) collective-permute-start(bf16[4,256,256]{2,1,0:T(8,128)(2,1)S(1)} %pad_maximum_fusion.6.gv_own), channel_id=1, source_target_pairs={{0,1},{1,0},{2,3},{3,2},{4,5},{5,4},{6,7},{7,6},{8,9},{9,8},{10,11... | collective-permute-start | bytes 1572872 | tf_op jit(solution)/shard_map/ppermute | solution.py:49
  69.0 2.2 %copy-start = (bf16[16,256,512]{2,1,0:T(8,128)(2,1)S(1)}, bf16[16,256,512]{2,1,0:T(8,128)(2,1)}, u32[]{:S(2)}) copy-start(bf16[16,256,512]{2,1,0:T(8,128)(2,1)} %t_own.3) | copy-start | bytes 12582916
  71.2 10.6 %copy-start.1 = (bf16[16,256,512]{2,1,0:T(8,128)(2,1)S(1)}, bf16[16,256,512]{2,1,0:T(8,128)(2,1)}, u32[]{:S(2)}) copy-start(bf16[16,256,512]{2,1,0:T(8,128)(2,1)} %t_own.3) | copy-start | bytes 12582916
  79.3 14.9 %collective-permute-start.15 = (bf16[4,4,128,256]{3,2,1,0:T(8,128)(2,1)S(1)}, bf16[4,4,128,256]{3,2,1,0:T(8,128)(2,1)S(1)}, u32[]{:S(2)}, u32[]{:S(2)}) collective-permute-start(bf16[4,4,128,256]{3,2,1,0:T(8,128)(2,1)S(1)} %get-tuple-element.10), channel_id=1, source_target_pairs={{0,8},{1,25},{2,10},{3,27},{4,12},{5,29},{6,14},{7,31},{8,0},{9,17... | collective-permute-start | bytes 3145736 | tf_op jit(solution)/shard_map/ppermute | solution.py:49
  89.7 15.1 %collective-permute-start.19 = (bf16[4,4,128,256]{3,2,1,0:T(8,128)(2,1)S(1)}, bf16[4,4,128,256]{3,2,1,0:T(8,128)(2,1)S(1)}, u32[]{:S(2)}, u32[]{:S(2)}) collective-permute-start(bf16[4,4,128,256]{3,2,1,0:T(8,128)(2,1)S(1)} %get-tuple-element.12), channel_id=1, source_target_pairs={{0,2},{1,7},{2,0},{3,5},{4,6},{5,3},{6,4},{7,1},{8,10},{9,15},{10,... | collective-permute-start | bytes 3145736 | tf_op jit(solution)/shard_map/ppermute | solution.py:49
  94.4 10.8 %collective-permute-start.16 = (bf16[4,4,64,256]{3,2,1,0:T(8,128)(2,1)S(1)}, bf16[4,4,64,256]{3,2,1,0:T(8,128)(2,1)S(1)}, u32[]{:S(2)}, u32[]{:S(2)}) collective-permute-start(bf16[4,4,64,256]{3,2,1,0:T(8,128)(2,1)S(1)} %add_convert_fusion.1), channel_id=1, source_target_pairs={{0,24},{1,9},{2,26},{3,11},{4,28},{5,13},{6,30},{7,15},{8,16},{9,1... | collective-permute-start | bytes 1572872 | tf_op jit(solution)/shard_map/ppermute | solution.py:49
  104.9 10.9 %collective-permute-start.20 = (bf16[4,4,64,256]{3,2,1,0:T(8,128)(2,1)S(1)}, bf16[4,4,64,256]{3,2,1,0:T(8,128)(2,1)S(1)}, u32[]{:S(2)}, u32[]{:S(2)}) collective-permute-start(bf16[4,4,64,256]{3,2,1,0:T(8,128)(2,1)S(1)} %add_convert_fusion), channel_id=1, source_target_pairs={{0,6},{1,3},{2,4},{3,1},{4,2},{5,7},{6,0},{7,5},{8,14},{9,11},{10,... | collective-permute-start | bytes 1572872 | tf_op jit(solution)/shard_map/ppermute | solution.py:49
  105.3 10.8 %collective-permute-start.17 = (bf16[4,4,32,256]{3,2,1,0:T(8,128)(2,1)S(1)}, bf16[4,4,32,256]{3,2,1,0:T(8,128)(2,1)S(1)}, u32[]{:S(2)}, u32[]{:S(2)}) collective-permute-start(bf16[4,4,32,256]{3,2,1,0:T(8,128)(2,1)S(1)} %add_convert_fusion.3), channel_id=1, source_target_pairs={{0,2},{1,7},{2,0},{3,5},{4,6},{5,3},{6,4},{7,1},{8,10},{9,15},{10,... | collective-permute-start | bytes 786440 | tf_op jit(solution)/shard_map/ppermute | solution.py:49
  116.0 6.8 %collective-permute-start.21 = (bf16[4,4,32,256]{3,2,1,0:T(8,128)(2,1)S(1)}, bf16[4,4,32,256]{3,2,1,0:T(8,128)(2,1)S(1)}, u32[]{:S(2)}, u32[]{:S(2)}) collective-permute-start(bf16[4,4,32,256]{3,2,1,0:T(8,128)(2,1)S(1)} %add_convert_fusion.2), channel_id=1, source_target_pairs={{0,8},{1,25},{2,10},{3,27},{4,12},{5,29},{6,14},{7,31},{8,0},{9,17... | collective-permute-start | bytes 786440 | tf_op jit(solution)/shard_map/ppermute | solution.py:49
  116.2 6.8 %collective-permute-start.18 = (bf16[4,4,16,256]{3,2,1,0:T(8,128)(2,1)S(1)}, bf16[4,4,16,256]{3,2,1,0:T(8,128)(2,1)S(1)}, u32[]{:S(2)}, u32[]{:S(2)}) collective-permute-start(bf16[4,4,16,256]{3,2,1,0:T(8,128)(2,1)S(1)} %add_convert_fusion.5), channel_id=1, source_target_pairs={{0,6},{1,3},{2,4},{3,1},{4,2},{5,7},{6,0},{7,5},{8,14},{9,11},{10,... | collective-permute-start | bytes 393224 | tf_op jit(solution)/shard_map/ppermute | solution.py:49
  122.9 3.9 %collective-permute-start.22 = (bf16[4,4,16,256]{3,2,1,0:T(8,128)(2,1)S(1)}, bf16[4,4,16,256]{3,2,1,0:T(8,128)(2,1)S(1)}, u32[]{:S(2)}, u32[]{:S(2)}) collective-permute-start(bf16[4,4,16,256]{3,2,1,0:T(8,128)(2,1)S(1)} %add_convert_fusion.4), channel_id=1, source_target_pairs={{0,24},{1,9},{2,26},{3,11},{4,28},{5,13},{6,30},{7,15},{8,16},{9,1... | collective-permute-start | bytes 393224 | tf_op jit(solution)/shard_map/ppermute | solution.py:49
  126.9 7.1 %copy-start.4 = (s32[64,1]{0,1:T(1,128)S(1)}, s32[64,1]{0,1:T(1,128)}, u32[]{:S(2)}) copy-start(s32[64,1]{0,1:T(1,128)} %param.13) | copy-start | bytes 772
  127.0 6.6 %collective-permute-start.23 = (f32[2,8,16,256]{3,2,0,1:T(8,128)S(1)}, f32[2,8,16,256]{3,2,0,1:T(8,128)S(1)}, u32[]{:S(2)}, u32[]{:S(2)}) collective-permute-start(f32[2,8,16,256]{3,2,0,1:T(8,128)S(1)} %pad_maximum_fusion.12), channel_id=1, source_target_pairs={{0,32},{1,97},{2,34},{3,99},{4,36},{5,101},{6,38},{7,103},{8,40},{... | collective-permute-start | bytes 786440 | tf_op jit(solution)/shard_map/ppermute | solution.py:49
  133.6 5.5 %collective-permute-start.24 = (f32[2,8,16,256]{3,2,0,1:T(8,128)S(1)}, f32[2,8,16,256]{3,2,0,1:T(8,128)S(1)}, u32[]{:S(2)}, u32[]{:S(2)}) collective-permute-start(f32[2,8,16,256]{3,2,0,1:T(8,128)S(1)} %pad_maximum_fusion.13), channel_id=1, source_target_pairs={{0,96},{1,33},{2,98},{3,35},{4,100},{5,37},{6,102},{7,39},{8,104},... | collective-permute-start | bytes 786440 | tf_op jit(solution)/shard_map/ppermute | solution.py:49
  139.2 6.0 %collective-permute-start.25 = (f32[4,8,8,256]{3,2,0,1:T(8,128)S(1)}, f32[4,8,8,256]{3,2,0,1:T(8,128)S(1)}, u32[]{:S(2)}, u32[]{:S(2)}) collective-permute-start(f32[4,8,8,256]{3,2,0,1:T(8,128)S(1)} %get-tuple-element.17), channel_id=1, source_target_pairs={{0,1},{1,0},{2,3},{3,2},{4,5},{5,4},{6,7},{7,6},{8,9},{9,8},{10,11... | collective-permute-start | bytes 786440 | tf_op jit(solution)/shard_map/ppermute | solution.py:49

commit v2 on v0

v2 whole, which is shorter than its diff:
```python
import jax
import jax.numpy as jnp
from jax import lax
from jax.experimental import pallas as pl
from jax.experimental.pallas import tpu as pltpu
from jax.sharding import PartitionSpec as P

CAP = 3
AXES = ("grp", "sub")
BF = jnp.bfloat16
F32 = jnp.float32
STACK = 4


def pairs(target):
    out = []
    for z in range(4):
        for x in range(4):
            for y in range(4):
                for c in range(2):
                    tz, tx, ty, tc = target(z, x, y, c)
                    to = (tz % 4) * 32 + ((tx % 4) * 4 + ty % 4) * 2 + tc
                    out.append((z * 32 + (x * 4 + y) * 2 + c, to))
    return out


def along(number, d):
    def target(z, x, y, c):
        return (z, x + d, y, c) if c == number else (z, x, y + d, c)

    return pairs(target)


CORE = pairs(lambda z, x, y, c: (z, x, y, 1 - c))
FIRST = [along(0, d) for d in range(4)]
SECOND = [along(1, d) for d in range(4)]
DEPTH = [pairs(lambda z, x, y, c, d=d: (z + d, x, y, c)) for d in range(4)]


def move(value, permutation):
    return lax.ppermute(value, AXES, permutation)


def whole(shape):
    return pl.BlockSpec(shape, lambda *_: (0,) * len(shape))


def pick_body(sc, set0, set1, set2, set3, out, sem):
    c = sc[0]
    for k in range(4):
        block = sc[3 + k]
        tx, ty, tc = block // 8, (block // 2) % 4, block % 2
        t1 = jnp.where(c == 0, tx, ty)
        t2 = jnp.where(c == 0, ty, tx)
        at = ((sc[1] - t1 + 4) % 4) * 2 + tc
        far = (sc[2] - t2 + 4) % 4
        for e, source in enumerate((set0, set1, set2, set3)):

            @pl.when(far == e)
            def _(source=source):
                pltpu.make_async_copy(source.at[at], out.at[k], sem.at[k]).start()

    for k in range(4):
        pltpu.make_async_copy(set0.at[0], out.at[k], sem.at[k]).wait()


def pick(scalars, *sets):
    return pl.pallas_call(
        pick_body,
        grid_spec=pltpu.PrefetchScalarGridSpec(
            num_scalar_prefetch=1,
            grid=(1,),
            in_specs=[pl.BlockSpec(memory_space=pl.ANY)] * 4,
            out_specs=pl.BlockSpec(memory_space=pl.ANY),
            scratch_shapes=[pltpu.SemaphoreType.DMA((4,))],
        ),
        out_shape=jax.ShapeDtypeStruct((4, 128, 256), BF),
        cost_estimate=pl.CostEstimate(flops=0, bytes_accessed=600_000, transcendentals=0),
    )(scalars, *sets)


def order_body(sc, own, oth, out):
    for k in range(16):
        rows = pl.ds(pl.multiple_of(sc[k] * 16, 16), 16)
        for g in range(4):
            out[g, k * 16 : (k + 1) * 16, 0:256] = own[g, rows, :]
            out[g, k * 16 : (k + 1) * 16, 256:512] = oth[g, rows, :]


def order_rows(strips, own, oth):
    return pl.pallas_call(
        order_body,
        grid_spec=pltpu.PrefetchScalarGridSpec(
            num_scalar_prefetch=1,
            grid=(1,),
            in_specs=[whole((4, 256, 256))] * 2,
            out_specs=whole((4, 256, 512)),
        ),
        out_shape=jax.ShapeDtypeStruct((4, 256, 512), BF),
        cost_estimate=pl.CostEstimate(flops=0, bytes_accessed=2_000_000, transcendentals=0),
    )(strips, own, oth)


def products_body(sc, t_own, t_oth, go, gv, send1, send2, send3, keep):
    c = sc[0]
    count = go.shape[0] // 2
    for r in range(count):
        half_own = jnp.dot(
            t_own[...].reshape(STACK * 256, 512), go[2 * r + c], preferred_element_type=F32
        ).astype(BF)
        half_oth = jnp.dot(
            t_oth[...].reshape(STACK * 256, 512), go[2 * r + 1 - c], preferred_element_type=F32
        ).astype(BF)
        for p in range(STACK):
            rows = slice(p * 256, (p + 1) * 256)
            out = jnp.dot(gv[r, :, 0:256], half_own[rows], preferred_element_type=F32)
            out += jnp.dot(gv[r, :, 256:512], half_oth[rows], preferred_element_type=F32)
            send1[p, r] = out[0:64].astype(BF)
            send2[p, r] = out[64:128].astype(BF)
            send3[p, r] = out[128:192].astype(BF)
            keep[p, r] = out[192:256]


def products_of(core, t_own, t_oth, go, gv):
    count = gv.shape[0]
    block = pl.BlockSpec((STACK, count, 64, 256), lambda p, sc: (p, 0, 0, 0))
    shape = (8, count, 64, 256)
    return pl.pallas_call(
        products_body,
        grid_spec=pltpu.PrefetchScalarGridSpec(
            num_scalar_prefetch=1,
            grid=(8 // STACK,),
            in_specs=[
                pl.BlockSpec((STACK, 256, 512), lambda p, sc: (sc[0] * (8 // STACK) + p, 0, 0)),
                pl.BlockSpec((STACK, 256, 512), lambda p, sc: (p, 0, 0)),
                whole((2 * count, 512, 256)),
                whole((count, 256, 512)),
            ],
            out_specs=[block] * 4,
        ),
        out_shape=[jax.ShapeDtypeStruct(shape, BF)] * 3 + [jax.ShapeDtypeStruct(shape, F32)],
        compiler_params=pltpu.CompilerParams(vmem_limit_bytes=40 * 1024 * 1024),
        cost_estimate=pl.CostEstimate(
            flops=1_600_000_000 * count, bytes_accessed=4_000_000 * count, transcendentals=0
        ),
    )(core, t_own, t_oth, go, gv)


def slots_body(sc, pieces, out):
    for s in range(32 * CAP):
        out[s] = pieces[sc[s]]


def fill_slots(source, pieces):
    return pl.pallas_call(
        slots_body,
        grid_spec=pltpu.PrefetchScalarGridSpec(
            num_scalar_prefetch=1,
            grid=(1,),
            in_specs=[whole((65, 16, 128))],
            out_specs=whole((32 * CAP, 16, 128)),
        ),
        out_shape=jax.ShapeDtypeStruct((32 * CAP, 16, 128), BF),
    )(source, pieces)


def per_device(three_centre, pair_blocks, green_occ, occ_mask, green_virt, virt_mask, owner):
    z = lax.axis_index("grp")
    sub = lax.axis_index("sub")
    x, y, c = sub // 8, (sub // 2) % 4, sub % 2
    q1, q2 = jnp.where(c == 0, x, y), jnp.where(c == 0, y, x)

    def by_core(mine, other):
        return jnp.where(c == 0, jnp.stack([mine, other]), jnp.stack([other, mine]))

    go = green_occ * occ_mask[0, 0].astype(BF)
    go = by_core(
        lax.dynamic_slice_in_dim(go, c * 128, 128, 0),
        move(lax.dynamic_slice_in_dim(go, (1 - c) * 128, 128, 0), CORE),
    )
    near = jnp.concatenate([go] + [move(go, FIRST[d]) for d in (1, 2, 3)])
    sets = [near] + [move(near, SECOND[e]) for e in (1, 2, 3)]

    t_oth = move(lax.dynamic_slice_in_dim(three_centre, (1 - c) * 8, 8, 0), CORE)

    gv = green_virt * virt_mask[0, 0].astype(BF)
    gv = jnp.stack([gv] + [move(gv, DEPTH[r]) for r in (1, 2, 3)])
    strips = [
        jnp.where(c == 0, s1 * 4 + s2, s2 * 4 + s1)
        for s1 in [(q1 + d) % 4 for d in (1, 2, 3, 0)]
        for s2 in [(q2 + e) % 4 for e in range(4)]
    ]
    gv = order_rows(jnp.stack(strips).astype(jnp.int32), gv, move(gv, CORE))

    partners = by_core(pair_blocks[0], move(pair_blocks, CORE)[0]).reshape(4)
    places = jnp.concatenate([jnp.stack([c, q1, q2]), partners]).astype(jnp.int32)
    picked = pick(places, *sets)
    picks = [picked] + [move(picked, DEPTH[r]) for r in (1, 2, 3)]

    def rows_of(part):
        halves = by_core(part, move(part, CORE))
        return halves.transpose(1, 0, 2, 3).reshape(2, 512, 256)

    core = c.reshape(1).astype(jnp.int32)
    lists = []
    for begin, end in ((0, 1), (1, 4)):
        lists.append(
            products_of(
                core,
                three_centre,
                t_oth,
                jnp.concatenate([rows_of(picks[r]) for r in range(begin, end)]),
                gv[begin:end],
            )
        )

    sums = []
    for send1, send2, send3, keep in lists:
        total = keep
        for d, send in ((1, send1), (2, send2), (3, send3)):
            total = total + move(send, FIRST[d]).astype(F32)
        sums.append(total)

    def strip(e):
        return jnp.concatenate([t[:, :, e * 16 : (e + 1) * 16] for t in sums], axis=1)

    total = strip(0)
    for e in (1, 2, 3):
        total = total + move(strip(e).astype(BF), SECOND[e]).astype(F32)
    total = total.astype(BF)

    rows = jnp.stack([total[:, 0]] + [move(total[:, r], DEPTH[4 - r]) for r in (1, 2, 3)])
    mine = lax.dynamic_slice_in_dim(rows, c * 128, 128, 3)
    other = move(lax.dynamic_slice_in_dim(rows, (1 - c) * 128, 128, 3), CORE)
    pieces = jnp.concatenate(
        [mine.reshape(32, 16, 128), other.reshape(32, 16, 128), jnp.zeros((1, 16, 128), BF)]
    )

    owner_flat = owner[:, 0]
    slab = owner_flat.shape[0]
    numbers = jnp.arange(slab, dtype=jnp.int32)
    earlier = (owner_flat[None, :] == owner_flat[:, None]) & (numbers[None, :] < numbers[:, None])
    position = jnp.sum(earlier.astype(jnp.int32), axis=1)
    slots = owner_flat * CAP + position
    distance = (numbers // 16 - z + 4) % 4
    at = jnp.where((numbers // 8) % 2 == c, 0, 32) + distance * 8 + numbers % 8
    match = slots[None, :] == jnp.arange(32 * CAP, dtype=jnp.int32)[:, None]
    source = jnp.min(jnp.where(match, at[None, :], 64), axis=1)
    outgoing = fill_slots(source, pieces)
    arrived = lax.all_to_all(
        outgoing.reshape(32, CAP, 16, 128), "sub", split_axis=0, concat_axis=0, tiled=True
    )
    arrived = arrived.reshape(16, 2, CAP, 16, 128).transpose(2, 0, 3, 1, 4)
    return arrived.reshape(1, CAP, 256, 256).astype(F32)


def solution(mesh):
    in_specs = (
        P("grp", "sub", None),
        P("sub", None),
        P("sub", "grp"),
        P("sub", "grp"),
        P("grp", "sub"),
        P("grp", "sub"),
        P(),
    )
    out_specs = P("grp", "sub", None, None)
    return jax.shard_map(
        per_device, mesh=mesh, in_specs=in_specs, out_specs=out_specs, check_vma=False
    )
```

time: 496 us -> 154 us (0.31)
  the two profiles are of different devices: /device:TPU:12 before, /device:TPU:1 now
where the time goes in v2:
time: 154 us; the launch traced here: 153 us
  starting transfers between devices  54.2 us (35%)
  waiting for transfers between devices  39.8 us (26%)
  Pallas kernels  22.3 us (14%)
  blocking collectives  16.9 us (11%)
  local copies, waits for them, and re-layouts  10.2 us (7%)
  other arithmetic  7.88 us (5%)
  between operations  1.72 us (1%)
    ppermute x33, starting transfers between devices, move(): return lax.ppermute(value, AXES, permutation)  54.2 us
    ppermute x33, waiting for transfers between devices, move(): return lax.ppermute(value, AXES, permutation)  39.8 us
    all_to_all x1, blocking collectives, per_device(): lax.all_to_all(outgoing.reshape(32, CAP, 16, 128), 'sub', split_axis=0, c...  16.9 us
    pallas_call x1, Pallas kernels, pick(): pl.pallas_call(pick_body, grid_spec=pltpu.PrefetchScalarGridSpec(num_scal...  9.76 us
    pallas_call x2, Pallas kernels, products_of(): pl.pallas_call(products_body, grid_spec=pltpu.PrefetchScalarGridSpec(num_...  7.22 us
    transpose x4, other arithmetic, rows_of(): return halves.transpose(1, 0, 2, 3).reshape(2, 512, 256)  3.41 us
    dynamic_slice x1, local copies, waits for them, and re-layouts, per_device(): lax.dynamic_slice_in_dim(three_centre, (1 - c) * 8, 8, 0)  3.12 us
  transfers between devices with their start and end apart: 33, of which 13 were waited for; matrix products, arithmetic and copies ran while one was open for 8% of the time, Pallas kernels for 12%

profile of v2, /device:TPU:1, one launch (start us, length us, event | category | flops | bytes accessed | tf_op | source)
XLA Modules:
  0.0 153.0 jit_solution(4283366898415712257)
XLA Ops:
  1.6 1.5 collective-permute-start.2
  3.1 3.1 %constant_dynamic-slice_fusion.3 = bf16[8,256,512]{2,1,0:T(8,128)(2,1)} fusion(bf16[16,256,512]{2,1,0:T(8,128)(2,1)} %t_own.3, s32[]{:T(128)S(6)} %select_n.241), kind=kLoop, calls=%fused_computation.49 | loop fusion | bytes 4194308 | tf_op jit(solution)/shard_map/dynamic_slice | solution.py:184
  8.4 2.6 %collective-permute-start.4 = (bf16[2,128,256]{2,1,0:T(8,128)(2,1)S(1)}, bf16[2,128,256]{2,1,0:T(8,128)(2,1)S(1)}, u32[]{:S(2)}, u32[]{:S(2)}) collective-permute-start(bf16[2,128,256]{2,1,0:T(8,128)(2,1)S(1)} %maximum_select_fusion.4), channel_id=1, source_target_pairs={{0,16},{1,5},{2,18},{3,7},{4,20},{5,1},{6,22},{7,3},{8,24},{9,13},... | collective-permute-start | bytes 393224 | tf_op jit(solution)/shard_map/ppermute | solution.py:41
  12.1 1.7 %collective-permute-start.10 = (bf16[256,256]{1,0:T(8,128)(2,1)S(1)}, bf16[256,256]{1,0:T(8,128)(2,1)S(1)}, u32[]{:S(2)}, u32[]{:S(2)}) collective-permute-start(bf16[256,256]{1,0:T(8,128)(2,1)S(1)} %broadcast_multiply_fusion), channel_id=1, source_target_pairs={{0,32},{1,33},{2,34},{3,35},{4,36},{5,37},{6,38},{7,39},{8,40},{9,... | collective-permute-start | bytes 393224 | tf_op jit(solution)/shard_map/ppermute | solution.py:41
  13.8 3.3 %collective-permute-start.11 = (bf16[256,256]{1,0:T(8,128)(2,1)S(1)}, bf16[256,256]{1,0:T(8,128)(2,1)S(1)}, u32[]{:S(2)}, u32[]{:S(2)}) collective-permute-start(bf16[256,256]{1,0:T(8,128)(2,1)S(1)} %broadcast_multiply_fusion), channel_id=1, source_target_pairs={{0,64},{1,65},{2,66},{3,67},{4,68},{5,69},{6,70},{7,71},{8,72},{9,... | collective-permute-start | bytes 393224 | tf_op jit(solution)/shard_map/ppermute | solution.py:41
  17.1 1.7 %collective-permute-start.12 = (bf16[256,256]{1,0:T(8,128)(2,1)S(1)}, bf16[256,256]{1,0:T(8,128)(2,1)S(1)}, u32[]{:S(2)}, u32[]{:S(2)}) collective-permute-start(bf16[256,256]{1,0:T(8,128)(2,1)S(1)} %broadcast_multiply_fusion), channel_id=1, source_target_pairs={{0,96},{1,97},{2,98},{3,99},{4,100},{5,101},{6,102},{7,103},{8,104... | collective-permute-start | bytes 393224 | tf_op jit(solution)/shard_map/ppermute | solution.py:41
  19.9 2.5 %collective-permute-start.7 = (bf16[8,128,256]{2,1,0:T(8,128)(2,1)S(1)}, bf16[8,128,256]{2,1,0:T(8,128)(2,1)}, u32[]{:S(2)}, u32[]{:S(2)}) collective-permute-start(bf16[8,128,256]{2,1,0:T(8,128)(2,1)S(1)} %pad_maximum_fusion.1.set0), channel_id=1, source_target_pairs={{0,4},{1,17},{2,6},{3,19},{4,0},{5,21},{6,2},{7,23},{8,12},{9,25},... | collective-permute-start | bytes 1572872 | tf_op jit(solution)/shard_map/ppermute | solution.py:41
  22.4 2.7 %collective-permute-start.8 = (bf16[8,128,256]{2,1,0:T(8,128)(2,1)S(1)}, bf16[8,128,256]{2,1,0:T(8,128)(2,1)}, u32[]{:S(2)}, u32[]{:S(2)}) collective-permute-start(bf16[8,128,256]{2,1,0:T(8,128)(2,1)S(1)} %pad_maximum_fusion.1.set0), channel_id=1, source_target_pairs={{0,6},{1,25},{2,0},{3,27},{4,2},{5,29},{6,4},{7,31},{8,14},{9,1},{... | collective-permute-start | bytes 1572872 | tf_op jit(solution)/shard_map/ppermute | solution.py:41
  28.6 6.3 %collective-permute-done.7.set2 = bf16[8,128,256]{2,1,0:T(8,128)(2,1)} collective-permute-done((bf16[8,128,256]{2,1,0:T(8,128)(2,1)S(1)}, bf16[8,128,256]{2,1,0:T(8,128)(2,1)}, u32[]{:S(2)}, u32[]{:S(2)}) %collective-permute-start.7) | collective-permute-done | bytes 524320 | tf_op jit(solution)/shard_map/ppermute | solution.py:41
  35.0 9.8 %shard_map.73 = bf16[4,128,256]{2,1,0:T(8,128)(2,1)} custom-call(s32[7]{0:T(128)} %pad_add_fusion.sc, bf16[8,128,256]{2,1,0:T(8,128)(2,1)} %copy-done.2, bf16[8,128,256]{2,1,0:T(8,128)(2,1)} %collective-permute-done.6.set1, bf16[8,128,256]{2,1,0:T(8,128)(2,1)} %collective-permute-done.7.set2, bf16[8,128,256]{2,1,0:T(8,128)(2,1)} %collective-permute-done.8.set3), custom_call_target="tpu_custom_call" | custom-call | bytes 600000 | tf_op jit(solution)/shard_map/pallas_call | solution.py:68
  44.9 3.3 %collective-permute-start.19 = (bf16[4,128,256]{2,1,0:T(8,128)(2,1)}, bf16[4,128,256]{2,1,0:T(8,128)(2,1)S(1)}, u32[]{:S(2)}, u32[]{:S(2)}) collective-permute-start(bf16[4,128,256]{2,1,0:T(8,128)(2,1)} %shard_map.73), channel_id=1, source_target_pairs={{0,64},{1,65},{2,66},{3,67},{4,68},{5,69},{6,70},{7,71},{8,72},{9,... | collective-permute-start | bytes 786440 | tf_op jit(solution)/shard_map/ppermute | solution.py:41
  48.2 3.5 %collective-permute-start.9 = (bf16[4,128,256]{2,1,0:T(8,128)(2,1)}, bf16[4,128,256]{2,1,0:T(8,128)(2,1)}, u32[]{:S(2)}, u32[]{:S(2)}) collective-permute-start(bf16[4,128,256]{2,1,0:T(8,128)(2,1)} %shard_map.73), channel_id=1, source_target_pairs={{0,1},{1,0},{2,3},{3,2},{4,5},{5,4},{6,7},{7,6},{8,9},{9,8},{10,11... | collective-permute-start | bytes 786440 | tf_op jit(solution)/shard_map/ppermute | solution.py:41
  51.7 5.5 %collective-permute-start.18 = (bf16[4,128,256]{2,1,0:T(8,128)(2,1)S(1)}, bf16[4,128,256]{2,1,0:T(8,128)(2,1)}, u32[]{:S(2)}, u32[]{:S(2)}) collective-permute-start(bf16[4,128,256]{2,1,0:T(8,128)(2,1)S(1)} %collective-permute-done.17), channel_id=1, source_target_pairs={{0,1},{1,0},{2,3},{3,2},{4,5},{5,4},{6,7},{7,6},{8,9},{9,8},{10,11... | collective-permute-start | bytes 786440 | tf_op jit(solution)/shard_map/ppermute | solution.py:41
  58.7 2.6 %collective-permute-start.20 = (bf16[4,128,256]{2,1,0:T(8,128)(2,1)S(1)}, bf16[4,128,256]{2,1,0:T(8,128)(2,1)}, u32[]{:S(2)}, u32[]{:S(2)}) collective-permute-start(bf16[4,128,256]{2,1,0:T(8,128)(2,1)S(1)} %collective-permute-done.19), channel_id=1, source_target_pairs={{0,1},{1,0},{2,3},{3,2},{4,5},{5,4},{6,7},{7,6},{8,9},{9,8},{10,11... | collective-permute-start | bytes 786440 | tf_op jit(solution)/shard_map/ppermute | solution.py:41
  61.9 2.9 %shard_map.74 = bf16[4,256,512]{2,1,0:T(8,128)(2,1)} custom-call(s32[16]{0:T(128)} %stack.189.sc, bf16[4,256,256]{2,1,0:T(8,128)(2,1)} %copy-done.1, bf16[4,256,256]{2,1,0:T(8,128)(2,1)} %collective-permute-done.13.oth), custom_call_target="tpu_custom_call" | custom-call | bytes 2000000 | tf_op jit(solution)/shard_map/pallas_call | solution.py:91
  71.0 1.9 %copy-done = bf16[16,256,512]{2,1,0:T(8,128)(2,1)S(1)} copy-done((bf16[16,256,512]{2,1,0:T(8,128)(2,1)S(1)}, bf16[16,256,512]{2,1,0:T(8,128)(2,1)}, u32[]{:S(2)}) %copy-start) | copy-done | bytes 4194328
  72.9 2.0 %shard_map.75 = (bf16[8,1,64,256]{3,2,1,0:T(8,128)(2,1)S(1)}, bf16[8,1,64,256]{3,2,1,0:T(8,128)(2,1)S(1)}, bf16[8,1,64,256]{3,2,1,0:T(8,128)(2,1)S(1)}, f32[8,1,64,256]{3,2,1,0:T(8,128)S(1)}) custom-call(s32[1]{0:T(128)} %bitcast.1.sc, bf16[16,256,512]{2,1,0:T(8,128)(2,1)S(1)} %copy-done, bf16[8,256,512]{2,1,0:T(8,128)(2,1)S(1)} %collective-permute-done.t_oth, ...), custom_call_target="tpu_custom_call" | custom-call | flops 1600000000 | bytes 4000000 | tf_op jit(solution)/shard_map/pallas_call | solution.py:128
  76.0 5.2 %shard_map.76 = (bf16[8,3,64,256]{3,2,1,0:T(8,128)(2,1)S(1)}, bf16[8,3,64,256]{3,2,1,0:T(8,128)(2,1)S(1)}, bf16[8,3,64,256]{3,2,1,0:T(8,128)(2,1)S(1)}, f32[8,3,64,256]{3,2,1,0:T(8,128)S(1)}) custom-call(s32[1]{0:T(128)} %bitcast.1.sc, bf16[16,256,512]{2,1,0:T(8,128)(2,1)S(1)} %copy-done, bf16[8,256,512]{2,1,0:T(8,128)(2,1)S(1)} %collective-permute-done.t_oth, ...), custom_call_target="tpu_custom_call" | custom-call | flops 4800000000 | bytes 12000000 | tf_op jit(solution)/shard_map/pallas_call | solution.py:128
  81.4 2.8 %collective-permute-start.24 = (bf16[8,3,64,256]{3,2,1,0:T(8,128)(2,1)S(1)}, bf16[8,3,64,256]{3,2,1,0:T(8,128)(2,1)S(1)}, u32[]{:S(2)}, u32[]{:S(2)}) collective-permute-start(bf16[8,3,64,256]{3,2,1,0:T(8,128)(2,1)S(1)} %get-tuple-element.19), channel_id=1, source_target_pairs={{0,16},{1,5},{2,18},{3,7},{4,20},{5,1},{6,22},{7,3},{8,24},{9,13},... | collective-permute-start | bytes 2359304 | tf_op jit(solution)/shard_map/ppermute | solution.py:41
  84.2 2.2 %collective-permute-start.15 = (bf16[8,1,64,256]{3,2,1,0:T(8,128)(2,1)S(1)}, bf16[8,1,64,256]{3,2,1,0:T(8,128)(2,1)S(1)}, u32[]{:S(2)}, u32[]{:S(2)}) collective-permute-start(bf16[8,1,64,256]{3,2,1,0:T(8,128)(2,1)S(1)} %get-tuple-element.15), channel_id=1, source_target_pairs={{0,16},{1,5},{2,18},{3,7},{4,20},{5,1},{6,22},{7,3},{8,24},{9,13},... | collective-permute-start | bytes 786440 | tf_op jit(solution)/shard_map/ppermute | solution.py:41
  86.4 1.6 %collective-permute-start.16 = (bf16[8,1,64,256]{3,2,1,0:T(8,128)(2,1)S(1)}, bf16[8,1,64,256]{3,2,1,0:T(8,128)(2,1)S(1)}, u32[]{:S(2)}, u32[]{:S(2)}) collective-permute-start(bf16[8,1,64,256]{3,2,1,0:T(8,128)(2,1)S(1)} %get-tuple-element.16), channel_id=1, source_target_pairs={{0,24},{1,7},{2,26},{3,1},{4,28},{5,3},{6,30},{7,5},{8,0},{9,15},{... | collective-permute-start | bytes 786440 | tf_op jit(solution)/shard_map/ppermute | solution.py:41
  88.0 17.0 %collective-permute-done.15 = bf16[8,1,64,256]{3,2,1,0:T(8,128)(2,1)S(1)} collective-permute-done((bf16[8,1,64,256]{3,2,1,0:T(8,128)(2,1)S(1)}, bf16[8,1,64,256]{3,2,1,0:T(8,128)(2,1)S(1)}, u32[]{:S(2)}, u32[]{:S(2)}) %collective-permute-start.15) | collective-permute-done | bytes 262176 | tf_op jit(solution)/shard_map/ppermute | solution.py:41
  105.1 3.3 %collective-permute-done.16 = bf16[8,1,64,256]{3,2,1,0:T(8,128)(2,1)S(1)} collective-permute-done((bf16[8,1,64,256]{3,2,1,0:T(8,128)(2,1)S(1)}, bf16[8,1,64,256]{3,2,1,0:T(8,128)(2,1)S(1)}, u32[]{:S(2)}, u32[]{:S(2)}) %collective-permute-start.16) | collective-permute-done | bytes 262176 | tf_op jit(solution)/shard_map/ppermute | solution.py:41
  110.4 1.8 %collective-permute-start.27 = (bf16[8,4,16,256]{3,2,1,0:T(8,128)(2,1)S(1)}, bf16[8,4,16,256]{3,2,1,0:T(8,128)(2,1)S(1)}, u32[]{:S(2)}, u32[]{:S(2)}) collective-permute-start(bf16[8,4,16,256]{3,2,1,0:T(8,128)(2,1)S(1)} %pad_maximum_fusion.4), channel_id=1, source_target_pairs={{0,4},{1,17},{2,6},{3,19},{4,0},{5,21},{6,2},{7,23},{8,12},{9,25},... | collective-permute-start | bytes 786440 | tf_op jit(solution)/shard_map/ppermute | solution.py:41
  113.6 2.5 %collective-permute-done.26 = bf16[8,4,16,256]{3,2,1,0:T(8,128)(2,1)S(1)} collective-permute-done((bf16[8,4,16,256]{3,2,1,0:T(8,128)(2,1)S(1)}, bf16[8,4,16,256]{3,2,1,0:T(8,128)(2,1)S(1)}, u32[]{:S(2)}, u32[]{:S(2)}) %collective-permute-start.26) | collective-permute-done | bytes 262176 | tf_op jit(solution)/shard_map/ppermute | solution.py:41
  116.1 2.9 %collective-permute-done.27 = bf16[8,4,16,256]{3,2,1,0:T(8,128)(2,1)S(1)} collective-permute-done((bf16[8,4,16,256]{3,2,1,0:T(8,128)(2,1)S(1)}, bf16[8,4,16,256]{3,2,1,0:T(8,128)(2,1)S(1)}, u32[]{:S(2)}, u32[]{:S(2)}) %collective-permute-start.27) | collective-permute-done | bytes 262176 | tf_op jit(solution)/shard_map/ppermute | solution.py:41
  121.3 1.6 %collective-permute-done.29 = bf16[8,16,256]{2,1,0:T(8,128)(2,1)S(1)} collective-permute-done((bf16[8,16,256]{2,1,0:T(8,128)(2,1)S(1)}, bf16[8,16,256]{2,1,0:T(8,128)(2,1)S(1)}, u32[]{:S(2)}, u32[]{:S(2)}) %collective-permute-start.29) | collective-permute-done | bytes 65568 | tf_op jit(solution)/shard_map/ppermute | solution.py:41
  123.0 1.6 %collective-permute-done.30 = bf16[8,16,256]{2,1,0:T(8,128)(2,1)S(1)} collective-permute-done((bf16[8,16,256]{2,1,0:T(8,128)(2,1)S(1)}, bf16[8,16,256]{2,1,0:T(8,128)(2,1)S(1)}, u32[]{:S(2)}, u32[]{:S(2)}) %collective-permute-start.30) | collective-permute-done | bytes 65568 | tf_op jit(solution)/shard_map/ppermute | solution.py:41
  125.5 4.5 %collective-permute-start.32 = (bf16[4,8,16,128]{3,2,1,0:T(8,128)(2,1)S(1)}, bf16[4,8,16,128]{3,2,1,0:T(8,128)(2,1)S(1)}, u32[]{:S(2)}, u32[]{:S(2)}) collective-permute-start(bf16[4,8,16,128]{3,2,1,0:T(8,128)(2,1)S(1)} %get-tuple-element.29), channel_id=1, source_target_pairs={{0,1},{1,0},{2,3},{3,2},{4,5},{5,4},{6,7},{7,6},{8,9},{9,8},{10,11... | collective-permute-start | bytes 393224 | tf_op jit(solution)/shard_map/ppermute | solution.py:41
  131.9 2.4 %shard_map.77 = bf16[96,16,128]{2,1,0:T(8,128)(2,1)} custom-call(s32[96]{0:T(128)} %select_reduce_fusion.sc, bf16[65,16,128]{2,1,0:T(8,128)(2,1)} %maximum_maximum_fusion.pieces), custom_call_target="tpu_custom_call" | custom-call | tf_op jit(solution)/shard_map/pallas_call | solution.py:155
  134.3 16.9 %all_to_all.5 = bf16[32,3,16,128]{3,2,1,0:T(8,128)(2,1)S(1)} all-to-all(bf16[32,3,16,128]{3,2,1,0:T(8,128)(2,1)} %bitcast.82), channel_id=1, replica_groups=mesh['grp'=4,'sub'=32] {'sub'}, dimensions={0} | all-to-all | bytes 786432 | tf_op jit(solution)/shard_map/all_to_all | solution.py:250
  151.5 1.5 reshape.123
  (98 shorter events, 26.2 us)
Async XLA Ops:
  1.6 5.3 %collective-permute-start.2 = (bf16[128,256]{1,0:T(8,128)(2,1)S(1)}, bf16[128,256]{1,0:T(8,128)(2,1)S(1)}, u32[]{:S(2)}, u32[]{:S(2)}) collective-permute-start(bf16[128,256]{1,0:T(8,128)(2,1)S(1)} %get-tuple-element.38), channel_id=1, source_target_pairs={{0,1},{1,0},{2,3},{3,2},{4,5},{5,4},{6,7},{7,6},{8,9},{9,8},{10,11... | collective-permute-start | bytes 196616 | tf_op jit(solution)/shard_map/ppermute | solution.py:41
  6.2 64.7 %collective-permute-start = (bf16[8,256,512]{2,1,0:T(8,128)(2,1)}, bf16[8,256,512]{2,1,0:T(8,128)(2,1)S(1)}, u32[]{:S(2)}, u32[]{:S(2)}) collective-permute-start(bf16[8,256,512]{2,1,0:T(8,128)(2,1)} %constant_dynamic-slice_fusion.3), channel_id=1, source_target_pairs={{0,1},{1,0},{2,3},{3,2},{4,5},{5,4},{6,7},{7,6},{8,9},{9,8},{10,11... | collective-permute-start | bytes 6291464 | tf_op jit(solution)/shard_map/ppermute | solution.py:41
  7.0 6.9 %collective-permute-start.3 = (bf16[2,128,256]{2,1,0:T(8,128)(2,1)S(1)}, bf16[2,128,256]{2,1,0:T(8,128)(2,1)S(1)}, u32[]{:S(2)}, u32[]{:S(2)}) collective-permute-start(bf16[2,128,256]{2,1,0:T(8,128)(2,1)S(1)} %maximum_select_fusion.4), channel_id=1, source_target_pairs={{0,8},{1,3},{2,10},{3,5},{4,12},{5,7},{6,14},{7,1},{8,16},{9,11},{... | collective-permute-start | bytes 393224 | tf_op jit(solution)/shard_map/ppermute | solution.py:41
  8.4 8.7 %collective-permute-start.4 = (bf16[2,128,256]{2,1,0:T(8,128)(2,1)S(1)}, bf16[2,128,256]{2,1,0:T(8,128)(2,1)S(1)}, u32[]{:S(2)}, u32[]{:S(2)}) collective-permute-start(bf16[2,128,256]{2,1,0:T(8,128)(2,1)S(1)} %maximum_select_fusion.4), channel_id=1, source_target_pairs={{0,16},{1,5},{2,18},{3,7},{4,20},{5,1},{6,22},{7,3},{8,24},{9,13},... | collective-permute-start | bytes 393224 | tf_op jit(solution)/shard_map/ppermute | solution.py:41
  11.0 7.8 %collective-permute-start.5 = (bf16[2,128,256]{2,1,0:T(8,128)(2,1)S(1)}, bf16[2,128,256]{2,1,0:T(8,128)(2,1)S(1)}, u32[]{:S(2)}, u32[]{:S(2)}) collective-permute-start(bf16[2,128,256]{2,1,0:T(8,128)(2,1)S(1)} %maximum_select_fusion.4), channel_id=1, source_target_pairs={{0,24},{1,7},{2,26},{3,1},{4,28},{5,3},{6,30},{7,5},{8,0},{9,15},{... | collective-permute-start | bytes 393224 | tf_op jit(solution)/shard_map/ppermute | solution.py:41
  12.1 7.8 %collective-permute-start.10 = (bf16[256,256]{1,0:T(8,128)(2,1)S(1)}, bf16[256,256]{1,0:T(8,128)(2,1)S(1)}, u32[]{:S(2)}, u32[]{:S(2)}) collective-permute-start(bf16[256,256]{1,0:T(8,128)(2,1)S(1)} %broadcast_multiply_fusion), channel_id=1, source_target_pairs={{0,32},{1,33},{2,34},{3,35},{4,36},{5,37},{6,38},{7,39},{8,40},{9,... | collective-permute-start | bytes 393224 | tf_op jit(solution)/shard_map/ppermute | solution.py:41
  13.8 8.5 %collective-permute-start.11 = (bf16[256,256]{1,0:T(8,128)(2,1)S(1)}, bf16[256,256]{1,0:T(8,128)(2,1)S(1)}, u32[]{:S(2)}, u32[]{:S(2)}) collective-permute-start(bf16[256,256]{1,0:T(8,128)(2,1)S(1)} %broadcast_multiply_fusion), channel_id=1, source_target_pairs={{0,64},{1,65},{2,66},{3,67},{4,68},{5,69},{6,70},{7,71},{8,72},{9,... | collective-permute-start | bytes 393224 | tf_op jit(solution)/shard_map/ppermute | solution.py:41
  17.1 7.9 %collective-permute-start.12 = (bf16[256,256]{1,0:T(8,128)(2,1)S(1)}, bf16[256,256]{1,0:T(8,128)(2,1)S(1)}, u32[]{:S(2)}, u32[]{:S(2)}) collective-permute-start(bf16[256,256]{1,0:T(8,128)(2,1)S(1)} %broadcast_multiply_fusion), channel_id=1, source_target_pairs={{0,96},{1,97},{2,98},{3,99},{4,100},{5,101},{6,102},{7,103},{8,104... | collective-permute-start | bytes 393224 | tf_op jit(solution)/shard_map/ppermute | solution.py:41
  18.9 9.7 %collective-permute-start.6 = (bf16[8,128,256]{2,1,0:T(8,128)(2,1)S(1)}, bf16[8,128,256]{2,1,0:T(8,128)(2,1)}, u32[]{:S(2)}, u32[]{:S(2)}) collective-permute-start(bf16[8,128,256]{2,1,0:T(8,128)(2,1)S(1)} %pad_maximum_fusion.1.set0), channel_id=1, source_target_pairs={{0,2},{1,9},{2,4},{3,11},{4,6},{5,13},{6,0},{7,15},{8,10},{9,17},{... | collective-permute-start | bytes 1572872 | tf_op jit(solution)/shard_map/ppermute | solution.py:41
  19.9 15.0 %collective-permute-start.7 = (bf16[8,128,256]{2,1,0:T(8,128)(2,1)S(1)}, bf16[8,128,256]{2,1,0:T(8,128)(2,1)}, u32[]{:S(2)}, u32[]{:S(2)}) collective-permute-start(bf16[8,128,256]{2,1,0:T(8,128)(2,1)S(1)} %pad_maximum_fusion.1.set0), channel_id=1, source_target_pairs={{0,4},{1,17},{2,6},{3,19},{4,0},{5,21},{6,2},{7,23},{8,12},{9,25},... | collective-permute-start | bytes 1572872 | tf_op jit(solution)/shard_map/ppermute | solution.py:41
  22.4 12.6 %collective-permute-start.8 = (bf16[8,128,256]{2,1,0:T(8,128)(2,1)S(1)}, bf16[8,128,256]{2,1,0:T(8,128)(2,1)}, u32[]{:S(2)}, u32[]{:S(2)}) collective-permute-start(bf16[8,128,256]{2,1,0:T(8,128)(2,1)S(1)} %pad_maximum_fusion.1.set0), channel_id=1, source_target_pairs={{0,6},{1,25},{2,0},{3,27},{4,2},{5,29},{6,4},{7,31},{8,14},{9,1},{... | collective-permute-start | bytes 1572872 | tf_op jit(solution)/shard_map/ppermute | solution.py:41
  27.1 21.1 %collective-permute-start.13 = (bf16[4,256,256]{2,1,0:T(8,128)(2,1)S(1)}, bf16[4,256,256]{2,1,0:T(8,128)(2,1)}, u32[]{:S(2)}, u32[]{:S(2)}) collective-permute-start(bf16[4,256,256]{2,1,0:T(8,128)(2,1)S(1)} %pad_maximum_fusion.2.own), channel_id=1, source_target_pairs={{0,1},{1,0},{2,3},{3,2},{4,5},{5,4},{6,7},{7,6},{8,9},{9,8},{10,11... | collective-permute-start | bytes 1572872 | tf_op jit(solution)/shard_map/ppermute | solution.py:41
  44.7 7.0 %collective-permute-start.17 = (bf16[4,128,256]{2,1,0:T(8,128)(2,1)}, bf16[4,128,256]{2,1,0:T(8,128)(2,1)S(1)}, u32[]{:S(2)}, u32[]{:S(2)}) collective-permute-start(bf16[4,128,256]{2,1,0:T(8,128)(2,1)} %shard_map.73), channel_id=1, source_target_pairs={{0,32},{1,33},{2,34},{3,35},{4,36},{5,37},{6,38},{7,39},{8,40},{9,... | collective-permute-start | bytes 786440 | tf_op jit(solution)/shard_map/ppermute | solution.py:41
  44.9 13.8 %collective-permute-start.19 = (bf16[4,128,256]{2,1,0:T(8,128)(2,1)}, bf16[4,128,256]{2,1,0:T(8,128)(2,1)S(1)}, u32[]{:S(2)}, u32[]{:S(2)}) collective-permute-start(bf16[4,128,256]{2,1,0:T(8,128)(2,1)} %shard_map.73), channel_id=1, source_target_pairs={{0,64},{1,65},{2,66},{3,67},{4,68},{5,69},{6,70},{7,71},{8,72},{9,... | collective-permute-start | bytes 786440 | tf_op jit(solution)/shard_map/ppermute | solution.py:41
  48.2 18.9 %collective-permute-start.21 = (bf16[4,128,256]{2,1,0:T(8,128)(2,1)}, bf16[4,128,256]{2,1,0:T(8,128)(2,1)S(1)}, u32[]{:S(2)}, u32[]{:S(2)}) collective-permute-start(bf16[4,128,256]{2,1,0:T(8,128)(2,1)} %shard_map.73), channel_id=1, source_target_pairs={{0,96},{1,97},{2,98},{3,99},{4,100},{5,101},{6,102},{7,103},{8,104... | collective-permute-start | bytes 786440 | tf_op jit(solution)/shard_map/ppermute | solution.py:41
  48.2 18.9 %collective-permute-start.9 = (bf16[4,128,256]{2,1,0:T(8,128)(2,1)}, bf16[4,128,256]{2,1,0:T(8,128)(2,1)}, u32[]{:S(2)}, u32[]{:S(2)}) collective-permute-start(bf16[4,128,256]{2,1,0:T(8,128)(2,1)} %shard_map.73), channel_id=1, source_target_pairs={{0,1},{1,0},{2,3},{3,2},{4,5},{5,4},{6,7},{7,6},{8,9},{9,8},{10,11... | collective-permute-start | bytes 786440 | tf_op jit(solution)/shard_map/ppermute | solution.py:41
  51.7 16.6 %collective-permute-start.18 = (bf16[4,128,256]{2,1,0:T(8,128)(2,1)S(1)}, bf16[4,128,256]{2,1,0:T(8,128)(2,1)}, u32[]{:S(2)}, u32[]{:S(2)}) collective-permute-start(bf16[4,128,256]{2,1,0:T(8,128)(2,1)S(1)} %collective-permute-done.17), channel_id=1, source_target_pairs={{0,1},{1,0},{2,3},{3,2},{4,5},{5,4},{6,7},{7,6},{8,9},{9,8},{10,11... | collective-permute-start | bytes 786440 | tf_op jit(solution)/shard_map/ppermute | solution.py:41
  58.7 10.8 %collective-permute-start.20 = (bf16[4,128,256]{2,1,0:T(8,128)(2,1)S(1)}, bf16[4,128,256]{2,1,0:T(8,128)(2,1)}, u32[]{:S(2)}, u32[]{:S(2)}) collective-permute-start(bf16[4,128,256]{2,1,0:T(8,128)(2,1)S(1)} %collective-permute-done.19), channel_id=1, source_target_pairs={{0,1},{1,0},{2,3},{3,2},{4,5},{5,4},{6,7},{7,6},{8,9},{9,8},{10,11... | collective-permute-start | bytes 786440 | tf_op jit(solution)/shard_map/ppermute | solution.py:41
  67.0 3.6 %collective-permute-start.22 = (bf16[4,128,256]{2,1,0:T(8,128)(2,1)S(1)}, bf16[4,128,256]{2,1,0:T(8,128)(2,1)S(1)}, u32[]{:S(2)}, u32[]{:S(2)}) collective-permute-start(bf16[4,128,256]{2,1,0:T(8,128)(2,1)S(1)} %collective-permute-done.21), channel_id=1, source_target_pairs={{0,1},{1,0},{2,3},{3,2},{4,5},{5,4},{6,7},{7,6},{8,9},{9,8},{10,11... | collective-permute-start | bytes 786440 | tf_op jit(solution)/shard_map/ppermute | solution.py:41
  74.9 11.5 %collective-permute-start.14 = (bf16[8,1,64,256]{3,2,1,0:T(8,128)(2,1)S(1)}, bf16[8,1,64,256]{3,2,1,0:T(8,128)(2,1)S(1)}, u32[]{:S(2)}, u32[]{:S(2)}) collective-permute-start(bf16[8,1,64,256]{3,2,1,0:T(8,128)(2,1)S(1)} %get-tuple-element.14), channel_id=1, source_target_pairs={{0,8},{1,3},{2,10},{3,5},{4,12},{5,7},{6,14},{7,1},{8,16},{9,11},{... | collective-permute-start | bytes 786440 | tf_op jit(solution)/shard_map/ppermute | solution.py:41
  81.3 27.3 %collective-permute-start.23 = (bf16[8,3,64,256]{3,2,1,0:T(8,128)(2,1)S(1)}, bf16[8,3,64,256]{3,2,1,0:T(8,128)(2,1)S(1)}, u32[]{:S(2)}, u32[]{:S(2)}) collective-permute-start(bf16[8,3,64,256]{3,2,1,0:T(8,128)(2,1)S(1)} %get-tuple-element.18), channel_id=1, source_target_pairs={{0,8},{1,3},{2,10},{3,5},{4,12},{5,7},{6,14},{7,1},{8,16},{9,11},{... | collective-permute-start | bytes 2359304 | tf_op jit(solution)/shard_map/ppermute | solution.py:41
  81.4 27.2 %collective-permute-start.24 = (bf16[8,3,64,256]{3,2,1,0:T(8,128)(2,1)S(1)}, bf16[8,3,64,256]{3,2,1,0:T(8,128)(2,1)S(1)}, u32[]{:S(2)}, u32[]{:S(2)}) collective-permute-start(bf16[8,3,64,256]{3,2,1,0:T(8,128)(2,1)S(1)} %get-tuple-element.19), channel_id=1, source_target_pairs={{0,16},{1,5},{2,18},{3,7},{4,20},{5,1},{6,22},{7,3},{8,24},{9,13},... | collective-permute-start | bytes 2359304 | tf_op jit(solution)/shard_map/ppermute | solution.py:41
  84.2 24.4 %collective-permute-start.25 = (bf16[8,3,64,256]{3,2,1,0:T(8,128)(2,1)S(1)}, bf16[8,3,64,256]{3,2,1,0:T(8,128)(2,1)S(1)}, u32[]{:S(2)}, u32[]{:S(2)}) collective-permute-start(bf16[8,3,64,256]{3,2,1,0:T(8,128)(2,1)S(1)} %get-tuple-element.20), channel_id=1, source_target_pairs={{0,24},{1,7},{2,26},{3,1},{4,28},{5,3},{6,30},{7,5},{8,0},{9,15},{... | collective-permute-start | bytes 2359304 | tf_op jit(solution)/shard_map/ppermute | solution.py:41
  84.2 20.9 %collective-permute-start.15 = (bf16[8,1,64,256]{3,2,1,0:T(8,128)(2,1)S(1)}, bf16[8,1,64,256]{3,2,1,0:T(8,128)(2,1)S(1)}, u32[]{:S(2)}, u32[]{:S(2)}) collective-permute-start(bf16[8,1,64,256]{3,2,1,0:T(8,128)(2,1)S(1)} %get-tuple-element.15), channel_id=1, source_target_pairs={{0,16},{1,5},{2,18},{3,7},{4,20},{5,1},{6,22},{7,3},{8,24},{9,13},... | collective-permute-start | bytes 786440 | tf_op jit(solution)/shard_map/ppermute | solution.py:41
  86.4 22.0 %collective-permute-start.16 = (bf16[8,1,64,256]{3,2,1,0:T(8,128)(2,1)S(1)}, bf16[8,1,64,256]{3,2,1,0:T(8,128)(2,1)S(1)}, u32[]{:S(2)}, u32[]{:S(2)}) collective-permute-start(bf16[8,1,64,256]{3,2,1,0:T(8,128)(2,1)S(1)} %get-tuple-element.16), channel_id=1, source_target_pairs={{0,24},{1,7},{2,26},{3,1},{4,28},{5,3},{6,30},{7,5},{8,0},{9,15},{... | collective-permute-start | bytes 786440 | tf_op jit(solution)/shard_map/ppermute | solution.py:41
  109.3 6.8 %collective-permute-start.26 = (bf16[8,4,16,256]{3,2,1,0:T(8,128)(2,1)S(1)}, bf16[8,4,16,256]{3,2,1,0:T(8,128)(2,1)S(1)}, u32[]{:S(2)}, u32[]{:S(2)}) collective-permute-start(bf16[8,4,16,256]{3,2,1,0:T(8,128)(2,1)S(1)} %pad_maximum_fusion.3), channel_id=1, source_target_pairs={{0,2},{1,9},{2,4},{3,11},{4,6},{5,13},{6,0},{7,15},{8,10},{9,17},{... | collective-permute-start | bytes 786440 | tf_op jit(solution)/shard_map/ppermute | solution.py:41
  110.4 8.5 %collective-permute-start.27 = (bf16[8,4,16,256]{3,2,1,0:T(8,128)(2,1)S(1)}, bf16[8,4,16,256]{3,2,1,0:T(8,128)(2,1)S(1)}, u32[]{:S(2)}, u32[]{:S(2)}) collective-permute-start(bf16[8,4,16,256]{3,2,1,0:T(8,128)(2,1)S(1)} %pad_maximum_fusion.4), channel_id=1, source_target_pairs={{0,4},{1,17},{2,6},{3,19},{4,0},{5,21},{6,2},{7,23},{8,12},{9,25},... | collective-permute-start | bytes 786440 | tf_op jit(solution)/shard_map/ppermute | solution.py:41
  112.3 7.4 %collective-permute-start.28 = (bf16[8,4,16,256]{3,2,1,0:T(8,128)(2,1)S(1)}, bf16[8,4,16,256]{3,2,1,0:T(8,128)(2,1)S(1)}, u32[]{:S(2)}, u32[]{:S(2)}) collective-permute-start(bf16[8,4,16,256]{3,2,1,0:T(8,128)(2,1)S(1)} %pad_maximum_fusion.5), channel_id=1, source_target_pairs={{0,6},{1,25},{2,0},{3,27},{4,2},{5,29},{6,4},{7,31},{8,14},{9,1},{... | collective-permute-start | bytes 786440 | tf_op jit(solution)/shard_map/ppermute | solution.py:41
  119.8 3.2 %collective-permute-start.29 = (bf16[8,16,256]{2,1,0:T(8,128)(2,1)S(1)}, bf16[8,16,256]{2,1,0:T(8,128)(2,1)S(1)}, u32[]{:S(2)}, u32[]{:S(2)}) collective-permute-start(bf16[8,16,256]{2,1,0:T(8,128)(2,1)S(1)} %get-tuple-element.31), channel_id=1, source_target_pairs={{0,96},{1,97},{2,98},{3,99},{4,100},{5,101},{6,102},{7,103},{8,104... | collective-permute-start | bytes 196616 | tf_op jit(solution)/shard_map/ppermute | solution.py:41
  119.9 4.7 %collective-permute-start.30 = (bf16[8,16,256]{2,1,0:T(8,128)(2,1)S(1)}, bf16[8,16,256]{2,1,0:T(8,128)(2,1)S(1)}, u32[]{:S(2)}, u32[]{:S(2)}) collective-permute-start(bf16[8,16,256]{2,1,0:T(8,128)(2,1)S(1)} %get-tuple-element.33), channel_id=1, source_target_pairs={{0,64},{1,65},{2,66},{3,67},{4,68},{5,69},{6,70},{7,71},{8,72},{9,... | collective-permute-start | bytes 196616 | tf_op jit(solution)/shard_map/ppermute | solution.py:41
  120.0 5.4 %collective-permute-start.31 = (bf16[8,16,256]{2,1,0:T(8,128)(2,1)S(1)}, bf16[8,16,256]{2,1,0:T(8,128)(2,1)S(1)}, u32[]{:S(2)}, u32[]{:S(2)}) collective-permute-start(bf16[8,16,256]{2,1,0:T(8,128)(2,1)S(1)} %get-tuple-element.32), channel_id=1, source_target_pairs={{0,32},{1,33},{2,34},{3,35},{4,36},{5,37},{6,38},{7,39},{8,40},{9,... | collective-permute-start | bytes 196616 | tf_op jit(solution)/shard_map/ppermute | solution.py:41
  125.5 5.5 %collective-permute-start.32 = (bf16[4,8,16,128]{3,2,1,0:T(8,128)(2,1)S(1)}, bf16[4,8,16,128]{3,2,1,0:T(8,128)(2,1)S(1)}, u32[]{:S(2)}, u32[]{:S(2)}) collective-permute-start(bf16[4,8,16,128]{3,2,1,0:T(8,128)(2,1)S(1)} %get-tuple-element.29), channel_id=1, source_target_pairs={{0,1},{1,0},{2,3},{3,2},{4,5},{5,4},{6,7},{7,6},{8,9},{9,8},{10,11... | collective-permute-start | bytes 393224 | tf_op jit(solution)/shard_map/ppermute | solution.py:41
  (8 other events, 90.1 us)

commit v3 on v2

--- a/solution.py
+++ b/solution.py
@@ -9,6 +9,7 @@
 AXES = ("grp", "sub")
 BF = jnp.bfloat16
 F32 = jnp.float32
+MIB = 1024 * 1024
 STACK = 4
 
 
@@ -41,6 +42,10 @@
     return lax.ppermute(value, AXES, permutation)
 
 
+def tie(*values):
+    return lax.optimization_barrier(values)
+
+
 def whole(shape):
     return pl.BlockSpec(shape, lambda *_: (0,) * len(shape))
 
@@ -71,10 +76,11 @@
             num_scalar_prefetch=1,
             grid=(1,),
             in_specs=[pl.BlockSpec(memory_space=pl.ANY)] * 4,
-            out_specs=pl.BlockSpec(memory_space=pl.ANY),
+            out_specs=whole((4, 128, 256)),
             scratch_shapes=[pltpu.SemaphoreType.DMA((4,))],
         ),
         out_shape=jax.ShapeDtypeStruct((4, 128, 256), BF),
+        compiler_params=pltpu.CompilerParams(vmem_limit_bytes=4 * MIB),
         cost_estimate=pl.CostEstimate(flops=0, bytes_accessed=600_000, transcendentals=0),
     )(scalars, *sets)
 
@@ -82,28 +88,41 @@
 def order_body(sc, own, oth, out):
     for k in range(16):
         rows = pl.ds(pl.multiple_of(sc[k] * 16, 16), 16)
-        for g in range(4):
-            out[g, k * 16 : (k + 1) * 16, 0:256] = own[g, rows, :]
-            out[g, k * 16 : (k + 1) * 16, 256:512] = oth[g, rows, :]
+        to = slice(k * 16, (k + 1) * 16)
+        for r in range(out.shape[0]):
+            out[r, to, 0:256] = own[r, rows, :]
+            out[r, to, 256:512] = oth[r, rows, :]
 
 
 def order_rows(strips, own, oth):
+    count = own.shape[0]
     return pl.pallas_call(
         order_body,
         grid_spec=pltpu.PrefetchScalarGridSpec(
             num_scalar_prefetch=1,
             grid=(1,),
-            in_specs=[whole((4, 256, 256))] * 2,
-            out_specs=whole((4, 256, 512)),
-        ),
-        out_shape=jax.ShapeDtypeStruct((4, 256, 512), BF),
-        cost_estimate=pl.CostEstimate(flops=0, bytes_accessed=2_000_000, transcendentals=0),
+            in_specs=[whole((count, 256, 256))] * 2,
+            out_specs=whole((count, 256, 512)),
+        ),
+        out_shape=jax.ShapeDtypeStruct((count, 256, 512), BF),
+        compiler_params=pltpu.CompilerParams(vmem_limit_bytes=8 * MIB),
+        cost_estimate=pl.CostEstimate(flops=0, bytes_accessed=500_000 * count, transcendentals=0),
     )(strips, own, oth)
 
 
-def products_body(sc, t_own, t_oth, go, gv, send1, send2, send3, keep):
+def products_body(sc, t_own, t_oth, gv, *refs):
+    halves, (send1, send2, send3, keep, go) = refs[:-5], refs[-5:]
+    count = len(halves) // 2
     c = sc[0]
-    count = go.shape[0] // 2
+
+    @pl.when(pl.program_id(0) == 0)
+    def _():
+        for r in range(count):
+            for n, half in enumerate((c, 1 - c)):
+                for k in range(4):
+                    rows = pl.ds(pl.multiple_of((k % 2) * 256 + half * 128, 128), 128)
+                    go[2 * r + k // 2, rows, :] = halves[2 * r + n][k]
+
     for r in range(count):
         half_own = jnp.dot(
             t_own[...].reshape(STACK * 256, 512), go[2 * r + c], preferred_element_type=F32
@@ -121,29 +140,28 @@
             keep[p, r] = out[192:256]
 
 
-def products_of(core, t_own, t_oth, go, gv):
+def products_of(core, t_own, t_oth, gv, halves):
     count = gv.shape[0]
     block = pl.BlockSpec((STACK, count, 64, 256), lambda p, sc: (p, 0, 0, 0))
     shape = (8, count, 64, 256)
+    functions = pl.BlockSpec((STACK, 256, 512), lambda p, sc: (sc[0] * (8 // STACK) + p, 0, 0))
     return pl.pallas_call(
         products_body,
         grid_spec=pltpu.PrefetchScalarGridSpec(
             num_scalar_prefetch=1,
             grid=(8 // STACK,),
-            in_specs=[
-                pl.BlockSpec((STACK, 256, 512), lambda p, sc: (sc[0] * (8 // STACK) + p, 0, 0)),
-                pl.BlockSpec((STACK, 256, 512), lambda p, sc: (p, 0, 0)),
-                whole((2 * count, 512, 256)),
-                whole((count, 256, 512)),
-            ],
+            in_specs=[functions] * 2
+            + [whole((count, 256, 512))]
+            + [whole((4, 128, 256))] * (2 * count),
             out_specs=[block] * 4,
+            scratch_shapes=[pltpu.VMEM((2 * count, 512, 256), BF)],
         ),
         out_shape=[jax.ShapeDtypeStruct(shape, BF)] * 3 + [jax.ShapeDtypeStruct(shape, F32)],
-        compiler_params=pltpu.CompilerParams(vmem_limit_bytes=40 * 1024 * 1024),
+        compiler_params=pltpu.CompilerParams(vmem_limit_bytes=(12 + 4 * count) * MIB),
         cost_estimate=pl.CostEstimate(
             flops=1_600_000_000 * count, bytes_accessed=4_000_000 * count, transcendentals=0
         ),
-    )(core, t_own, t_oth, go, gv)
+    )(core, pltpu.with_memory_space_constraint(t_own, pltpu.HBM), t_oth, gv, *halves)
 
 
 def slots_body(sc, pieces, out):
@@ -161,6 +179,7 @@
             out_specs=whole((32 * CAP, 16, 128)),
         ),
         out_shape=jax.ShapeDtypeStruct((32 * CAP, 16, 128), BF),
+        compiler_params=pltpu.CompilerParams(vmem_limit_bytes=4 * MIB),
     )(source, pieces)
 
 
@@ -178,48 +197,46 @@
         lax.dynamic_slice_in_dim(go, c * 128, 128, 0),
         move(lax.dynamic_slice_in_dim(go, (1 - c) * 128, 128, 0), CORE),
     )
+    go, theirs = tie(go, three_centre)
+    t_oth = move(theirs, CORE)
+
     near = jnp.concatenate([go] + [move(go, FIRST[d]) for d in (1, 2, 3)])
+    gv = green_virt * virt_mask[0, 0].astype(BF)
+    near, gv = tie(near, gv)
     sets = [near] + [move(near, SECOND[e]) for e in (1, 2, 3)]
-
-    t_oth = move(lax.dynamic_slice_in_dim(three_centre, (1 - c) * 8, 8, 0), CORE)
-
-    gv = green_virt * virt_mask[0, 0].astype(BF)
-    gv = jnp.stack([gv] + [move(gv, DEPTH[r]) for r in (1, 2, 3)])
-    strips = [
-        jnp.where(c == 0, s1 * 4 + s2, s2 * 4 + s1)
-        for s1 in [(q1 + d) % 4 for d in (1, 2, 3, 0)]
-        for s2 in [(q2 + e) % 4 for e in range(4)]
-    ]
-    gv = order_rows(jnp.stack(strips).astype(jnp.int32), gv, move(gv, CORE))
+    gv_far = jnp.stack([move(gv, DEPTH[r]) for r in (1, 2, 3)])
+    gv = gv.reshape(1, 256, 256)
+    strips = jnp.stack(
+        [
+            jnp.where(c == 0, s1 * 4 + s2, s2 * 4 + s1)
+            for s1 in [(q1 + d) % 4 for d in (1, 2, 3, 0)]
+            for s2 in [(q2 + e) % 4 for e in range(4)]
+        ]
+    ).astype(jnp.int32)
+    gv_near = order_rows(strips, gv, move(gv, CORE))
 
     partners = by_core(pair_blocks[0], move(pair_blocks, CORE)[0]).reshape(4)
     places = jnp.concatenate([jnp.stack([c, q1, q2]), partners]).astype(jnp.int32)
+    places, gv_near, gv_far, *sets = tie(places, gv_near, gv_far, *sets)
     picked = pick(places, *sets)
-    picks = [picked] + [move(picked, DEPTH[r]) for r in (1, 2, 3)]
-
-    def rows_of(part):
-        halves = by_core(part, move(part, CORE))
-        return halves.transpose(1, 0, 2, 3).reshape(2, 512, 256)
+    arriving = [move(picked, DEPTH[r]) for r in (1, 2, 3)]
+    gv_far = order_rows(strips, gv_far, move(gv_far, CORE))
 
     core = c.reshape(1).astype(jnp.int32)
-    lists = []
-    for begin, end in ((0, 1), (1, 4)):
-        lists.append(
-            products_of(
-                core,
-                three_centre,
-                t_oth,
-                jnp.concatenate([rows_of(picks[r]) for r in range(begin, end)]),
-                gv[begin:end],
-            )
-        )
-
-    sums = []
-    for send1, send2, send3, keep in lists:
-        total = keep
-        for d, send in ((1, send1), (2, send2), (3, send3)):
-            total = total + move(send, FIRST[d]).astype(F32)
-        sums.append(total)
+    sends0 = products_of(core, three_centre, t_oth, gv_near, (picked, move(picked, CORE)))
+    got0 = [move(sends0[d - 1], FIRST[d]) for d in (1, 2, 3)]
+    *got0, a1, a2, a3 = tie(*got0, *arriving)
+    halves = [h for a in (a1, a2, a3) for h in (a, move(a, CORE))]
+    sends1 = products_of(core, three_centre, t_oth, gv_far, halves)
+
+    def sum_of(sends, got):
+        total = sends[3]
+        for part in got:
+            total = total + part.astype(F32)
+        return total
+
+    got1 = [move(sends1[d - 1], FIRST[d]) for d in (1, 2, 3)]
+    sums = [sum_of(sends0, got0), sum_of(sends1, got1)]
 
     def strip(e):
         return jnp.concatenate([t[:, :, e * 16 : (e + 1) * 16] for t in sums], axis=1)

time: 154 us -> 131 us (0.85)
  starting transfers between devices: 54.2 us -> 42.8 us
  waiting for transfers between devices: 39.8 us -> 51.2 us
  Pallas kernels: 22.3 us -> 13.4 us
  local copies, waits for them, and re-layouts: 10.2 us -> 2.26 us
  other arithmetic: 7.88 us -> 4.58 us
  blocking collectives: 16.9 us -> 15.1 us
    ppermute x33 -> x34, waiting for transfers between devices: 39.8 us -> 51.2 us  [move(): return lax.ppermute(value, AXES, permutation)]
    ppermute x33 -> x34, starting transfers between devices: 54.2 us -> 42.8 us  [move(): return lax.ppermute(value, AXES, permutation)]
    pallas_call x1, Pallas kernels: 9.76 us -> 1.09 us  [pick(): pl.pallas_call(pick_body, grid_spec=pltpu.PrefetchScalarGridSpec(num_scal...]
    transpose x4 -> x0, other arithmetic: 3.41 us -> none  [rows_of(): return halves.transpose(1, 0, 2, 3).reshape(2, 512, 256)]
    pallas_call x2, Pallas kernels: 7.22 us -> 10.5 us  [products_of(): pl.pallas_call(products_body, grid_spec=pltpu.PrefetchScalarGridSpec(num_...]
    dynamic_slice x1 -> x0, local copies, waits for them, and re-layouts: 3.12 us -> none  [per_device(): lax.dynamic_slice_in_dim(three_centre, (1 - c) * 8, 8, 0)]
    slice x2 -> x0, local copies, waits for them, and re-layouts: 2.2 us -> none  [per_device(): gv[begin:end]]
    unnamed x14 -> x4, local copies, waits for them, and re-layouts: 1.98 us -> 0.01 us
  transfers between devices with their start and end apart: 33 -> 34, of which waited for: 13 -> 19; matrix products, arithmetic and copies ran while one was open for 8% -> 1% of each run, Pallas kernels for 12% -> 4%
where the time goes in v3:
time: 131 us
  waiting for transfers between devices  51.2 us (39%)
  starting transfers between devices  42.8 us (33%)
  blocking collectives  15.1 us (12%)
  Pallas kernels  13.4 us (10%)
  other arithmetic  4.58 us (3%)
  local copies, waits for them, and re-layouts  2.26 us (2%)
  between operations  1.58 us (1%)
    ppermute x34, waiting for transfers between devices, move(): return lax.ppermute(value, AXES, permutation)  51.2 us
    ppermute x34, starting transfers between devices, move(): return lax.ppermute(value, AXES, permutation)  42.8 us
    all_to_all x1, blocking collectives, per_device(): lax.all_to_all(outgoing.reshape(32, CAP, 16, 128), 'sub', split_axis=0, c...  15.1 us
    pallas_call x2, Pallas kernels, products_of(): pl.pallas_call(products_body, grid_spec=pltpu.PrefetchScalarGridSpec(num_...  10.5 us
  transfers between devices with their start and end apart: 34, of which 19 were waited for; matrix products, arithmetic and copies ran while one was open for 1% of the time, Pallas kernels for 4%

profile of v3, /device:TPU:1, one launch (start us, length us, event | category | flops | bytes accessed | tf_op | source)
XLA Modules:
  0.0 130.9 jit_solution(13711026459729991746)
XLA Ops:
  1.6 1.5 %collective-permute-start = (bf16[128,256]{1,0:T(8,128)(2,1)S(1)}, bf16[128,256]{1,0:T(8,128)(2,1)S(1)}, u32[]{:S(2)}, u32[]{:S(2)}) collective-permute-start(bf16[128,256]{1,0:T(8,128)(2,1)S(1)} %get-tuple-element.72), channel_id=1, source_target_pairs={{0,1},{1,0},{2,3},{3,2},{4,5},{5,4},{6,7},{7,6},{8,9},{9,8},{10,11... | collective-permute-start | bytes 196616 | tf_op jit(solution)/shard_map/ppermute | solution.py:42
  5.1 2.9 %collective-permute-start.5 = (bf16[2,128,256]{2,1,0:T(8,128)(2,1)S(1)}, bf16[2,128,256]{2,1,0:T(8,128)(2,1)S(1)}, u32[]{:S(2)}, u32[]{:S(2)}) collective-permute-start(bf16[2,128,256]{2,1,0:T(8,128)(2,1)S(1)} %maximum_select_fusion), channel_id=1, source_target_pairs={{0,24},{1,7},{2,26},{3,1},{4,28},{5,3},{6,30},{7,5},{8,0},{9,15},{... | collective-permute-start | bytes 393224 | tf_op jit(solution)/shard_map/ppermute | solution.py:42
  10.0 1.4 %collective-permute-done.5 = bf16[2,128,256]{2,1,0:T(8,128)(2,1)S(1)} collective-permute-done((bf16[2,128,256]{2,1,0:T(8,128)(2,1)S(1)}, bf16[2,128,256]{2,1,0:T(8,128)(2,1)S(1)}, u32[]{:S(2)}, u32[]{:S(2)}) %collective-permute-start.5) | collective-permute-done | bytes 131104 | tf_op jit(solution)/shard_map/ppermute | solution.py:42
  11.3 2.3 %collective-permute-done.4 = bf16[2,128,256]{2,1,0:T(8,128)(2,1)S(1)} collective-permute-done((bf16[2,128,256]{2,1,0:T(8,128)(2,1)S(1)}, bf16[2,128,256]{2,1,0:T(8,128)(2,1)S(1)}, u32[]{:S(2)}, u32[]{:S(2)}) %collective-permute-start.4) | collective-permute-done | bytes 131104 | tf_op jit(solution)/shard_map/ppermute | solution.py:42
  13.6 1.4 %collective-permute-done.3 = bf16[2,128,256]{2,1,0:T(8,128)(2,1)S(1)} collective-permute-done((bf16[2,128,256]{2,1,0:T(8,128)(2,1)S(1)}, bf16[2,128,256]{2,1,0:T(8,128)(2,1)S(1)}, u32[]{:S(2)}, u32[]{:S(2)}) %collective-permute-start.3) | collective-permute-done | bytes 131104 | tf_op jit(solution)/shard_map/ppermute | solution.py:42
  15.1 1.1 collective-permute-start.6
  16.2 3.8 %collective-permute-start.9 = (bf16[256,256]{1,0:T(8,128)(2,1)S(1)}, bf16[256,256]{1,0:T(8,128)(2,1)S(1)}, u32[]{:S(2)}, u32[]{:S(2)}) collective-permute-start(bf16[256,256]{1,0:T(8,128)(2,1)S(1)} %broadcast_multiply_fusion), channel_id=1, source_target_pairs={{0,96},{1,97},{2,98},{3,99},{4,100},{5,101},{6,102},{7,103},{8,104... | collective-permute-start | bytes 393224 | tf_op jit(solution)/shard_map/ppermute | solution.py:42
  20.4 1.6 %collective-permute-start.12 = (bf16[8,128,256]{2,1,0:T(8,128)(2,1)S(1)}, bf16[8,128,256]{2,1,0:T(8,128)(2,1)S(1)}, u32[]{:S(2)}, u32[]{:S(2)}) collective-permute-start(bf16[8,128,256]{2,1,0:T(8,128)(2,1)S(1)} %pad_maximum_fusion.set0), channel_id=1, source_target_pairs={{0,6},{1,25},{2,0},{3,27},{4,2},{5,29},{6,4},{7,31},{8,14},{9,1},{... | collective-permute-start | bytes 1572872 | tf_op jit(solution)/shard_map/ppermute | solution.py:42
  23.3 1.6 %collective-permute-start.8 = (bf16[256,256]{1,0:T(8,128)(2,1)S(1)}, bf16[256,256]{1,0:T(8,128)(2,1)S(1)}, u32[]{:S(2)}, u32[]{:S(2)}) collective-permute-start(bf16[256,256]{1,0:T(8,128)(2,1)S(1)} %broadcast_multiply_fusion), channel_id=1, source_target_pairs={{0,64},{1,65},{2,66},{3,67},{4,68},{5,69},{6,70},{7,71},{8,72},{9,... | collective-permute-start | bytes 393224 | tf_op jit(solution)/shard_map/ppermute | solution.py:42
  25.0 4.0 %collective-permute-done.8 = bf16[256,256]{1,0:T(8,128)(2,1)S(1)} collective-permute-done((bf16[256,256]{1,0:T(8,128)(2,1)S(1)}, bf16[256,256]{1,0:T(8,128)(2,1)S(1)}, u32[]{:S(2)}, u32[]{:S(2)}) %collective-permute-start.8) | collective-permute-done | bytes 131104 | tf_op jit(solution)/shard_map/ppermute | solution.py:42
  30.6 4.0 %collective-permute-done.7 = bf16[256,256]{1,0:T(8,128)(2,1)S(1)} collective-permute-done((bf16[256,256]{1,0:T(8,128)(2,1)S(1)}, bf16[256,256]{1,0:T(8,128)(2,1)S(1)}, u32[]{:S(2)}, u32[]{:S(2)}) %collective-permute-start.7) | collective-permute-done | bytes 131104 | tf_op jit(solution)/shard_map/ppermute | solution.py:42
  34.6 2.7 %collective-permute-done.10.set1 = bf16[8,128,256]{2,1,0:T(8,128)(2,1)S(1)} collective-permute-done((bf16[8,128,256]{2,1,0:T(8,128)(2,1)S(1)}, bf16[8,128,256]{2,1,0:T(8,128)(2,1)S(1)}, u32[]{:S(2)}, u32[]{:S(2)}) %collective-permute-start.10) | collective-permute-done | bytes 524320 | tf_op jit(solution)/shard_map/ppermute | solution.py:42
  38.5 2.5 %collective-permute-start.13 = (bf16[4,128,256]{2,1,0:T(8,128)(2,1)S(1)}, bf16[4,128,256]{2,1,0:T(8,128)(2,1)S(1)}, u32[]{:S(2)}, u32[]{:S(2)}) collective-permute-start(bf16[4,128,256]{2,1,0:T(8,128)(2,1)S(1)} %shard_map.74.refs_0_), channel_id=1, source_target_pairs={{0,1},{1,0},{2,3},{3,2},{4,5},{5,4},{6,7},{7,6},{8,9},{9,8},{10,11... | collective-permute-start | bytes 786440 | tf_op jit(solution)/shard_map/ppermute | solution.py:42
  41.2 1.3 %collective-permute-start.17 = (bf16[4,128,256]{2,1,0:T(8,128)(2,1)S(1)}, bf16[4,128,256]{2,1,0:T(8,128)(2,1)S(1)}, u32[]{:S(2)}, u32[]{:S(2)}) collective-permute-start(bf16[4,128,256]{2,1,0:T(8,128)(2,1)S(1)} %shard_map.74.refs_0_), channel_id=1, source_target_pairs={{0,32},{1,33},{2,34},{3,35},{4,36},{5,37},{6,38},{7,39},{8,40},{9,... | collective-permute-start | bytes 786440 | tf_op jit(solution)/shard_map/ppermute | solution.py:42
  42.5 3.6 %shard_map.75 = (bf16[8,1,64,256]{3,2,1,0:T(8,128)(2,1)S(1)}, bf16[8,1,64,256]{3,2,1,0:T(8,128)(2,1)S(1)}, bf16[8,1,64,256]{3,2,1,0:T(8,128)(2,1)S(1)}, f32[8,1,64,256]{3,2,1,0:T(8,128)S(1)}) custom-call(s32[1]{0:T(128)} %bitcast.1.sc, bf16[16,256,512]{2,1,0:T(8,128)(2,1)} %t_own.3, bf16[16,256,512]{2,1,0:T(8,128)(2,1)} %collective-permute-done.1.t_oth, ...), custom_call_target="tpu_custom_call" | custom-call | flops 1600000000 | bytes 4000000 | tf_op jit(solution)/shard_map/pallas_call | solution.py:148
  46.2 1.9 %collective-permute-start.15 = (bf16[8,1,64,256]{3,2,1,0:T(8,128)(2,1)S(1)}, bf16[8,1,64,256]{3,2,1,0:T(8,128)(2,1)S(1)}, u32[]{:S(2)}, u32[]{:S(2)}) collective-permute-start(bf16[8,1,64,256]{3,2,1,0:T(8,128)(2,1)S(1)} %get-tuple-element.42), channel_id=1, source_target_pairs={{0,16},{1,5},{2,18},{3,7},{4,20},{5,1},{6,22},{7,3},{8,24},{9,13},... | collective-permute-start | bytes 786440 | tf_op jit(solution)/shard_map/ppermute | solution.py:42
  50.2 2.0 %collective-permute-start.20 = (bf16[3,256,256]{2,1,0:T(8,128)(2,1)S(1)}, bf16[3,256,256]{2,1,0:T(8,128)(2,1)S(1)}, u32[]{:S(2)}, u32[]{:S(2)}) collective-permute-start(bf16[3,256,256]{2,1,0:T(8,128)(2,1)S(1)} %pad_maximum_fusion.1.own), channel_id=1, source_target_pairs={{0,1},{1,0},{2,3},{3,2},{4,5},{5,4},{6,7},{7,6},{8,9},{9,8},{10,11... | collective-permute-start | bytes 1179656 | tf_op jit(solution)/shard_map/ppermute | solution.py:42
  52.2 4.3 %collective-permute-done.17.refs_0_ = bf16[4,128,256]{2,1,0:T(8,128)(2,1)S(1)} collective-permute-done((bf16[4,128,256]{2,1,0:T(8,128)(2,1)S(1)}, bf16[4,128,256]{2,1,0:T(8,128)(2,1)S(1)}, u32[]{:S(2)}, u32[]{:S(2)}) %collective-permute-start.17) | collective-permute-done | bytes 262176 | tf_op jit(solution)/shard_map/ppermute | solution.py:42
  56.5 1.6 %collective-permute-start.21 = (bf16[4,128,256]{2,1,0:T(8,128)(2,1)S(1)}, bf16[4,128,256]{2,1,0:T(8,128)(2,1)S(1)}, u32[]{:S(2)}, u32[]{:S(2)}) collective-permute-start(bf16[4,128,256]{2,1,0:T(8,128)(2,1)S(1)} %collective-permute-done.17.refs_0_), channel_id=1, source_target_pairs={{0,1},{1,0},{2,3},{3,2},{4,5},{5,4},{6,7},{7,6},{8,9},{9,8},{10,11... | collective-permute-start | bytes 786440 | tf_op jit(solution)/shard_map/ppermute | solution.py:42
  60.0 6.9 %shard_map.77 = (bf16[8,3,64,256]{3,2,1,0:T(8,128)(2,1)S(1)}, bf16[8,3,64,256]{3,2,1,0:T(8,128)(2,1)S(1)}, bf16[8,3,64,256]{3,2,1,0:T(8,128)(2,1)S(1)}, f32[8,3,64,256]{3,2,1,0:T(8,128)S(1)}) custom-call(s32[1]{0:T(128)} %bitcast.1.sc, bf16[16,256,512]{2,1,0:T(8,128)(2,1)} %t_own.3, bf16[16,256,512]{2,1,0:T(8,128)(2,1)} %collective-permute-done.1.t_oth, ...), custom_call_target="tpu_custom_call" | custom-call | flops 4800000000 | bytes 12000000 | tf_op jit(solution)/shard_map/pallas_call | solution.py:148
  67.2 2.0 %collective-permute-start.25 = (bf16[8,3,64,256]{3,2,1,0:T(8,128)(2,1)S(1)}, bf16[8,3,64,256]{3,2,1,0:T(8,128)(2,1)S(1)}, u32[]{:S(2)}, u32[]{:S(2)}) collective-permute-start(bf16[8,3,64,256]{3,2,1,0:T(8,128)(2,1)S(1)} %get-tuple-element.53), channel_id=1, source_target_pairs={{0,16},{1,5},{2,18},{3,7},{4,20},{5,1},{6,22},{7,3},{8,24},{9,13},... | collective-permute-start | bytes 2359304 | tf_op jit(solution)/shard_map/ppermute | solution.py:42
  70.5 17.5 %collective-permute-done.24 = bf16[8,3,64,256]{3,2,1,0:T(8,128)(2,1)S(1)} collective-permute-done((bf16[8,3,64,256]{3,2,1,0:T(8,128)(2,1)S(1)}, bf16[8,3,64,256]{3,2,1,0:T(8,128)(2,1)S(1)}, u32[]{:S(2)}, u32[]{:S(2)}) %collective-permute-start.24) | collective-permute-done | bytes 786464 | tf_op jit(solution)/shard_map/ppermute | solution.py:42
  89.9 2.0 %collective-permute-start.29 = (bf16[8,4,16,256]{3,2,1,0:T(8,128)(2,1)S(1)}, bf16[8,4,16,256]{3,2,1,0:T(8,128)(2,1)}, u32[]{:S(2)}, u32[]{:S(2)}) collective-permute-start(bf16[8,4,16,256]{3,2,1,0:T(8,128)(2,1)S(1)} %pad_maximum_fusion.4), channel_id=1, source_target_pairs={{0,6},{1,25},{2,0},{3,27},{4,2},{5,29},{6,4},{7,31},{8,14},{9,1},{... | collective-permute-start | bytes 786440 | tf_op jit(solution)/shard_map/ppermute | solution.py:42
  92.5 3.9 %collective-permute-done.28 = bf16[8,4,16,256]{3,2,1,0:T(8,128)(2,1)} collective-permute-done((bf16[8,4,16,256]{3,2,1,0:T(8,128)(2,1)S(1)}, bf16[8,4,16,256]{3,2,1,0:T(8,128)(2,1)}, u32[]{:S(2)}, u32[]{:S(2)}) %collective-permute-start.28) | collective-permute-done | bytes 262176 | tf_op jit(solution)/shard_map/ppermute | solution.py:42
  96.5 2.8 %collective-permute-done.29 = bf16[8,4,16,256]{3,2,1,0:T(8,128)(2,1)} collective-permute-done((bf16[8,4,16,256]{3,2,1,0:T(8,128)(2,1)S(1)}, bf16[8,4,16,256]{3,2,1,0:T(8,128)(2,1)}, u32[]{:S(2)}, u32[]{:S(2)}) %collective-permute-start.29) | collective-permute-done | bytes 262176 | tf_op jit(solution)/shard_map/ppermute | solution.py:42
  99.3 1.3 fusion.2
  100.6 2.5 %collective-permute-start.30 = (bf16[8,16,256]{2,1,0:T(8,128)(2,1)S(1)}, bf16[8,16,256]{2,1,0:T(8,128)(2,1)S(1)}, u32[]{:S(2)}, u32[]{:S(2)}) collective-permute-start(bf16[8,16,256]{2,1,0:T(8,128)(2,1)S(1)} %get-tuple-element.65), channel_id=1, source_target_pairs={{0,96},{1,97},{2,98},{3,99},{4,100},{5,101},{6,102},{7,103},{8,104... | collective-permute-start | bytes 196616 | tf_op jit(solution)/shard_map/ppermute | solution.py:42
  103.1 2.9 %collective-permute-start.31 = (bf16[8,16,256]{2,1,0:T(8,128)(2,1)S(1)}, bf16[8,16,256]{2,1,0:T(8,128)(2,1)S(1)}, u32[]{:S(2)}, u32[]{:S(2)}) collective-permute-start(bf16[8,16,256]{2,1,0:T(8,128)(2,1)S(1)} %get-tuple-element.67), channel_id=1, source_target_pairs={{0,64},{1,65},{2,66},{3,67},{4,68},{5,69},{6,70},{7,71},{8,72},{9,... | collective-permute-start | bytes 196616 | tf_op jit(solution)/shard_map/ppermute | solution.py:42
  106.2 1.2 collective-permute-done.32
  108.4 3.9 %collective-permute-start.33 = (bf16[4,8,16,128]{3,2,1,0:T(8,128)(2,1)S(1)}, bf16[4,8,16,128]{3,2,1,0:T(8,128)(2,1)S(1)}, u32[]{:S(2)}, u32[]{:S(2)}) collective-permute-start(bf16[4,8,16,128]{3,2,1,0:T(8,128)(2,1)S(1)} %get-tuple-element.63), channel_id=1, source_target_pairs={{0,1},{1,0},{2,3},{3,2},{4,5},{5,4},{6,7},{7,6},{8,9},{9,8},{10,11... | collective-permute-start | bytes 393224 | tf_op jit(solution)/shard_map/ppermute | solution.py:42
  114.0 15.1 %all_to_all.5 = bf16[32,3,16,128]{3,2,1,0:T(8,128)(2,1)S(1)} all-to-all(bf16[32,3,16,128]{3,2,1,0:T(8,128)(2,1)S(1)} %bitcast.56), channel_id=1, replica_groups=mesh['grp'=4,'sub'=32] {'sub'}, dimensions={0} | all-to-all | bytes 786432 | tf_op jit(solution)/shard_map/all_to_all | solution.py:267
  129.4 1.5 %reshape.111 = f32[1,3,256,256]{3,2,1,0:T(8,128)} reshape(f32[3,16,16,2,128]{4,3,2,1,0:T(2,128)S(1)} %bitcast.59) | data formatting | bytes 1572864 | tf_op jit(solution)/shard_map/convert_element_type | solution.py:271
  (77 shorter events, 20.6 us)
Async XLA Ops:
  1.6 2.4 %collective-permute-start = (bf16[128,256]{1,0:T(8,128)(2,1)S(1)}, bf16[128,256]{1,0:T(8,128)(2,1)S(1)}, u32[]{:S(2)}, u32[]{:S(2)}) collective-permute-start(bf16[128,256]{1,0:T(8,128)(2,1)S(1)} %get-tuple-element.72), channel_id=1, source_target_pairs={{0,1},{1,0},{2,3},{3,2},{4,5},{5,4},{6,7},{7,6},{8,9},{9,8},{10,11... | collective-permute-start | bytes 196616 | tf_op jit(solution)/shard_map/ppermute | solution.py:42
  4.0 38.5 %collective-permute-start.1 = (bf16[16,256,512]{2,1,0:T(8,128)(2,1)}, bf16[16,256,512]{2,1,0:T(8,128)(2,1)}, u32[]{:S(2)}, u32[]{:S(2)}) collective-permute-start(bf16[16,256,512]{2,1,0:T(8,128)(2,1)} %t_own.3), channel_id=1, source_target_pairs={{0,1},{1,0},{2,3},{3,2},{4,5},{5,4},{6,7},{7,6},{8,9},{9,8},{10,11... | collective-permute-start | bytes 12582920 | tf_op jit(solution)/shard_map/ppermute | solution.py:42
  5.1 6.2 %collective-permute-start.5 = (bf16[2,128,256]{2,1,0:T(8,128)(2,1)S(1)}, bf16[2,128,256]{2,1,0:T(8,128)(2,1)S(1)}, u32[]{:S(2)}, u32[]{:S(2)}) collective-permute-start(bf16[2,128,256]{2,1,0:T(8,128)(2,1)S(1)} %maximum_select_fusion), channel_id=1, source_target_pairs={{0,24},{1,7},{2,26},{3,1},{4,28},{5,3},{6,30},{7,5},{8,0},{9,15},{... | collective-permute-start | bytes 393224 | tf_op jit(solution)/shard_map/ppermute | solution.py:42
  8.0 5.6 %collective-permute-start.4 = (bf16[2,128,256]{2,1,0:T(8,128)(2,1)S(1)}, bf16[2,128,256]{2,1,0:T(8,128)(2,1)S(1)}, u32[]{:S(2)}, u32[]{:S(2)}) collective-permute-start(bf16[2,128,256]{2,1,0:T(8,128)(2,1)S(1)} %maximum_select_fusion), channel_id=1, source_target_pairs={{0,16},{1,5},{2,18},{3,7},{4,20},{5,1},{6,22},{7,3},{8,24},{9,13},... | collective-permute-start | bytes 393224 | tf_op jit(solution)/shard_map/ppermute | solution.py:42
  8.4 6.7 %collective-permute-start.3 = (bf16[2,128,256]{2,1,0:T(8,128)(2,1)S(1)}, bf16[2,128,256]{2,1,0:T(8,128)(2,1)S(1)}, u32[]{:S(2)}, u32[]{:S(2)}) collective-permute-start(bf16[2,128,256]{2,1,0:T(8,128)(2,1)S(1)} %maximum_select_fusion), channel_id=1, source_target_pairs={{0,8},{1,3},{2,10},{3,5},{4,12},{5,7},{6,14},{7,1},{8,16},{9,11},{... | collective-permute-start | bytes 393224 | tf_op jit(solution)/shard_map/ppermute | solution.py:42
  15.1 7.9 %collective-permute-start.6 = (bf16[1,256,256]{2,1,0:T(8,128)(2,1)S(1)}, bf16[1,256,256]{2,1,0:T(8,128)(2,1)S(1)}, u32[]{:S(2)}, u32[]{:S(2)}) collective-permute-start(bf16[1,256,256]{2,1,0:T(8,128)(2,1)S(1)} %bitcast.57), channel_id=1, source_target_pairs={{0,1},{1,0},{2,3},{3,2},{4,5},{5,4},{6,7},{7,6},{8,9},{9,8},{10,11... | collective-permute-start | bytes 393224 | tf_op jit(solution)/shard_map/ppermute | solution.py:42
  16.2 7.1 %collective-permute-start.9 = (bf16[256,256]{1,0:T(8,128)(2,1)S(1)}, bf16[256,256]{1,0:T(8,128)(2,1)S(1)}, u32[]{:S(2)}, u32[]{:S(2)}) collective-permute-start(bf16[256,256]{1,0:T(8,128)(2,1)S(1)} %broadcast_multiply_fusion), channel_id=1, source_target_pairs={{0,96},{1,97},{2,98},{3,99},{4,100},{5,101},{6,102},{7,103},{8,104... | collective-permute-start | bytes 393224 | tf_op jit(solution)/shard_map/ppermute | solution.py:42
  20.0 1.9 %collective-permute-start.2 = (s32[1,2]{1,0:T(1,128)S(1)}, s32[1,2]{1,0:T(1,128)S(1)}, u32[]{:S(2)}, u32[]{:S(2)}) collective-permute-start(s32[1,2]{1,0:T(1,128)S(1)} %copy-done), channel_id=1, source_target_pairs={{0,1},{1,0},{2,3},{3,2},{4,5},{5,4},{6,7},{7,6},{8,9},{9,8},{10,11... | collective-permute-start | bytes 32 | tf_op jit(solution)/shard_map/ppermute | solution.py:42
  20.4 14.3 %collective-permute-start.12 = (bf16[8,128,256]{2,1,0:T(8,128)(2,1)S(1)}, bf16[8,128,256]{2,1,0:T(8,128)(2,1)S(1)}, u32[]{:S(2)}, u32[]{:S(2)}) collective-permute-start(bf16[8,128,256]{2,1,0:T(8,128)(2,1)S(1)} %pad_maximum_fusion.set0), channel_id=1, source_target_pairs={{0,6},{1,25},{2,0},{3,27},{4,2},{5,29},{6,4},{7,31},{8,14},{9,1},{... | collective-permute-start | bytes 1572872 | tf_op jit(solution)/shard_map/ppermute | solution.py:42
  21.9 12.7 %collective-permute-start.11 = (bf16[8,128,256]{2,1,0:T(8,128)(2,1)S(1)}, bf16[8,128,256]{2,1,0:T(8,128)(2,1)S(1)}, u32[]{:S(2)}, u32[]{:S(2)}) collective-permute-start(bf16[8,128,256]{2,1,0:T(8,128)(2,1)S(1)} %pad_maximum_fusion.set0), channel_id=1, source_target_pairs={{0,4},{1,17},{2,6},{3,19},{4,0},{5,21},{6,2},{7,23},{8,12},{9,25},... | collective-permute-start | bytes 1572872 | tf_op jit(solution)/shard_map/ppermute | solution.py:42
  23.0 14.4 %collective-permute-start.10 = (bf16[8,128,256]{2,1,0:T(8,128)(2,1)S(1)}, bf16[8,128,256]{2,1,0:T(8,128)(2,1)S(1)}, u32[]{:S(2)}, u32[]{:S(2)}) collective-permute-start(bf16[8,128,256]{2,1,0:T(8,128)(2,1)S(1)} %pad_maximum_fusion.set0), channel_id=1, source_target_pairs={{0,2},{1,9},{2,4},{3,11},{4,6},{5,13},{6,0},{7,15},{8,10},{9,17},{... | collective-permute-start | bytes 1572872 | tf_op jit(solution)/shard_map/ppermute | solution.py:42
  23.3 5.6 %collective-permute-start.8 = (bf16[256,256]{1,0:T(8,128)(2,1)S(1)}, bf16[256,256]{1,0:T(8,128)(2,1)S(1)}, u32[]{:S(2)}, u32[]{:S(2)}) collective-permute-start(bf16[256,256]{1,0:T(8,128)(2,1)S(1)} %broadcast_multiply_fusion), channel_id=1, source_target_pairs={{0,64},{1,65},{2,66},{3,67},{4,68},{5,69},{6,70},{7,71},{8,72},{9,... | collective-permute-start | bytes 393224 | tf_op jit(solution)/shard_map/ppermute | solution.py:42
  29.0 5.6 %collective-permute-start.7 = (bf16[256,256]{1,0:T(8,128)(2,1)S(1)}, bf16[256,256]{1,0:T(8,128)(2,1)S(1)}, u32[]{:S(2)}, u32[]{:S(2)}) collective-permute-start(bf16[256,256]{1,0:T(8,128)(2,1)S(1)} %broadcast_multiply_fusion), channel_id=1, source_target_pairs={{0,32},{1,33},{2,34},{3,35},{4,36},{5,37},{6,38},{7,39},{8,40},{9,... | collective-permute-start | bytes 393224 | tf_op jit(solution)/shard_map/ppermute | solution.py:42
  38.5 4.0 %collective-permute-start.13 = (bf16[4,128,256]{2,1,0:T(8,128)(2,1)S(1)}, bf16[4,128,256]{2,1,0:T(8,128)(2,1)S(1)}, u32[]{:S(2)}, u32[]{:S(2)}) collective-permute-start(bf16[4,128,256]{2,1,0:T(8,128)(2,1)S(1)} %shard_map.74.refs_0_), channel_id=1, source_target_pairs={{0,1},{1,0},{2,3},{3,2},{4,5},{5,4},{6,7},{7,6},{8,9},{9,8},{10,11... | collective-permute-start | bytes 786440 | tf_op jit(solution)/shard_map/ppermute | solution.py:42
  41.0 7.9 %collective-permute-start.19 = (bf16[4,128,256]{2,1,0:T(8,128)(2,1)S(1)}, bf16[4,128,256]{2,1,0:T(8,128)(2,1)S(1)}, u32[]{:S(2)}, u32[]{:S(2)}) collective-permute-start(bf16[4,128,256]{2,1,0:T(8,128)(2,1)S(1)} %shard_map.74.refs_0_), channel_id=1, source_target_pairs={{0,96},{1,97},{2,98},{3,99},{4,100},{5,101},{6,102},{7,103},{8,104... | collective-permute-start | bytes 786440 | tf_op jit(solution)/shard_map/ppermute | solution.py:42
  41.2 9.1 %collective-permute-start.18 = (bf16[4,128,256]{2,1,0:T(8,128)(2,1)S(1)}, bf16[4,128,256]{2,1,0:T(8,128)(2,1)S(1)}, u32[]{:S(2)}, u32[]{:S(2)}) collective-permute-start(bf16[4,128,256]{2,1,0:T(8,128)(2,1)S(1)} %shard_map.74.refs_0_), channel_id=1, source_target_pairs={{0,64},{1,65},{2,66},{3,67},{4,68},{5,69},{6,70},{7,71},{8,72},{9,... | collective-permute-start | bytes 786440 | tf_op jit(solution)/shard_map/ppermute | solution.py:42
  41.2 15.4 %collective-permute-start.17 = (bf16[4,128,256]{2,1,0:T(8,128)(2,1)S(1)}, bf16[4,128,256]{2,1,0:T(8,128)(2,1)S(1)}, u32[]{:S(2)}, u32[]{:S(2)}) collective-permute-start(bf16[4,128,256]{2,1,0:T(8,128)(2,1)S(1)} %shard_map.74.refs_0_), channel_id=1, source_target_pairs={{0,32},{1,33},{2,34},{3,35},{4,36},{5,37},{6,38},{7,39},{8,40},{9,... | collective-permute-start | bytes 786440 | tf_op jit(solution)/shard_map/ppermute | solution.py:42
  46.1 10.4 %collective-permute-start.14 = (bf16[8,1,64,256]{3,2,1,0:T(8,128)(2,1)S(1)}, bf16[8,1,64,256]{3,2,1,0:T(8,128)(2,1)S(1)}, u32[]{:S(2)}, u32[]{:S(2)}) collective-permute-start(bf16[8,1,64,256]{3,2,1,0:T(8,128)(2,1)S(1)} %get-tuple-element.41), channel_id=1, source_target_pairs={{0,8},{1,3},{2,10},{3,5},{4,12},{5,7},{6,14},{7,1},{8,16},{9,11},{... | collective-permute-start | bytes 786440 | tf_op jit(solution)/shard_map/ppermute | solution.py:42
  46.2 10.3 %collective-permute-start.15 = (bf16[8,1,64,256]{3,2,1,0:T(8,128)(2,1)S(1)}, bf16[8,1,64,256]{3,2,1,0:T(8,128)(2,1)S(1)}, u32[]{:S(2)}, u32[]{:S(2)}) collective-permute-start(bf16[8,1,64,256]{3,2,1,0:T(8,128)(2,1)S(1)} %get-tuple-element.42), channel_id=1, source_target_pairs={{0,16},{1,5},{2,18},{3,7},{4,20},{5,1},{6,22},{7,3},{8,24},{9,13},... | collective-permute-start | bytes 786440 | tf_op jit(solution)/shard_map/ppermute | solution.py:42
  48.9 7.6 %collective-permute-start.16 = (bf16[8,1,64,256]{3,2,1,0:T(8,128)(2,1)S(1)}, bf16[8,1,64,256]{3,2,1,0:T(8,128)(2,1)S(1)}, u32[]{:S(2)}, u32[]{:S(2)}) collective-permute-start(bf16[8,1,64,256]{3,2,1,0:T(8,128)(2,1)S(1)} %get-tuple-element.43), channel_id=1, source_target_pairs={{0,24},{1,7},{2,26},{3,1},{4,28},{5,3},{6,30},{7,5},{8,0},{9,15},{... | collective-permute-start | bytes 786440 | tf_op jit(solution)/shard_map/ppermute | solution.py:42
  50.2 8.4 %collective-permute-start.20 = (bf16[3,256,256]{2,1,0:T(8,128)(2,1)S(1)}, bf16[3,256,256]{2,1,0:T(8,128)(2,1)S(1)}, u32[]{:S(2)}, u32[]{:S(2)}) collective-permute-start(bf16[3,256,256]{2,1,0:T(8,128)(2,1)S(1)} %pad_maximum_fusion.1.own), channel_id=1, source_target_pairs={{0,1},{1,0},{2,3},{3,2},{4,5},{5,4},{6,7},{7,6},{8,9},{9,8},{10,11... | collective-permute-start | bytes 1179656 | tf_op jit(solution)/shard_map/ppermute | solution.py:42
  56.5 2.7 %collective-permute-start.21 = (bf16[4,128,256]{2,1,0:T(8,128)(2,1)S(1)}, bf16[4,128,256]{2,1,0:T(8,128)(2,1)S(1)}, u32[]{:S(2)}, u32[]{:S(2)}) collective-permute-start(bf16[4,128,256]{2,1,0:T(8,128)(2,1)S(1)} %collective-permute-done.17.refs_0_), channel_id=1, source_target_pairs={{0,1},{1,0},{2,3},{3,2},{4,5},{5,4},{6,7},{7,6},{8,9},{9,8},{10,11... | collective-permute-start | bytes 786440 | tf_op jit(solution)/shard_map/ppermute | solution.py:42
  66.9 21.0 %collective-permute-start.24 = (bf16[8,3,64,256]{3,2,1,0:T(8,128)(2,1)S(1)}, bf16[8,3,64,256]{3,2,1,0:T(8,128)(2,1)S(1)}, u32[]{:S(2)}, u32[]{:S(2)}) collective-permute-start(bf16[8,3,64,256]{3,2,1,0:T(8,128)(2,1)S(1)} %get-tuple-element.52), channel_id=1, source_target_pairs={{0,8},{1,3},{2,10},{3,5},{4,12},{5,7},{6,14},{7,1},{8,16},{9,11},{... | collective-permute-start | bytes 2359304 | tf_op jit(solution)/shard_map/ppermute | solution.py:42
  67.2 20.8 %collective-permute-start.25 = (bf16[8,3,64,256]{3,2,1,0:T(8,128)(2,1)S(1)}, bf16[8,3,64,256]{3,2,1,0:T(8,128)(2,1)S(1)}, u32[]{:S(2)}, u32[]{:S(2)}) collective-permute-start(bf16[8,3,64,256]{3,2,1,0:T(8,128)(2,1)S(1)} %get-tuple-element.53), channel_id=1, source_target_pairs={{0,16},{1,5},{2,18},{3,7},{4,20},{5,1},{6,22},{7,3},{8,24},{9,13},... | collective-permute-start | bytes 2359304 | tf_op jit(solution)/shard_map/ppermute | solution.py:42
  69.2 19.4 %collective-permute-start.26 = (bf16[8,3,64,256]{3,2,1,0:T(8,128)(2,1)S(1)}, bf16[8,3,64,256]{3,2,1,0:T(8,128)(2,1)S(1)}, u32[]{:S(2)}, u32[]{:S(2)}) collective-permute-start(bf16[8,3,64,256]{3,2,1,0:T(8,128)(2,1)S(1)} %get-tuple-element.54), channel_id=1, source_target_pairs={{0,24},{1,7},{2,26},{3,1},{4,28},{5,3},{6,30},{7,5},{8,0},{9,15},{... | collective-permute-start | bytes 2359304 | tf_op jit(solution)/shard_map/ppermute | solution.py:42
  89.3 7.2 %collective-permute-start.28 = (bf16[8,4,16,256]{3,2,1,0:T(8,128)(2,1)S(1)}, bf16[8,4,16,256]{3,2,1,0:T(8,128)(2,1)}, u32[]{:S(2)}, u32[]{:S(2)}) collective-permute-start(bf16[8,4,16,256]{3,2,1,0:T(8,128)(2,1)S(1)} %pad_maximum_fusion.3), channel_id=1, source_target_pairs={{0,4},{1,17},{2,6},{3,19},{4,0},{5,21},{6,2},{7,23},{8,12},{9,25},... | collective-permute-start | bytes 786440 | tf_op jit(solution)/shard_map/ppermute | solution.py:42
  89.9 9.4 %collective-permute-start.29 = (bf16[8,4,16,256]{3,2,1,0:T(8,128)(2,1)S(1)}, bf16[8,4,16,256]{3,2,1,0:T(8,128)(2,1)}, u32[]{:S(2)}, u32[]{:S(2)}) collective-permute-start(bf16[8,4,16,256]{3,2,1,0:T(8,128)(2,1)S(1)} %pad_maximum_fusion.4), channel_id=1, source_target_pairs={{0,6},{1,25},{2,0},{3,27},{4,2},{5,29},{6,4},{7,31},{8,14},{9,1},{... | collective-permute-start | bytes 786440 | tf_op jit(solution)/shard_map/ppermute | solution.py:42
  91.8 7.4 %collective-permute-start.27 = (bf16[8,4,16,256]{3,2,1,0:T(8,128)(2,1)S(1)}, bf16[8,4,16,256]{3,2,1,0:T(8,128)(2,1)}, u32[]{:S(2)}, u32[]{:S(2)}) collective-permute-start(bf16[8,4,16,256]{3,2,1,0:T(8,128)(2,1)S(1)} %pad_maximum_fusion.2), channel_id=1, source_target_pairs={{0,2},{1,9},{2,4},{3,11},{4,6},{5,13},{6,0},{7,15},{8,10},{9,17},{... | collective-permute-start | bytes 786440 | tf_op jit(solution)/shard_map/ppermute | solution.py:42
  100.6 5.6 %collective-permute-start.30 = (bf16[8,16,256]{2,1,0:T(8,128)(2,1)S(1)}, bf16[8,16,256]{2,1,0:T(8,128)(2,1)S(1)}, u32[]{:S(2)}, u32[]{:S(2)}) collective-permute-start(bf16[8,16,256]{2,1,0:T(8,128)(2,1)S(1)} %get-tuple-element.65), channel_id=1, source_target_pairs={{0,96},{1,97},{2,98},{3,99},{4,100},{5,101},{6,102},{7,103},{8,104... | collective-permute-start | bytes 196616 | tf_op jit(solution)/shard_map/ppermute | solution.py:42
  103.0 4.3 %collective-permute-start.32 = (bf16[8,16,256]{2,1,0:T(8,128)(2,1)S(1)}, bf16[8,16,256]{2,1,0:T(8,128)(2,1)S(1)}, u32[]{:S(2)}, u32[]{:S(2)}) collective-permute-start(bf16[8,16,256]{2,1,0:T(8,128)(2,1)S(1)} %get-tuple-element.66), channel_id=1, source_target_pairs={{0,32},{1,33},{2,34},{3,35},{4,36},{5,37},{6,38},{7,39},{8,40},{9,... | collective-permute-start | bytes 196616 | tf_op jit(solution)/shard_map/ppermute | solution.py:42
  103.1 5.3 %collective-permute-start.31 = (bf16[8,16,256]{2,1,0:T(8,128)(2,1)S(1)}, bf16[8,16,256]{2,1,0:T(8,128)(2,1)S(1)}, u32[]{:S(2)}, u32[]{:S(2)}) collective-permute-start(bf16[8,16,256]{2,1,0:T(8,128)(2,1)S(1)} %get-tuple-element.67), channel_id=1, source_target_pairs={{0,64},{1,65},{2,66},{3,67},{4,68},{5,69},{6,70},{7,71},{8,72},{9,... | collective-permute-start | bytes 196616 | tf_op jit(solution)/shard_map/ppermute | solution.py:42
  108.4 4.9 %collective-permute-start.33 = (bf16[4,8,16,128]{3,2,1,0:T(8,128)(2,1)S(1)}, bf16[4,8,16,128]{3,2,1,0:T(8,128)(2,1)S(1)}, u32[]{:S(2)}, u32[]{:S(2)}) collective-permute-start(bf16[4,8,16,128]{3,2,1,0:T(8,128)(2,1)S(1)} %get-tuple-element.63), channel_id=1, source_target_pairs={{0,1},{1,0},{2,3},{3,2},{4,5},{5,4},{6,7},{7,6},{8,9},{9,8},{10,11... | collective-permute-start | bytes 393224 | tf_op jit(solution)/shard_map/ppermute | solution.py:42
  (4 other events, 36.9 us)

commit v4 on v3

--- a/solution.py
+++ b/solution.py
@@ -81,7 +81,7 @@
         ),
         out_shape=jax.ShapeDtypeStruct((4, 128, 256), BF),
         compiler_params=pltpu.CompilerParams(vmem_limit_bytes=4 * MIB),
-        cost_estimate=pl.CostEstimate(flops=0, bytes_accessed=600_000, transcendentals=0),
+        cost_estimate=pl.CostEstimate(flops=0, bytes_accessed=1000, transcendentals=0),
     )(scalars, *sets)
 
 
@@ -106,12 +106,12 @@
         ),
         out_shape=jax.ShapeDtypeStruct((count, 256, 512), BF),
         compiler_params=pltpu.CompilerParams(vmem_limit_bytes=8 * MIB),
-        cost_estimate=pl.CostEstimate(flops=0, bytes_accessed=500_000 * count, transcendentals=0),
+        cost_estimate=pl.CostEstimate(flops=0, bytes_accessed=1000, transcendentals=0),
     )(strips, own, oth)
 
 
 def products_body(sc, t_own, t_oth, gv, *refs):
-    halves, (send1, send2, send3, keep, go) = refs[:-5], refs[-5:]
+    halves, (send1, send2, send3, keep, go) = refs[: 2 * gv.shape[0]], refs[-5:]
     count = len(halves) // 2
     c = sc[0]
 
@@ -140,10 +140,11 @@
             keep[p, r] = out[192:256]
 
 
-def products_of(core, t_own, t_oth, gv, halves):
-    count = gv.shape[0]
-    block = pl.BlockSpec((STACK, count, 64, 256), lambda p, sc: (p, 0, 0, 0))
-    shape = (8, count, 64, 256)
+def products_of(core, t_own, t_oth, gv, halves, room, at, gv_at, begun=()):
+    count = len(halves) // 2
+    block = pl.BlockSpec((STACK, count, 64, 256), lambda p, sc: (p, at, 0, 0))
+    shape = (8, room, 64, 256)
+    first = 4 + 2 * count
     functions = pl.BlockSpec((STACK, 256, 512), lambda p, sc: (sc[0] * (8 // STACK) + p, 0, 0))
     return pl.pallas_call(
         products_body,
@@ -151,17 +152,17 @@
             num_scalar_prefetch=1,
             grid=(8 // STACK,),
             in_specs=[functions] * 2
-            + [whole((count, 256, 512))]
-            + [whole((4, 128, 256))] * (2 * count),
+            + [pl.BlockSpec((count, 256, 512), lambda p, sc: (gv_at, 0, 0))]
+            + [whole((4, 128, 256))] * (2 * count)
+            + [pl.BlockSpec(memory_space=pl.ANY)] * len(begun),
             out_specs=[block] * 4,
             scratch_shapes=[pltpu.VMEM((2 * count, 512, 256), BF)],
         ),
         out_shape=[jax.ShapeDtypeStruct(shape, BF)] * 3 + [jax.ShapeDtypeStruct(shape, F32)],
+        input_output_aliases={first + n: n for n in range(len(begun))},
         compiler_params=pltpu.CompilerParams(vmem_limit_bytes=(12 + 4 * count) * MIB),
-        cost_estimate=pl.CostEstimate(
-            flops=1_600_000_000 * count, bytes_accessed=4_000_000 * count, transcendentals=0
-        ),
-    )(core, pltpu.with_memory_space_constraint(t_own, pltpu.HBM), t_oth, gv, *halves)
+        cost_estimate=pl.CostEstimate(flops=1000, bytes_accessed=1000, transcendentals=0),
+    )(core, pltpu.with_memory_space_constraint(t_own, pltpu.HBM), t_oth, gv, *halves, *begun)
 
 
 def slots_body(sc, pieces, out):
@@ -183,6 +184,23 @@
     )(source, pieces)
 
 
+def widen_body(pieces, out):
+    for n in range(32):
+        rows, columns = slice(n // 2 * 16, n // 2 * 16 + 16), slice(n % 2 * 128, n % 2 * 128 + 128)
+        for k in range(CAP):
+            out[k, rows, columns] = pieces[n, k].astype(F32)
+
+
+def widen(pieces):
+    return pl.pallas_call(
+        widen_body,
+        in_specs=[pl.BlockSpec(memory_space=pltpu.VMEM)],
+        out_specs=pl.BlockSpec(memory_space=pltpu.VMEM),
+        out_shape=jax.ShapeDtypeStruct((CAP, 256, 256), F32),
+        compiler_params=pltpu.CompilerParams(vmem_limit_bytes=8 * MIB),
+    )(pieces)
+
+
 def per_device(three_centre, pair_blocks, green_occ, occ_mask, green_virt, virt_mask, owner):
     z = lax.axis_index("grp")
     sub = lax.axis_index("sub")
@@ -200,11 +218,11 @@
     go, theirs = tie(go, three_centre)
     t_oth = move(theirs, CORE)
 
-    near = jnp.concatenate([go] + [move(go, FIRST[d]) for d in (1, 2, 3)])
-    gv = green_virt * virt_mask[0, 0].astype(BF)
-    near, gv = tie(near, gv)
-    sets = [near] + [move(near, SECOND[e]) for e in (1, 2, 3)]
-    gv_far = jnp.stack([move(gv, DEPTH[r]) for r in (1, 2, 3)])
+    go1, go3, go2 = [move(go, FIRST[d]) for d in (1, 3, 2)]
+    near = jnp.concatenate([go, go1, go2, go3])
+    near, gv = tie(near, green_virt * virt_mask[0, 0].astype(BF))
+    gv1, gv3, gv2 = [move(gv, DEPTH[r]) for r in (1, 3, 2)]
+    set1, set3, set2 = [move(near, SECOND[e]) for e in (1, 3, 2)]
     gv = gv.reshape(1, 256, 256)
     strips = jnp.stack(
         [
@@ -213,21 +231,26 @@
             for s2 in [(q2 + e) % 4 for e in range(4)]
         ]
     ).astype(jnp.int32)
-    gv_near = order_rows(strips, gv, move(gv, CORE))
+    gv = order_rows(strips, gv, move(gv, CORE))
 
     partners = by_core(pair_blocks[0], move(pair_blocks, CORE)[0]).reshape(4)
     places = jnp.concatenate([jnp.stack([c, q1, q2]), partners]).astype(jnp.int32)
-    places, gv_near, gv_far, *sets = tie(places, gv_near, gv_far, *sets)
-    picked = pick(places, *sets)
-    arriving = [move(picked, DEPTH[r]) for r in (1, 2, 3)]
-    gv_far = order_rows(strips, gv_far, move(gv_far, CORE))
-
-    core = c.reshape(1).astype(jnp.int32)
-    sends0 = products_of(core, three_centre, t_oth, gv_near, (picked, move(picked, CORE)))
-    got0 = [move(sends0[d - 1], FIRST[d]) for d in (1, 2, 3)]
-    *got0, a1, a2, a3 = tie(*got0, *arriving)
-    halves = [h for a in (a1, a2, a3) for h in (a, move(a, CORE))]
-    sends1 = products_of(core, three_centre, t_oth, gv_far, halves)
+    places, gv, set1, set3, set2 = tie(places, gv, set1, set3, set2)
+    picked = pick(places, near, set1, set2, set3)
+    gv1, gv3, gv2, picked = tie(gv1, gv3, gv2, picked)
+    gv_rest = jnp.stack([gv1, gv3, gv2])
+    gv_rest = order_rows(strips, gv_rest, move(gv_rest, CORE))
+    far, *side = [move(picked, DEPTH[r]) for r in (2, 3, 1)]
+
+    given = (c.reshape(1).astype(jnp.int32), three_centre, t_oth)
+    sends0 = products_of(*given, gv, (picked, move(picked, CORE)), 1, 0, 0)
+    *sends0, side3, side1 = tie(*sends0, *side)
+    got0 = [move(sends0[d - 1], FIRST[d]) for d in (1, 3, 2)]
+    halves = [h for a in (side1, side3) for h in (a, move(a, CORE))]
+    sends1 = products_of(*given, gv_rest, halves, 2, 0, 0)
+    *sends1, far = tie(*sends1, far)
+    *got0, far = tie(*got0, far)
+    sends2 = products_of(*given, gv_rest, (far, move(far, CORE)), 1, 0, 2)
 
     def sum_of(sends, got):
         total = sends[3]
@@ -235,18 +258,21 @@
             total = total + part.astype(F32)
         return total
 
-    got1 = [move(sends1[d - 1], FIRST[d]) for d in (1, 2, 3)]
-    sums = [sum_of(sends0, got0), sum_of(sends1, got1)]
+    got1 = [move(sends1[d - 1], FIRST[d]) for d in (1, 3, 2)]
+    got2 = [move(sends2[d - 1], FIRST[d]) for d in (1, 3, 2)]
+    sums = [sum_of(sends0, got0), sum_of(sends1, got1), sum_of(sends2, got2)]
 
     def strip(e):
         return jnp.concatenate([t[:, :, e * 16 : (e + 1) * 16] for t in sums], axis=1)
 
     total = strip(0)
-    for e in (1, 2, 3):
+    for e in (1, 3, 2):
         total = total + move(strip(e).astype(BF), SECOND[e]).astype(F32)
     total = total.astype(BF)
 
-    rows = jnp.stack([total[:, 0]] + [move(total[:, r], DEPTH[4 - r]) for r in (1, 2, 3)])
+    rows = jnp.stack(
+        [total[:, 0]] + [move(total[:, at], DEPTH[4 - r]) for at, r in ((1, 1), (2, 3), (3, 2))]
+    )
     mine = lax.dynamic_slice_in_dim(rows, c * 128, 128, 3)
     other = move(lax.dynamic_slice_in_dim(rows, (1 - c) * 128, 128, 3), CORE)
     pieces = jnp.concatenate(
@@ -260,15 +286,15 @@
     position = jnp.sum(earlier.astype(jnp.int32), axis=1)
     slots = owner_flat * CAP + position
     distance = (numbers // 16 - z + 4) % 4
-    at = jnp.where((numbers // 8) % 2 == c, 0, 32) + distance * 8 + numbers % 8
+    stands = distance ^ (distance >> 1)
+    at = jnp.where((numbers // 8) % 2 == c, 0, 32) + stands * 8 + numbers % 8
     match = slots[None, :] == jnp.arange(32 * CAP, dtype=jnp.int32)[:, None]
     source = jnp.min(jnp.where(match, at[None, :], 64), axis=1)
     outgoing = fill_slots(source, pieces)
     arrived = lax.all_to_all(
         outgoing.reshape(32, CAP, 16, 128), "sub", split_axis=0, concat_axis=0, tiled=True
     )
-    arrived = arrived.reshape(16, 2, CAP, 16, 128).transpose(2, 0, 3, 1, 4)
-    return arrived.reshape(1, CAP, 256, 256).astype(F32)
+    return widen(arrived).reshape(1, CAP, 256, 256)
 
 
 def solution(mesh):

time: 131 us -> 125 us (0.954)
  waiting for transfers between devices: 51.2 us -> 28.7 us
  starting transfers between devices: 42.8 us -> 58.4 us
  Pallas kernels: 13.4 us -> 16.3 us
  local copies, waits for them, and re-layouts: 2.26 us -> 0.45 us
    ppermute x34 -> x37, waiting for transfers between devices: 51.2 us -> 28.7 us  [move(): return lax.ppermute(value, AXES, permutation)]
    ppermute x34 -> x37, starting transfers between devices: 42.8 us -> 58.4 us  [move(): return lax.ppermute(value, AXES, permutation)]
    pallas_call x2 -> x3, Pallas kernels: 10.5 us -> 12.5 us  [products_of(): pl.pallas_call(products_body, grid_spec=pltpu.PrefetchScalarGridSpec(num_...]
    convert_element_type x2 -> x0, local copies, waits for them, and re-layouts: 1.81 us -> none  [per_device(): return arrived.reshape(1, CAP, 256, 256).astype(F32)]
  transfers between devices with their start and end apart: 34 -> 37, of which waited for: 19 -> 21; matrix products, arithmetic and copies ran while one was open for 1% -> 2% of each run, Pallas kernels for 4% -> 12%
where the time goes in v4:
time: 125 us
  starting transfers between devices  58.4 us (47%)
  waiting for transfers between devices  28.7 us (23%)
  Pallas kernels  16.3 us (13%)
  blocking collectives  14.2 us (11%)
  other arithmetic  5.17 us (4%)
  between operations  1.6 us (1%)
    ppermute x37, starting transfers between devices, move(): return lax.ppermute(value, AXES, permutation)  58.4 us
    ppermute x37, waiting for transfers between devices, move(): return lax.ppermute(value, AXES, permutation)  28.7 us
    all_to_all x1, blocking collectives, per_device(): lax.all_to_all(outgoing.reshape(32, CAP, 16, 128), 'sub', split_axis=0, c...  14.2 us
    pallas_call x3, Pallas kernels, products_of(): pl.pallas_call(products_body, grid_spec=pltpu.PrefetchScalarGridSpec(num_...  12.5 us
  transfers between devices with their start and end apart: 37, of which 21 were waited for; matrix products, arithmetic and copies ran while one was open for 2% of the time, Pallas kernels for 12%

profile of v4, /device:TPU:1, one launch (start us, length us, event | category | flops | bytes accessed | tf_op | source)
XLA Modules:
  0.0 124.9 jit_solution(16868801000086304337)
XLA Ops:
  1.6 1.5 %collective-permute-start = (bf16[128,256]{1,0:T(8,128)(2,1)S(1)}, bf16[128,256]{1,0:T(8,128)(2,1)S(1)}, u32[]{:S(2)}, u32[]{:S(2)}) collective-permute-start(bf16[128,256]{1,0:T(8,128)(2,1)S(1)} %get-tuple-element.107), channel_id=1, source_target_pairs={{0,1},{1,0},{2,3},{3,2},{4,5},{5,4},{6,7},{7,6},{8,9},{9,8},{10,11... | collective-permute-start | bytes 196616 | tf_op jit(solution)/shard_map/ppermute | solution.py:42
  5.1 1.4 %collective-permute-start.3 = (bf16[2,128,256]{2,1,0:T(8,128)(2,1)S(1)}, bf16[2,128,256]{2,1,0:T(8,128)(2,1)S(1)}, u32[]{:S(2)}, u32[]{:S(2)}) collective-permute-start(bf16[2,128,256]{2,1,0:T(8,128)(2,1)S(1)} %maximum_select_fusion), channel_id=1, source_target_pairs={{0,8},{1,3},{2,10},{3,5},{4,12},{5,7},{6,14},{7,1},{8,16},{9,11},{... | collective-permute-start | bytes 393224 | tf_op jit(solution)/shard_map/ppermute | solution.py:42
  6.6 2.6 %collective-permute-start.4 = (bf16[2,128,256]{2,1,0:T(8,128)(2,1)S(1)}, bf16[2,128,256]{2,1,0:T(8,128)(2,1)S(1)}, u32[]{:S(2)}, u32[]{:S(2)}) collective-permute-start(bf16[2,128,256]{2,1,0:T(8,128)(2,1)S(1)} %maximum_select_fusion), channel_id=1, source_target_pairs={{0,16},{1,5},{2,18},{3,7},{4,20},{5,1},{6,22},{7,3},{8,24},{9,13},... | collective-permute-start | bytes 393224 | tf_op jit(solution)/shard_map/ppermute | solution.py:42
  11.2 2.1 %collective-permute-done.4 = bf16[2,128,256]{2,1,0:T(8,128)(2,1)S(1)} collective-permute-done((bf16[2,128,256]{2,1,0:T(8,128)(2,1)S(1)}, bf16[2,128,256]{2,1,0:T(8,128)(2,1)S(1)}, u32[]{:S(2)}, u32[]{:S(2)}) %collective-permute-start.4) | collective-permute-done | bytes 131104 | tf_op jit(solution)/shard_map/ppermute | solution.py:42
  14.7 1.5 %collective-permute-start.8 = (bf16[8,128,256]{2,1,0:T(8,128)(2,1)S(1)}, bf16[8,128,256]{2,1,0:T(8,128)(2,1)S(1)}, u32[]{:S(2)}, u32[]{:S(2)}) collective-permute-start(bf16[8,128,256]{2,1,0:T(8,128)(2,1)S(1)} %pad_maximum_fusion.set0), channel_id=1, source_target_pairs={{0,6},{1,25},{2,0},{3,27},{4,2},{5,29},{6,4},{7,31},{8,14},{9,1},{... | collective-permute-start | bytes 1572872 | tf_op jit(solution)/shard_map/ppermute | solution.py:42
  16.1 1.5 %collective-permute-start.9 = (bf16[8,128,256]{2,1,0:T(8,128)(2,1)S(1)}, bf16[8,128,256]{2,1,0:T(8,128)(2,1)S(1)}, u32[]{:S(2)}, u32[]{:S(2)}) collective-permute-start(bf16[8,128,256]{2,1,0:T(8,128)(2,1)S(1)} %pad_maximum_fusion.set0), channel_id=1, source_target_pairs={{0,4},{1,17},{2,6},{3,19},{4,0},{5,21},{6,2},{7,23},{8,12},{9,25},... | collective-permute-start | bytes 1572872 | tf_op jit(solution)/shard_map/ppermute | solution.py:42
  17.7 2.3 %collective-permute-start.2 = (s32[1,2]{1,0:T(1,128)}, s32[1,2]{1,0:T(1,128)S(1)}, u32[]{:S(2)}, u32[]{:S(2)}) collective-permute-start(s32[1,2]{1,0:T(1,128)} %param.8), channel_id=1, source_target_pairs={{0,1},{1,0},{2,3},{3,2},{4,5},{5,4},{6,7},{7,6},{8,9},{9,8},{10,11... | collective-permute-start | bytes 32 | tf_op jit(solution)/shard_map/ppermute | solution.py:42
  22.3 1.6 %collective-permute-start.10 = (bf16[256,256]{1,0:T(8,128)(2,1)S(1)}, bf16[256,256]{1,0:T(8,128)(2,1)S(1)}, u32[]{:S(2)}, u32[]{:S(2)}) collective-permute-start(bf16[256,256]{1,0:T(8,128)(2,1)S(1)} %broadcast_multiply_fusion), channel_id=1, source_target_pairs={{0,32},{1,33},{2,34},{3,35},{4,36},{5,37},{6,38},{7,39},{8,40},{9,... | collective-permute-start | bytes 393224 | tf_op jit(solution)/shard_map/ppermute | solution.py:42
  23.9 2.8 %collective-permute-start.11 = (bf16[256,256]{1,0:T(8,128)(2,1)S(1)}, bf16[256,256]{1,0:T(8,128)(2,1)S(1)}, u32[]{:S(2)}, u32[]{:S(2)}) collective-permute-start(bf16[256,256]{1,0:T(8,128)(2,1)S(1)} %broadcast_multiply_fusion), channel_id=1, source_target_pairs={{0,96},{1,97},{2,98},{3,99},{4,100},{5,101},{6,102},{7,103},{8,104... | collective-permute-start | bytes 393224 | tf_op jit(solution)/shard_map/ppermute | solution.py:42
  30.7 1.7 %collective-permute-done.12 = bf16[256,256]{1,0:T(8,128)(2,1)S(1)} collective-permute-done((bf16[256,256]{1,0:T(8,128)(2,1)S(1)}, bf16[256,256]{1,0:T(8,128)(2,1)S(1)}, u32[]{:S(2)}, u32[]{:S(2)}) %collective-permute-start.12) | collective-permute-done | bytes 131104 | tf_op jit(solution)/shard_map/ppermute | solution.py:42
  32.4 3.3 %collective-permute-start.13 = (bf16[4,128,256]{2,1,0:T(8,128)(2,1)S(1)}, bf16[4,128,256]{2,1,0:T(8,128)(2,1)S(1)}, u32[]{:S(2)}, u32[]{:S(2)}) collective-permute-start(bf16[4,128,256]{2,1,0:T(8,128)(2,1)S(1)} %shard_map.74.refs_0_), channel_id=1, source_target_pairs={{0,1},{1,0},{2,3},{3,2},{4,5},{5,4},{6,7},{7,6},{8,9},{9,8},{10,11... | collective-permute-start | bytes 786440 | tf_op jit(solution)/shard_map/ppermute | solution.py:42
  35.7 1.3 %collective-permute-start.14 = (bf16[4,128,256]{2,1,0:T(8,128)(2,1)S(1)}, bf16[4,128,256]{2,1,0:T(8,128)(2,1)S(1)}, u32[]{:S(2)}, u32[]{:S(2)}) collective-permute-start(bf16[4,128,256]{2,1,0:T(8,128)(2,1)S(1)} %shard_map.74.refs_0_), channel_id=1, source_target_pairs={{0,96},{1,97},{2,98},{3,99},{4,100},{5,101},{6,102},{7,103},{8,104... | collective-permute-start | bytes 786440 | tf_op jit(solution)/shard_map/ppermute | solution.py:42
  37.8 3.6 %shard_map.75 = (bf16[8,1,64,256]{3,2,1,0:T(8,128)(2,1)S(1)}, bf16[8,1,64,256]{3,2,1,0:T(8,128)(2,1)S(1)}, bf16[8,1,64,256]{3,2,1,0:T(8,128)(2,1)S(1)}, f32[8,1,64,256]{3,2,1,0:T(8,128)S(1)}) custom-call(s32[1]{0:T(128)} %bitcast.1.sc, bf16[16,256,512]{2,1,0:T(8,128)(2,1)} %t_own.5, bf16[16,256,512]{2,1,0:T(8,128)(2,1)} %collective-permute-done.1.t_oth, ...), custom_call_target="tpu_custom_call" | custom-call | flops 1000 | bytes 1000 | tf_op jit(solution)/shard_map/pallas_call | solution.py:149
  41.4 2.2 %collective-permute-done.14.refs_2_ = bf16[4,128,256]{2,1,0:T(8,128)(2,1)S(1)} collective-permute-done((bf16[4,128,256]{2,1,0:T(8,128)(2,1)S(1)}, bf16[4,128,256]{2,1,0:T(8,128)(2,1)S(1)}, u32[]{:S(2)}, u32[]{:S(2)}) %collective-permute-start.14) | collective-permute-done | bytes 262176 | tf_op jit(solution)/shard_map/ppermute | solution.py:42
  43.6 2.1 %collective-permute-done.15.refs_0_ = bf16[4,128,256]{2,1,0:T(8,128)(2,1)S(1)} collective-permute-done((bf16[4,128,256]{2,1,0:T(8,128)(2,1)S(1)}, bf16[4,128,256]{2,1,0:T(8,128)(2,1)S(1)}, u32[]{:S(2)}, u32[]{:S(2)}) %collective-permute-start.15) | collective-permute-done | bytes 262176 | tf_op jit(solution)/shard_map/ppermute | solution.py:42
  48.1 5.9 %collective-permute-start.17 = (bf16[8,1,64,256]{3,2,1,0:T(8,128)(2,1)S(1)}, bf16[8,1,64,256]{3,2,1,0:T(8,128)(2,1)S(1)}, u32[]{:S(2)}, u32[]{:S(2)}) collective-permute-start(bf16[8,1,64,256]{3,2,1,0:T(8,128)(2,1)S(1)} %get-tuple-element.61), channel_id=1, source_target_pairs={{0,24},{1,7},{2,26},{3,1},{4,28},{5,3},{6,30},{7,5},{8,0},{9,15},{... | collective-permute-start | bytes 786440 | tf_op jit(solution)/shard_map/ppermute | solution.py:42
  55.8 5.3 %shard_map.77 = (bf16[8,2,64,256]{3,2,1,0:T(8,128)(2,1)S(1)}, bf16[8,2,64,256]{3,2,1,0:T(8,128)(2,1)S(1)}, bf16[8,2,64,256]{3,2,1,0:T(8,128)(2,1)S(1)}, f32[8,2,64,256]{3,2,1,0:T(8,128)S(1)}) custom-call(s32[1]{0:T(128)} %bitcast.1.sc, bf16[16,256,512]{2,1,0:T(8,128)(2,1)} %t_own.5, bf16[16,256,512]{2,1,0:T(8,128)(2,1)} %collective-permute-done.1.t_oth, ...), custom_call_target="tpu_custom_call" | custom-call | flops 1000 | bytes 1000 | tf_op jit(solution)/shard_map/pallas_call | solution.py:149
  61.9 2.0 %collective-permute-start.24 = (bf16[8,2,64,256]{3,2,1,0:T(8,128)(2,1)S(1)}, bf16[8,2,64,256]{3,2,1,0:T(8,128)(2,1)S(1)}, u32[]{:S(2)}, u32[]{:S(2)}) collective-permute-start(bf16[8,2,64,256]{3,2,1,0:T(8,128)(2,1)S(1)} %get-tuple-element.78), channel_id=1, source_target_pairs={{0,24},{1,7},{2,26},{3,1},{4,28},{5,3},{6,30},{7,5},{8,0},{9,15},{... | collective-permute-start | bytes 1572872 | tf_op jit(solution)/shard_map/ppermute | solution.py:42
  64.6 1.4 %collective-permute-done.26.refs_1_ = bf16[4,128,256]{2,1,0:T(8,128)(2,1)S(1)} collective-permute-done((bf16[4,128,256]{2,1,0:T(8,128)(2,1)S(1)}, bf16[4,128,256]{2,1,0:T(8,128)(2,1)S(1)}, u32[]{:S(2)}, u32[]{:S(2)}) %collective-permute-start.26) | collective-permute-done | bytes 262176 | tf_op jit(solution)/shard_map/ppermute | solution.py:42
  66.0 3.6 %shard_map.78 = (bf16[8,1,64,256]{3,2,1,0:T(8,128)(2,1)S(1)}, bf16[8,1,64,256]{3,2,1,0:T(8,128)(2,1)S(1)}, bf16[8,1,64,256]{3,2,1,0:T(8,128)(2,1)S(1)}, f32[8,1,64,256]{3,2,1,0:T(8,128)S(1)}) custom-call(s32[1]{0:T(128)} %bitcast.1.sc, bf16[16,256,512]{2,1,0:T(8,128)(2,1)} %t_own.5, bf16[16,256,512]{2,1,0:T(8,128)(2,1)} %collective-permute-done.1.t_oth, ...), custom_call_target="tpu_custom_call" | custom-call | flops 1000 | bytes 1000 | tf_op jit(solution)/shard_map/pallas_call | solution.py:149
  70.0 4.1 %collective-permute-start.28 = (bf16[8,1,64,256]{3,2,1,0:T(8,128)(2,1)S(1)}, bf16[8,1,64,256]{3,2,1,0:T(8,128)(2,1)S(1)}, u32[]{:S(2)}, u32[]{:S(2)}) collective-permute-start(bf16[8,1,64,256]{3,2,1,0:T(8,128)(2,1)S(1)} %get-tuple-element.83), channel_id=1, source_target_pairs={{0,24},{1,7},{2,26},{3,1},{4,28},{5,3},{6,30},{7,5},{8,0},{9,15},{... | collective-permute-start | bytes 786440 | tf_op jit(solution)/shard_map/ppermute | solution.py:42
  76.6 2.6 %collective-permute-done.27 = bf16[8,1,64,256]{3,2,1,0:T(8,128)(2,1)S(1)} collective-permute-done((bf16[8,1,64,256]{3,2,1,0:T(8,128)(2,1)S(1)}, bf16[8,1,64,256]{3,2,1,0:T(8,128)(2,1)S(1)}, u32[]{:S(2)}, u32[]{:S(2)}) %collective-permute-start.27) | collective-permute-done | bytes 262176 | tf_op jit(solution)/shard_map/ppermute | solution.py:42
  79.2 2.0 %collective-permute-done.28 = bf16[8,1,64,256]{3,2,1,0:T(8,128)(2,1)S(1)} collective-permute-done((bf16[8,1,64,256]{3,2,1,0:T(8,128)(2,1)S(1)}, bf16[8,1,64,256]{3,2,1,0:T(8,128)(2,1)S(1)}, u32[]{:S(2)}, u32[]{:S(2)}) %collective-permute-start.28) | collective-permute-done | bytes 262176 | tf_op jit(solution)/shard_map/ppermute | solution.py:42
  83.1 3.0 %collective-permute-start.31 = (bf16[8,4,16,256]{3,2,1,0:T(8,128)(2,1)S(1)}, bf16[8,4,16,256]{3,2,1,0:T(8,128)(2,1)}, u32[]{:S(2)}, u32[]{:S(2)}) collective-permute-start(bf16[8,4,16,256]{3,2,1,0:T(8,128)(2,1)S(1)} %pad_maximum_fusion.3), channel_id=1, source_target_pairs={{0,6},{1,25},{2,0},{3,27},{4,2},{5,29},{6,4},{7,31},{8,14},{9,1},{... | collective-permute-start | bytes 786440 | tf_op jit(solution)/shard_map/ppermute | solution.py:42
  87.5 2.7 %collective-permute-done.30 = bf16[8,4,16,256]{3,2,1,0:T(8,128)(2,1)} collective-permute-done((bf16[8,4,16,256]{3,2,1,0:T(8,128)(2,1)S(1)}, bf16[8,4,16,256]{3,2,1,0:T(8,128)(2,1)}, u32[]{:S(2)}, u32[]{:S(2)}) %collective-permute-start.30) | collective-permute-done | bytes 262176 | tf_op jit(solution)/shard_map/ppermute | solution.py:42
  90.2 2.1 %collective-permute-done.31 = bf16[8,4,16,256]{3,2,1,0:T(8,128)(2,1)} collective-permute-done((bf16[8,4,16,256]{3,2,1,0:T(8,128)(2,1)S(1)}, bf16[8,4,16,256]{3,2,1,0:T(8,128)(2,1)}, u32[]{:S(2)}, u32[]{:S(2)}) %collective-permute-start.31) | collective-permute-done | bytes 262176 | tf_op jit(solution)/shard_map/ppermute | solution.py:42
  92.3 1.9 %collective-permute-done.32 = bf16[8,4,16,256]{3,2,1,0:T(8,128)(2,1)} collective-permute-done((bf16[8,4,16,256]{3,2,1,0:T(8,128)(2,1)S(1)}, bf16[8,4,16,256]{3,2,1,0:T(8,128)(2,1)}, u32[]{:S(2)}, u32[]{:S(2)}) %collective-permute-start.32) | collective-permute-done | bytes 262176 | tf_op jit(solution)/shard_map/ppermute | solution.py:42
  95.4 1.4 %collective-permute-start.33 = (bf16[8,16,256]{2,1,0:T(8,128)(2,1)S(1)}, bf16[8,16,256]{2,1,0:T(8,128)(2,1)S(1)}, u32[]{:S(2)}, u32[]{:S(2)}) collective-permute-start(bf16[8,16,256]{2,1,0:T(8,128)(2,1)S(1)} %get-tuple-element.97), channel_id=1, source_target_pairs={{0,96},{1,97},{2,98},{3,99},{4,100},{5,101},{6,102},{7,103},{8,104... | collective-permute-start | bytes 196616 | tf_op jit(solution)/shard_map/ppermute | solution.py:42
  97.0 2.7 %collective-permute-start.35 = (bf16[8,16,256]{2,1,0:T(8,128)(2,1)S(1)}, bf16[8,16,256]{2,1,0:T(8,128)(2,1)S(1)}, u32[]{:S(2)}, u32[]{:S(2)}) collective-permute-start(bf16[8,16,256]{2,1,0:T(8,128)(2,1)S(1)} %get-tuple-element.98), channel_id=1, source_target_pairs={{0,64},{1,65},{2,66},{3,67},{4,68},{5,69},{6,70},{7,71},{8,72},{9,... | collective-permute-start | bytes 196616 | tf_op jit(solution)/shard_map/ppermute | solution.py:42
  99.8 1.3 %collective-permute-done.34 = bf16[8,16,256]{2,1,0:T(8,128)(2,1)S(1)} collective-permute-done((bf16[8,16,256]{2,1,0:T(8,128)(2,1)S(1)}, bf16[8,16,256]{2,1,0:T(8,128)(2,1)S(1)}, u32[]{:S(2)}, u32[]{:S(2)}) %collective-permute-start.34) | collective-permute-done | bytes 65568 | tf_op jit(solution)/shard_map/ppermute | solution.py:42
  102.1 5.9 %collective-permute-start.36 = (bf16[4,8,16,128]{3,2,1,0:T(8,128)(2,1)S(1)}, bf16[4,8,16,128]{3,2,1,0:T(8,128)(2,1)S(1)}, u32[]{:S(2)}, u32[]{:S(2)}) collective-permute-start(bf16[4,8,16,128]{3,2,1,0:T(8,128)(2,1)S(1)} %get-tuple-element.95), channel_id=1, source_target_pairs={{0,1},{1,0},{2,3},{3,2},{4,5},{5,4},{6,7},{7,6},{8,9},{9,8},{10,11... | collective-permute-start | bytes 393224 | tf_op jit(solution)/shard_map/ppermute | solution.py:42
  109.7 14.2 %all_to_all.5.pieces = bf16[32,3,16,128]{3,2,1,0:T(8,128)(2,1)S(1)} all-to-all(bf16[32,3,16,128]{3,2,1,0:T(8,128)(2,1)S(1)} %bitcast.52), channel_id=1, replica_groups=mesh['grp'=4,'sub'=32] {'sub'}, dimensions={0} | all-to-all | bytes 786432 | tf_op jit(solution)/shard_map/all_to_all | solution.py:294
  (83 shorter events, 29.7 us)
Async XLA Ops:
  4.0 33.8 %collective-permute-start.1 = (bf16[16,256,512]{2,1,0:T(8,128)(2,1)}, bf16[16,256,512]{2,1,0:T(8,128)(2,1)}, u32[]{:S(2)}, u32[]{:S(2)}) collective-permute-start(bf16[16,256,512]{2,1,0:T(8,128)(2,1)} %t_own.5), channel_id=1, source_target_pairs={{0,1},{1,0},{2,3},{3,2},{4,5},{5,4},{6,7},{7,6},{8,9},{9,8},{10,11... | collective-permute-start | bytes 12582920 | tf_op jit(solution)/shard_map/ppermute | solution.py:42
  5.1 6.1 %collective-permute-start.3 = (bf16[2,128,256]{2,1,0:T(8,128)(2,1)S(1)}, bf16[2,128,256]{2,1,0:T(8,128)(2,1)S(1)}, u32[]{:S(2)}, u32[]{:S(2)}) collective-permute-start(bf16[2,128,256]{2,1,0:T(8,128)(2,1)S(1)} %maximum_select_fusion), channel_id=1, source_target_pairs={{0,8},{1,3},{2,10},{3,5},{4,12},{5,7},{6,14},{7,1},{8,16},{9,11},{... | collective-permute-start | bytes 393224 | tf_op jit(solution)/shard_map/ppermute | solution.py:42
  6.6 6.7 %collective-permute-start.4 = (bf16[2,128,256]{2,1,0:T(8,128)(2,1)S(1)}, bf16[2,128,256]{2,1,0:T(8,128)(2,1)S(1)}, u32[]{:S(2)}, u32[]{:S(2)}) collective-permute-start(bf16[2,128,256]{2,1,0:T(8,128)(2,1)S(1)} %maximum_select_fusion), channel_id=1, source_target_pairs={{0,16},{1,5},{2,18},{3,7},{4,20},{5,1},{6,22},{7,3},{8,24},{9,13},... | collective-permute-start | bytes 393224 | tf_op jit(solution)/shard_map/ppermute | solution.py:42
  13.4 10.5 %collective-permute-start.7 = (bf16[8,128,256]{2,1,0:T(8,128)(2,1)S(1)}, bf16[8,128,256]{2,1,0:T(8,128)(2,1)S(1)}, u32[]{:S(2)}, u32[]{:S(2)}) collective-permute-start(bf16[8,128,256]{2,1,0:T(8,128)(2,1)S(1)} %pad_maximum_fusion.set0), channel_id=1, source_target_pairs={{0,2},{1,9},{2,4},{3,11},{4,6},{5,13},{6,0},{7,15},{8,10},{9,17},{... | collective-permute-start | bytes 1572872 | tf_op jit(solution)/shard_map/ppermute | solution.py:42
  14.7 12.1 %collective-permute-start.8 = (bf16[8,128,256]{2,1,0:T(8,128)(2,1)S(1)}, bf16[8,128,256]{2,1,0:T(8,128)(2,1)S(1)}, u32[]{:S(2)}, u32[]{:S(2)}) collective-permute-start(bf16[8,128,256]{2,1,0:T(8,128)(2,1)S(1)} %pad_maximum_fusion.set0), channel_id=1, source_target_pairs={{0,6},{1,25},{2,0},{3,27},{4,2},{5,29},{6,4},{7,31},{8,14},{9,1},{... | collective-permute-start | bytes 1572872 | tf_op jit(solution)/shard_map/ppermute | solution.py:42
  16.1 13.5 %collective-permute-start.9 = (bf16[8,128,256]{2,1,0:T(8,128)(2,1)S(1)}, bf16[8,128,256]{2,1,0:T(8,128)(2,1)S(1)}, u32[]{:S(2)}, u32[]{:S(2)}) collective-permute-start(bf16[8,128,256]{2,1,0:T(8,128)(2,1)S(1)} %pad_maximum_fusion.set0), channel_id=1, source_target_pairs={{0,4},{1,17},{2,6},{3,19},{4,0},{5,21},{6,2},{7,23},{8,12},{9,25},... | collective-permute-start | bytes 1572872 | tf_op jit(solution)/shard_map/ppermute | solution.py:42
  22.3 8.4 %collective-permute-start.10 = (bf16[256,256]{1,0:T(8,128)(2,1)S(1)}, bf16[256,256]{1,0:T(8,128)(2,1)S(1)}, u32[]{:S(2)}, u32[]{:S(2)}) collective-permute-start(bf16[256,256]{1,0:T(8,128)(2,1)S(1)} %broadcast_multiply_fusion), channel_id=1, source_target_pairs={{0,32},{1,33},{2,34},{3,35},{4,36},{5,37},{6,38},{7,39},{8,40},{9,... | collective-permute-start | bytes 393224 | tf_op jit(solution)/shard_map/ppermute | solution.py:42
  23.9 6.8 %collective-permute-start.11 = (bf16[256,256]{1,0:T(8,128)(2,1)S(1)}, bf16[256,256]{1,0:T(8,128)(2,1)S(1)}, u32[]{:S(2)}, u32[]{:S(2)}) collective-permute-start(bf16[256,256]{1,0:T(8,128)(2,1)S(1)} %broadcast_multiply_fusion), channel_id=1, source_target_pairs={{0,96},{1,97},{2,98},{3,99},{4,100},{5,101},{6,102},{7,103},{8,104... | collective-permute-start | bytes 393224 | tf_op jit(solution)/shard_map/ppermute | solution.py:42
  26.7 5.6 %collective-permute-start.12 = (bf16[256,256]{1,0:T(8,128)(2,1)S(1)}, bf16[256,256]{1,0:T(8,128)(2,1)S(1)}, u32[]{:S(2)}, u32[]{:S(2)}) collective-permute-start(bf16[256,256]{1,0:T(8,128)(2,1)S(1)} %broadcast_multiply_fusion), channel_id=1, source_target_pairs={{0,64},{1,65},{2,66},{3,67},{4,68},{5,69},{6,70},{7,71},{8,72},{9,... | collective-permute-start | bytes 393224 | tf_op jit(solution)/shard_map/ppermute | solution.py:42
  32.4 5.4 %collective-permute-start.13 = (bf16[4,128,256]{2,1,0:T(8,128)(2,1)S(1)}, bf16[4,128,256]{2,1,0:T(8,128)(2,1)S(1)}, u32[]{:S(2)}, u32[]{:S(2)}) collective-permute-start(bf16[4,128,256]{2,1,0:T(8,128)(2,1)S(1)} %shard_map.74.refs_0_), channel_id=1, source_target_pairs={{0,1},{1,0},{2,3},{3,2},{4,5},{5,4},{6,7},{7,6},{8,9},{9,8},{10,11... | collective-permute-start | bytes 786440 | tf_op jit(solution)/shard_map/ppermute | solution.py:42
  35.7 7.9 %collective-permute-start.14 = (bf16[4,128,256]{2,1,0:T(8,128)(2,1)S(1)}, bf16[4,128,256]{2,1,0:T(8,128)(2,1)S(1)}, u32[]{:S(2)}, u32[]{:S(2)}) collective-permute-start(bf16[4,128,256]{2,1,0:T(8,128)(2,1)S(1)} %shard_map.74.refs_0_), channel_id=1, source_target_pairs={{0,96},{1,97},{2,98},{3,99},{4,100},{5,101},{6,102},{7,103},{8,104... | collective-permute-start | bytes 786440 | tf_op jit(solution)/shard_map/ppermute | solution.py:42
  37.0 8.8 %collective-permute-start.15 = (bf16[4,128,256]{2,1,0:T(8,128)(2,1)S(1)}, bf16[4,128,256]{2,1,0:T(8,128)(2,1)S(1)}, u32[]{:S(2)}, u32[]{:S(2)}) collective-permute-start(bf16[4,128,256]{2,1,0:T(8,128)(2,1)S(1)} %shard_map.74.refs_0_), channel_id=1, source_target_pairs={{0,32},{1,33},{2,34},{3,35},{4,36},{5,37},{6,38},{7,39},{8,40},{9,... | collective-permute-start | bytes 786440 | tf_op jit(solution)/shard_map/ppermute | solution.py:42
  37.2 10.9 %collective-permute-start.19 = (bf16[3,256,256]{2,1,0:T(8,128)(2,1)S(1)}, bf16[3,256,256]{2,1,0:T(8,128)(2,1)S(1)}, u32[]{:S(2)}, u32[]{:S(2)}) collective-permute-start(bf16[3,256,256]{2,1,0:T(8,128)(2,1)S(1)} %pad_maximum_fusion.1.own), channel_id=1, source_target_pairs={{0,1},{1,0},{2,3},{3,2},{4,5},{5,4},{6,7},{7,6},{8,9},{9,8},{10,11... | collective-permute-start | bytes 1179656 | tf_op jit(solution)/shard_map/ppermute | solution.py:42
  45.7 8.2 %collective-permute-start.20 = (bf16[4,128,256]{2,1,0:T(8,128)(2,1)S(1)}, bf16[4,128,256]{2,1,0:T(8,128)(2,1)S(1)}, u32[]{:S(2)}, u32[]{:S(2)}) collective-permute-start(bf16[4,128,256]{2,1,0:T(8,128)(2,1)S(1)} %collective-permute-done.15.refs_0_), channel_id=1, source_target_pairs={{0,1},{1,0},{2,3},{3,2},{4,5},{5,4},{6,7},{7,6},{8,9},{9,8},{10,11... | collective-permute-start | bytes 786440 | tf_op jit(solution)/shard_map/ppermute | solution.py:42
  46.9 8.9 %collective-permute-start.21 = (bf16[4,128,256]{2,1,0:T(8,128)(2,1)S(1)}, bf16[4,128,256]{2,1,0:T(8,128)(2,1)S(1)}, u32[]{:S(2)}, u32[]{:S(2)}) collective-permute-start(bf16[4,128,256]{2,1,0:T(8,128)(2,1)S(1)} %collective-permute-done.14.refs_2_), channel_id=1, source_target_pairs={{0,1},{1,0},{2,3},{3,2},{4,5},{5,4},{6,7},{7,6},{8,9},{9,8},{10,11... | collective-permute-start | bytes 786440 | tf_op jit(solution)/shard_map/ppermute | solution.py:42
  46.9 14.2 %collective-permute-start.22 = (bf16[4,128,256]{2,1,0:T(8,128)(2,1)S(1)}, bf16[4,128,256]{2,1,0:T(8,128)(2,1)S(1)}, u32[]{:S(2)}, u32[]{:S(2)}) collective-permute-start(bf16[4,128,256]{2,1,0:T(8,128)(2,1)S(1)} %shard_map.74.refs_0_), channel_id=1, source_target_pairs={{0,64},{1,65},{2,66},{3,67},{4,68},{5,69},{6,70},{7,71},{8,72},{9,... | collective-permute-start | bytes 786440 | tf_op jit(solution)/shard_map/ppermute | solution.py:42
  46.9 17.0 %collective-permute-start.16 = (bf16[8,1,64,256]{3,2,1,0:T(8,128)(2,1)S(1)}, bf16[8,1,64,256]{3,2,1,0:T(8,128)(2,1)S(1)}, u32[]{:S(2)}, u32[]{:S(2)}) collective-permute-start(bf16[8,1,64,256]{3,2,1,0:T(8,128)(2,1)S(1)} %get-tuple-element.60), channel_id=1, source_target_pairs={{0,8},{1,3},{2,10},{3,5},{4,12},{5,7},{6,14},{7,1},{8,16},{9,11},{... | collective-permute-start | bytes 786440 | tf_op jit(solution)/shard_map/ppermute | solution.py:42
  48.1 16.3 %collective-permute-start.17 = (bf16[8,1,64,256]{3,2,1,0:T(8,128)(2,1)S(1)}, bf16[8,1,64,256]{3,2,1,0:T(8,128)(2,1)S(1)}, u32[]{:S(2)}, u32[]{:S(2)}) collective-permute-start(bf16[8,1,64,256]{3,2,1,0:T(8,128)(2,1)S(1)} %get-tuple-element.61), channel_id=1, source_target_pairs={{0,24},{1,7},{2,26},{3,1},{4,28},{5,3},{6,30},{7,5},{8,0},{9,15},{... | collective-permute-start | bytes 786440 | tf_op jit(solution)/shard_map/ppermute | solution.py:42
  54.0 10.4 %collective-permute-start.18 = (bf16[8,1,64,256]{3,2,1,0:T(8,128)(2,1)S(1)}, bf16[8,1,64,256]{3,2,1,0:T(8,128)(2,1)S(1)}, u32[]{:S(2)}, u32[]{:S(2)}) collective-permute-start(bf16[8,1,64,256]{3,2,1,0:T(8,128)(2,1)S(1)} %get-tuple-element.62), channel_id=1, source_target_pairs={{0,16},{1,5},{2,18},{3,7},{4,20},{5,1},{6,22},{7,3},{8,24},{9,13},... | collective-permute-start | bytes 786440 | tf_op jit(solution)/shard_map/ppermute | solution.py:42
  61.1 13.0 %collective-permute-start.23 = (bf16[8,2,64,256]{3,2,1,0:T(8,128)(2,1)S(1)}, bf16[8,2,64,256]{3,2,1,0:T(8,128)(2,1)S(1)}, u32[]{:S(2)}, u32[]{:S(2)}) collective-permute-start(bf16[8,2,64,256]{3,2,1,0:T(8,128)(2,1)S(1)} %get-tuple-element.77), channel_id=1, source_target_pairs={{0,8},{1,3},{2,10},{3,5},{4,12},{5,7},{6,14},{7,1},{8,16},{9,11},{... | collective-permute-start | bytes 1572872 | tf_op jit(solution)/shard_map/ppermute | solution.py:42
  61.9 13.7 %collective-permute-start.24 = (bf16[8,2,64,256]{3,2,1,0:T(8,128)(2,1)S(1)}, bf16[8,2,64,256]{3,2,1,0:T(8,128)(2,1)S(1)}, u32[]{:S(2)}, u32[]{:S(2)}) collective-permute-start(bf16[8,2,64,256]{3,2,1,0:T(8,128)(2,1)S(1)} %get-tuple-element.78), channel_id=1, source_target_pairs={{0,24},{1,7},{2,26},{3,1},{4,28},{5,3},{6,30},{7,5},{8,0},{9,15},{... | collective-permute-start | bytes 1572872 | tf_op jit(solution)/shard_map/ppermute | solution.py:42
  63.9 12.3 %collective-permute-start.25 = (bf16[8,2,64,256]{3,2,1,0:T(8,128)(2,1)S(1)}, bf16[8,2,64,256]{3,2,1,0:T(8,128)(2,1)S(1)}, u32[]{:S(2)}, u32[]{:S(2)}) collective-permute-start(bf16[8,2,64,256]{3,2,1,0:T(8,128)(2,1)S(1)} %get-tuple-element.79), channel_id=1, source_target_pairs={{0,16},{1,5},{2,18},{3,7},{4,20},{5,1},{6,22},{7,3},{8,24},{9,13},... | collective-permute-start | bytes 1572872 | tf_op jit(solution)/shard_map/ppermute | solution.py:42
  69.6 9.7 %collective-permute-start.27 = (bf16[8,1,64,256]{3,2,1,0:T(8,128)(2,1)S(1)}, bf16[8,1,64,256]{3,2,1,0:T(8,128)(2,1)S(1)}, u32[]{:S(2)}, u32[]{:S(2)}) collective-permute-start(bf16[8,1,64,256]{3,2,1,0:T(8,128)(2,1)S(1)} %get-tuple-element.82), channel_id=1, source_target_pairs={{0,8},{1,3},{2,10},{3,5},{4,12},{5,7},{6,14},{7,1},{8,16},{9,11},{... | collective-permute-start | bytes 786440 | tf_op jit(solution)/shard_map/ppermute | solution.py:42
  70.0 11.2 %collective-permute-start.28 = (bf16[8,1,64,256]{3,2,1,0:T(8,128)(2,1)S(1)}, bf16[8,1,64,256]{3,2,1,0:T(8,128)(2,1)S(1)}, u32[]{:S(2)}, u32[]{:S(2)}) collective-permute-start(bf16[8,1,64,256]{3,2,1,0:T(8,128)(2,1)S(1)} %get-tuple-element.83), channel_id=1, source_target_pairs={{0,24},{1,7},{2,26},{3,1},{4,28},{5,3},{6,30},{7,5},{8,0},{9,15},{... | collective-permute-start | bytes 786440 | tf_op jit(solution)/shard_map/ppermute | solution.py:42
  74.1 7.7 %collective-permute-start.29 = (bf16[8,1,64,256]{3,2,1,0:T(8,128)(2,1)S(1)}, bf16[8,1,64,256]{3,2,1,0:T(8,128)(2,1)S(1)}, u32[]{:S(2)}, u32[]{:S(2)}) collective-permute-start(bf16[8,1,64,256]{3,2,1,0:T(8,128)(2,1)S(1)} %get-tuple-element.84), channel_id=1, source_target_pairs={{0,16},{1,5},{2,18},{3,7},{4,20},{5,1},{6,22},{7,3},{8,24},{9,13},... | collective-permute-start | bytes 786440 | tf_op jit(solution)/shard_map/ppermute | solution.py:42
  82.0 8.1 %collective-permute-start.30 = (bf16[8,4,16,256]{3,2,1,0:T(8,128)(2,1)S(1)}, bf16[8,4,16,256]{3,2,1,0:T(8,128)(2,1)}, u32[]{:S(2)}, u32[]{:S(2)}) collective-permute-start(bf16[8,4,16,256]{3,2,1,0:T(8,128)(2,1)S(1)} %pad_maximum_fusion.2), channel_id=1, source_target_pairs={{0,2},{1,9},{2,4},{3,11},{4,6},{5,13},{6,0},{7,15},{8,10},{9,17},{... | collective-permute-start | bytes 786440 | tf_op jit(solution)/shard_map/ppermute | solution.py:42
  83.1 9.1 %collective-permute-start.31 = (bf16[8,4,16,256]{3,2,1,0:T(8,128)(2,1)S(1)}, bf16[8,4,16,256]{3,2,1,0:T(8,128)(2,1)}, u32[]{:S(2)}, u32[]{:S(2)}) collective-permute-start(bf16[8,4,16,256]{3,2,1,0:T(8,128)(2,1)S(1)} %pad_maximum_fusion.3), channel_id=1, source_target_pairs={{0,6},{1,25},{2,0},{3,27},{4,2},{5,29},{6,4},{7,31},{8,14},{9,1},{... | collective-permute-start | bytes 786440 | tf_op jit(solution)/shard_map/ppermute | solution.py:42
  86.2 8.0 %collective-permute-start.32 = (bf16[8,4,16,256]{3,2,1,0:T(8,128)(2,1)S(1)}, bf16[8,4,16,256]{3,2,1,0:T(8,128)(2,1)}, u32[]{:S(2)}, u32[]{:S(2)}) collective-permute-start(bf16[8,4,16,256]{3,2,1,0:T(8,128)(2,1)S(1)} %pad_maximum_fusion.4), channel_id=1, source_target_pairs={{0,4},{1,17},{2,6},{3,19},{4,0},{5,21},{6,2},{7,23},{8,12},{9,25},... | collective-permute-start | bytes 786440 | tf_op jit(solution)/shard_map/ppermute | solution.py:42
  95.4 4.4 %collective-permute-start.33 = (bf16[8,16,256]{2,1,0:T(8,128)(2,1)S(1)}, bf16[8,16,256]{2,1,0:T(8,128)(2,1)S(1)}, u32[]{:S(2)}, u32[]{:S(2)}) collective-permute-start(bf16[8,16,256]{2,1,0:T(8,128)(2,1)S(1)} %get-tuple-element.97), channel_id=1, source_target_pairs={{0,96},{1,97},{2,98},{3,99},{4,100},{5,101},{6,102},{7,103},{8,104... | collective-permute-start | bytes 196616 | tf_op jit(solution)/shard_map/ppermute | solution.py:42
  96.8 4.3 %collective-permute-start.34 = (bf16[8,16,256]{2,1,0:T(8,128)(2,1)S(1)}, bf16[8,16,256]{2,1,0:T(8,128)(2,1)S(1)}, u32[]{:S(2)}, u32[]{:S(2)}) collective-permute-start(bf16[8,16,256]{2,1,0:T(8,128)(2,1)S(1)} %get-tuple-element.99), channel_id=1, source_target_pairs={{0,32},{1,33},{2,34},{3,35},{4,36},{5,37},{6,38},{7,39},{8,40},{9,... | collective-permute-start | bytes 196616 | tf_op jit(solution)/shard_map/ppermute | solution.py:42
  97.0 5.0 %collective-permute-start.35 = (bf16[8,16,256]{2,1,0:T(8,128)(2,1)S(1)}, bf16[8,16,256]{2,1,0:T(8,128)(2,1)S(1)}, u32[]{:S(2)}, u32[]{:S(2)}) collective-permute-start(bf16[8,16,256]{2,1,0:T(8,128)(2,1)S(1)} %get-tuple-element.98), channel_id=1, source_target_pairs={{0,64},{1,65},{2,66},{3,67},{4,68},{5,69},{6,70},{7,71},{8,72},{9,... | collective-permute-start | bytes 196616 | tf_op jit(solution)/shard_map/ppermute | solution.py:42
  102.1 6.9 %collective-permute-start.36 = (bf16[4,8,16,128]{3,2,1,0:T(8,128)(2,1)S(1)}, bf16[4,8,16,128]{3,2,1,0:T(8,128)(2,1)S(1)}, u32[]{:S(2)}, u32[]{:S(2)}) collective-permute-start(bf16[4,8,16,128]{3,2,1,0:T(8,128)(2,1)S(1)} %get-tuple-element.95), channel_id=1, source_target_pairs={{0,1},{1,0},{2,3},{3,2},{4,5},{5,4},{6,7},{7,6},{8,9},{9,8},{10,11... | collective-permute-start | bytes 393224 | tf_op jit(solution)/shard_map/ppermute | solution.py:42
  (6 other events, 35.8 us)

commit v5 on v4

--- a/solution.py
+++ b/solution.py
@@ -110,6 +110,31 @@
     )(strips, own, oth)
 
 
+def keep_half_body(sc, own, oth, out_own, out_oth, sem):
+    rows = pl.ds(sc[0] * 8, 8)
+    copies = [
+        pltpu.make_async_copy(own.at[rows], out_own, sem.at[0]),
+        pltpu.make_async_copy(oth.at[rows], out_oth, sem.at[1]),
+    ]
+    for copy in copies:
+        copy.start()
+    for copy in copies:
+        copy.wait()
+
+
+def keep_half(core, own, oth):
+    shape = jax.ShapeDtypeStruct((8, 256, 512), BF)
+    return pl.pallas_call(
+        keep_half_body,
+        in_specs=[pl.BlockSpec(memory_space=pltpu.SMEM)] + [pl.BlockSpec(memory_space=pl.ANY)] * 2,
+        out_specs=[pl.BlockSpec(memory_space=pltpu.VMEM)] * 2,
+        scratch_shapes=[pltpu.SemaphoreType.DMA((2,))],
+        out_shape=[shape, shape],
+        compiler_params=pltpu.CompilerParams(vmem_limit_bytes=10 * MIB),
+        cost_estimate=pl.CostEstimate(flops=0, bytes_accessed=1000, transcendentals=0),
+    )(core, *[pltpu.with_memory_space_constraint(t, pltpu.HBM) for t in (own, oth)])
+
+
 def products_body(sc, t_own, t_oth, gv, *refs):
     halves, (send1, send2, send3, keep, go) = refs[: 2 * gv.shape[0]], refs[-5:]
     count = len(halves) // 2
@@ -134,18 +159,18 @@
             rows = slice(p * 256, (p + 1) * 256)
             out = jnp.dot(gv[r, :, 0:256], half_own[rows], preferred_element_type=F32)
             out += jnp.dot(gv[r, :, 256:512], half_oth[rows], preferred_element_type=F32)
-            send1[p, r] = out[0:64].astype(BF)
-            send2[p, r] = out[64:128].astype(BF)
-            send3[p, r] = out[128:192].astype(BF)
-            keep[p, r] = out[192:256]
+            send1[r, p] = out[0:64].astype(BF)
+            send2[r, p] = out[64:128].astype(BF)
+            send3[r, p] = out[128:192].astype(BF)
+            keep[r, p] = out[192:256]
 
 
 def products_of(core, t_own, t_oth, gv, halves, room, at, gv_at, begun=()):
     count = len(halves) // 2
-    block = pl.BlockSpec((STACK, count, 64, 256), lambda p, sc: (p, at, 0, 0))
-    shape = (8, room, 64, 256)
+    block = pl.BlockSpec((count, STACK, 64, 256), lambda p, sc: (at, p, 0, 0))
+    shape = (room, 8, 64, 256)
     first = 4 + 2 * count
-    functions = pl.BlockSpec((STACK, 256, 512), lambda p, sc: (sc[0] * (8 // STACK) + p, 0, 0))
+    functions = pl.BlockSpec((STACK, 256, 512), lambda p, sc: (p, 0, 0))
     return pl.pallas_call(
         products_body,
         grid_spec=pltpu.PrefetchScalarGridSpec(
@@ -162,7 +187,7 @@
         input_output_aliases={first + n: n for n in range(len(begun))},
         compiler_params=pltpu.CompilerParams(vmem_limit_bytes=(12 + 4 * count) * MIB),
         cost_estimate=pl.CostEstimate(flops=1000, bytes_accessed=1000, transcendentals=0),
-    )(core, pltpu.with_memory_space_constraint(t_own, pltpu.HBM), t_oth, gv, *halves, *begun)
+    )(core, t_own, t_oth, gv, *halves, *begun)
 
 
 def slots_body(sc, pieces, out):
@@ -242,10 +267,11 @@
     gv_rest = order_rows(strips, gv_rest, move(gv_rest, CORE))
     far, *side = [move(picked, DEPTH[r]) for r in (2, 3, 1)]
 
-    given = (c.reshape(1).astype(jnp.int32), three_centre, t_oth)
+    core = c.reshape(1).astype(jnp.int32)
+    given = (core, *keep_half(core, three_centre, t_oth))
     sends0 = products_of(*given, gv, (picked, move(picked, CORE)), 1, 0, 0)
     *sends0, side3, side1 = tie(*sends0, *side)
-    got0 = [move(sends0[d - 1], FIRST[d]) for d in (1, 3, 2)]
+    got0 = [move(sends0[d - 1], FIRST[d]) for d in (2, 1, 3)]
     halves = [h for a in (side1, side3) for h in (a, move(a, CORE))]
     sends1 = products_of(*given, gv_rest, halves, 2, 0, 0)
     *sends1, far = tie(*sends1, far)
@@ -258,20 +284,20 @@
             total = total + part.astype(F32)
         return total
 
-    got1 = [move(sends1[d - 1], FIRST[d]) for d in (1, 3, 2)]
-    got2 = [move(sends2[d - 1], FIRST[d]) for d in (1, 3, 2)]
+    got1 = [move(sends1[d - 1], FIRST[d]) for d in (2, 1, 3)]
+    got2 = [move(sends2[d - 1], FIRST[d]) for d in (2, 1, 3)]
     sums = [sum_of(sends0, got0), sum_of(sends1, got1), sum_of(sends2, got2)]
 
     def strip(e):
-        return jnp.concatenate([t[:, :, e * 16 : (e + 1) * 16] for t in sums], axis=1)
+        return jnp.concatenate([t[:, :, e * 16 : (e + 1) * 16] for t in sums])
 
     total = strip(0)
-    for e in (1, 3, 2):
+    for e in (2, 1, 3):
         total = total + move(strip(e).astype(BF), SECOND[e]).astype(F32)
     total = total.astype(BF)
 
     rows = jnp.stack(
-        [total[:, 0]] + [move(total[:, at], DEPTH[4 - r]) for at, r in ((1, 1), (2, 3), (3, 2))]
+        [total[0]] + [move(total[at], DEPTH[4 - r]) for at, r in ((3, 2), (1, 1), (2, 3))]
     )
     mine = lax.dynamic_slice_in_dim(rows, c * 128, 128, 3)
     other = move(lax.dynamic_slice_in_dim(rows, (1 - c) * 128, 128, 3), CORE)
@@ -286,7 +312,7 @@
     position = jnp.sum(earlier.astype(jnp.int32), axis=1)
     slots = owner_flat * CAP + position
     distance = (numbers // 16 - z + 4) % 4
-    stands = distance ^ (distance >> 1)
+    stands = (distance % 2) * 2 + distance // 2
     at = jnp.where((numbers // 8) % 2 == c, 0, 32) + stands * 8 + numbers % 8
     match = slots[None, :] == jnp.arange(32 * CAP, dtype=jnp.int32)[:, None]
     source = jnp.min(jnp.where(match, at[None, :], 64), axis=1)

time: 125 us -> 124 us (level)
  Pallas kernels: 16.3 us -> 14 us
  starting transfers between devices: 58.4 us -> 60.2 us
  waiting for transfers between devices: 28.7 us -> 27.1 us
    pallas_call x3, Pallas kernels: 12.5 us -> 7.96 us  [products_of(): pl.pallas_call(products_body, grid_spec=pltpu.PrefetchScalarGridSpec(num_...]
    pallas_call x0 -> x1, Pallas kernels: none -> 2.24 us  [keep_half(): pl.pallas_call(keep_half_body, in_specs=[pl.BlockSpec(memory_space=pltpu....]
    ppermute x37, starting transfers between devices: 58.4 us -> 60.2 us  [move(): return lax.ppermute(value, AXES, permutation)]
    ppermute x37, waiting for transfers between devices: 28.7 us -> 27.1 us  [move(): return lax.ppermute(value, AXES, permutation)]
  transfers between devices with their start and end apart: 37 -> 37, of which waited for: 21 -> 20; matrix products, arithmetic and copies ran while one was open for 2% -> 2% of each run, Pallas kernels for 12% -> 10%
where the time goes in v5:
time: 124 us
  starting transfers between devices  60.2 us (49%)
  waiting for transfers between devices  27.1 us (22%)
  blocking collectives  15.3 us (12%)
  Pallas kernels  14 us (11%)
  other arithmetic  5.21 us (4%)
  between operations  1.61 us (1%)
    ppermute x37, starting transfers between devices, move(): return lax.ppermute(value, AXES, permutation)  60.2 us
    ppermute x37, waiting for transfers between devices, move(): return lax.ppermute(value, AXES, permutation)  27.1 us
    all_to_all x1, blocking collectives, per_device(): lax.all_to_all(outgoing.reshape(32, CAP, 16, 128), 'sub', split_axis=0, c...  15.3 us
    pallas_call x3, Pallas kernels, products_of(): pl.pallas_call(products_body, grid_spec=pltpu.PrefetchScalarGridSpec(num_...  7.96 us
  transfers between devices with their start and end apart: 37, of which 20 were waited for; matrix products, arithmetic and copies ran while one was open for 2% of the time, Pallas kernels for 10%

profile of v5, /device:TPU:1, one launch (start us, length us, event | category | flops | bytes accessed | tf_op | source)
XLA Modules:
  0.0 123.8 jit_solution(9988666345222917769)
XLA Ops:
  1.6 1.5 %collective-permute-start = (bf16[128,256]{1,0:T(8,128)(2,1)S(1)}, bf16[128,256]{1,0:T(8,128)(2,1)S(1)}, u32[]{:S(2)}, u32[]{:S(2)}) collective-permute-start(bf16[128,256]{1,0:T(8,128)(2,1)S(1)} %get-tuple-element.111), channel_id=1, source_target_pairs={{0,1},{1,0},{2,3},{3,2},{4,5},{5,4},{6,7},{7,6},{8,9},{9,8},{10,11... | collective-permute-start | bytes 196616 | tf_op jit(solution)/shard_map/ppermute | solution.py:42
  5.1 1.4 %collective-permute-start.3 = (bf16[2,128,256]{2,1,0:T(8,128)(2,1)S(1)}, bf16[2,128,256]{2,1,0:T(8,128)(2,1)S(1)}, u32[]{:S(2)}, u32[]{:S(2)}) collective-permute-start(bf16[2,128,256]{2,1,0:T(8,128)(2,1)S(1)} %maximum_select_fusion), channel_id=1, source_target_pairs={{0,8},{1,3},{2,10},{3,5},{4,12},{5,7},{6,14},{7,1},{8,16},{9,11},{... | collective-permute-start | bytes 393224 | tf_op jit(solution)/shard_map/ppermute | solution.py:42
  6.6 2.6 %collective-permute-start.4 = (bf16[2,128,256]{2,1,0:T(8,128)(2,1)S(1)}, bf16[2,128,256]{2,1,0:T(8,128)(2,1)S(1)}, u32[]{:S(2)}, u32[]{:S(2)}) collective-permute-start(bf16[2,128,256]{2,1,0:T(8,128)(2,1)S(1)} %maximum_select_fusion), channel_id=1, source_target_pairs={{0,16},{1,5},{2,18},{3,7},{4,20},{5,1},{6,22},{7,3},{8,24},{9,13},... | collective-permute-start | bytes 393224 | tf_op jit(solution)/shard_map/ppermute | solution.py:42
  11.2 2.1 %collective-permute-done.4 = bf16[2,128,256]{2,1,0:T(8,128)(2,1)S(1)} collective-permute-done((bf16[2,128,256]{2,1,0:T(8,128)(2,1)S(1)}, bf16[2,128,256]{2,1,0:T(8,128)(2,1)S(1)}, u32[]{:S(2)}, u32[]{:S(2)}) %collective-permute-start.4) | collective-permute-done | bytes 131104 | tf_op jit(solution)/shard_map/ppermute | solution.py:42
  14.7 1.5 %collective-permute-start.8 = (bf16[8,128,256]{2,1,0:T(8,128)(2,1)S(1)}, bf16[8,128,256]{2,1,0:T(8,128)(2,1)S(1)}, u32[]{:S(2)}, u32[]{:S(2)}) collective-permute-start(bf16[8,128,256]{2,1,0:T(8,128)(2,1)S(1)} %pad_maximum_fusion.set0), channel_id=1, source_target_pairs={{0,6},{1,25},{2,0},{3,27},{4,2},{5,29},{6,4},{7,31},{8,14},{9,1},{... | collective-permute-start | bytes 1572872 | tf_op jit(solution)/shard_map/ppermute | solution.py:42
  16.1 1.5 %collective-permute-start.9 = (bf16[8,128,256]{2,1,0:T(8,128)(2,1)S(1)}, bf16[8,128,256]{2,1,0:T(8,128)(2,1)S(1)}, u32[]{:S(2)}, u32[]{:S(2)}) collective-permute-start(bf16[8,128,256]{2,1,0:T(8,128)(2,1)S(1)} %pad_maximum_fusion.set0), channel_id=1, source_target_pairs={{0,4},{1,17},{2,6},{3,19},{4,0},{5,21},{6,2},{7,23},{8,12},{9,25},... | collective-permute-start | bytes 1572872 | tf_op jit(solution)/shard_map/ppermute | solution.py:42
  17.7 2.3 %collective-permute-start.2 = (s32[1,2]{1,0:T(1,128)}, s32[1,2]{1,0:T(1,128)S(1)}, u32[]{:S(2)}, u32[]{:S(2)}) collective-permute-start(s32[1,2]{1,0:T(1,128)} %param.8), channel_id=1, source_target_pairs={{0,1},{1,0},{2,3},{3,2},{4,5},{5,4},{6,7},{7,6},{8,9},{9,8},{10,11... | collective-permute-start | bytes 32 | tf_op jit(solution)/shard_map/ppermute | solution.py:42
  22.3 1.6 %collective-permute-start.10 = (bf16[256,256]{1,0:T(8,128)(2,1)S(1)}, bf16[256,256]{1,0:T(8,128)(2,1)S(1)}, u32[]{:S(2)}, u32[]{:S(2)}) collective-permute-start(bf16[256,256]{1,0:T(8,128)(2,1)S(1)} %broadcast_multiply_fusion), channel_id=1, source_target_pairs={{0,32},{1,33},{2,34},{3,35},{4,36},{5,37},{6,38},{7,39},{8,40},{9,... | collective-permute-start | bytes 393224 | tf_op jit(solution)/shard_map/ppermute | solution.py:42
  23.9 2.8 %collective-permute-start.11 = (bf16[256,256]{1,0:T(8,128)(2,1)S(1)}, bf16[256,256]{1,0:T(8,128)(2,1)S(1)}, u32[]{:S(2)}, u32[]{:S(2)}) collective-permute-start(bf16[256,256]{1,0:T(8,128)(2,1)S(1)} %broadcast_multiply_fusion), channel_id=1, source_target_pairs={{0,96},{1,97},{2,98},{3,99},{4,100},{5,101},{6,102},{7,103},{8,104... | collective-permute-start | bytes 393224 | tf_op jit(solution)/shard_map/ppermute | solution.py:42
  30.7 1.7 %collective-permute-done.12 = bf16[256,256]{1,0:T(8,128)(2,1)S(1)} collective-permute-done((bf16[256,256]{1,0:T(8,128)(2,1)S(1)}, bf16[256,256]{1,0:T(8,128)(2,1)S(1)}, u32[]{:S(2)}, u32[]{:S(2)}) %collective-permute-start.12) | collective-permute-done | bytes 131104 | tf_op jit(solution)/shard_map/ppermute | solution.py:42
  32.4 3.3 %collective-permute-start.13 = (bf16[4,128,256]{2,1,0:T(8,128)(2,1)S(1)}, bf16[4,128,256]{2,1,0:T(8,128)(2,1)S(1)}, u32[]{:S(2)}, u32[]{:S(2)}) collective-permute-start(bf16[4,128,256]{2,1,0:T(8,128)(2,1)S(1)} %shard_map.75.refs_0_), channel_id=1, source_target_pairs={{0,1},{1,0},{2,3},{3,2},{4,5},{5,4},{6,7},{7,6},{8,9},{9,8},{10,11... | collective-permute-start | bytes 786440 | tf_op jit(solution)/shard_map/ppermute | solution.py:42
  37.8 2.2 %shard_map.73 = (bf16[8,256,512]{2,1,0:T(8,128)(2,1)S(1)}, bf16[8,256,512]{2,1,0:T(8,128)(2,1)S(1)}) custom-call(s32[1]{0:T(128)} %bitcast.1.sc, bf16[16,256,512]{2,1,0:T(8,128)(2,1)} %own.1, bf16[16,256,512]{2,1,0:T(8,128)(2,1)} %collective-permute-done.1.oth), custom_call_target="tpu_custom_call" | custom-call | bytes 1000 | tf_op jit(solution)/shard_map/pallas_call | solution.py:127
  40.1 2.0 %shard_map.76 = (bf16[1,8,64,256]{3,2,1,0:T(8,128)(2,1)S(1)}, bf16[1,8,64,256]{3,2,1,0:T(8,128)(2,1)S(1)}, bf16[1,8,64,256]{3,2,1,0:T(8,128)(2,1)S(1)}, f32[1,8,64,256]{3,2,1,0:T(8,128)S(1)}) custom-call(s32[1]{0:T(128)} %bitcast.1.sc, bf16[8,256,512]{2,1,0:T(8,128)(2,1)S(1)} %get-tuple-element.48.t_own, bf16[8,256,512]{2,1,0:T(8,128)(2,1)S(1)} %get-tuple-element.49.t_oth, ...), custom_call_target="tpu_custom_call" | custom-call | flops 1000 | bytes 1000 | tf_op jit(solution)/shard_map/pallas_call | solution.py:174
  42.1 1.5 %collective-permute-done.14.refs_2_ = bf16[4,128,256]{2,1,0:T(8,128)(2,1)S(1)} collective-permute-done((bf16[4,128,256]{2,1,0:T(8,128)(2,1)S(1)}, bf16[4,128,256]{2,1,0:T(8,128)(2,1)S(1)}, u32[]{:S(2)}, u32[]{:S(2)}) %collective-permute-start.14) | collective-permute-done | bytes 262176 | tf_op jit(solution)/shard_map/ppermute | solution.py:42
  43.6 2.1 %collective-permute-done.15.refs_0_ = bf16[4,128,256]{2,1,0:T(8,128)(2,1)S(1)} collective-permute-done((bf16[4,128,256]{2,1,0:T(8,128)(2,1)S(1)}, bf16[4,128,256]{2,1,0:T(8,128)(2,1)S(1)}, u32[]{:S(2)}, u32[]{:S(2)}) %collective-permute-start.15) | collective-permute-done | bytes 262176 | tf_op jit(solution)/shard_map/ppermute | solution.py:42
  46.9 6.8 %collective-permute-start.16 = (bf16[1,8,64,256]{3,2,1,0:T(8,128)(2,1)S(1)}, bf16[1,8,64,256]{3,2,1,0:T(8,128)(2,1)S(1)}, u32[]{:S(2)}, u32[]{:S(2)}) collective-permute-start(bf16[1,8,64,256]{3,2,1,0:T(8,128)(2,1)S(1)} %get-tuple-element.64), channel_id=1, source_target_pairs={{0,16},{1,5},{2,18},{3,7},{4,20},{5,1},{6,22},{7,3},{8,24},{9,13},... | collective-permute-start | bytes 786440 | tf_op jit(solution)/shard_map/ppermute | solution.py:42
  54.5 2.0 %collective-permute-start.18 = (bf16[1,8,64,256]{3,2,1,0:T(8,128)(2,1)S(1)}, bf16[1,8,64,256]{3,2,1,0:T(8,128)(2,1)S(1)}, u32[]{:S(2)}, u32[]{:S(2)}) collective-permute-start(bf16[1,8,64,256]{3,2,1,0:T(8,128)(2,1)S(1)} %get-tuple-element.66), channel_id=1, source_target_pairs={{0,24},{1,7},{2,26},{3,1},{4,28},{5,3},{6,30},{7,5},{8,0},{9,15},{... | collective-permute-start | bytes 786440 | tf_op jit(solution)/shard_map/ppermute | solution.py:42
  57.1 3.9 %shard_map.78 = (bf16[2,8,64,256]{3,2,1,0:T(8,128)(2,1)S(1)}, bf16[2,8,64,256]{3,2,1,0:T(8,128)(2,1)S(1)}, bf16[2,8,64,256]{3,2,1,0:T(8,128)(2,1)S(1)}, f32[2,8,64,256]{3,2,1,0:T(8,128)S(1)}) custom-call(s32[1]{0:T(128)} %bitcast.1.sc, bf16[8,256,512]{2,1,0:T(8,128)(2,1)S(1)} %get-tuple-element.48.t_own, bf16[8,256,512]{2,1,0:T(8,128)(2,1)S(1)} %get-tuple-element.49.t_oth, ...), custom_call_target="tpu_custom_call" | custom-call | flops 1000 | bytes 1000 | tf_op jit(solution)/shard_map/pallas_call | solution.py:174
  61.0 1.7 %collective-permute-start.23 = (bf16[2,8,64,256]{3,2,1,0:T(8,128)(2,1)S(1)}, bf16[2,8,64,256]{3,2,1,0:T(8,128)(2,1)S(1)}, u32[]{:S(2)}, u32[]{:S(2)}) collective-permute-start(bf16[2,8,64,256]{3,2,1,0:T(8,128)(2,1)S(1)} %get-tuple-element.81), channel_id=1, source_target_pairs={{0,16},{1,5},{2,18},{3,7},{4,20},{5,1},{6,22},{7,3},{8,24},{9,13},... | collective-permute-start | bytes 1572872 | tf_op jit(solution)/shard_map/ppermute | solution.py:42
  63.3 2.0 %collective-permute-start.25 = (bf16[2,8,64,256]{3,2,1,0:T(8,128)(2,1)S(1)}, bf16[2,8,64,256]{3,2,1,0:T(8,128)(2,1)S(1)}, u32[]{:S(2)}, u32[]{:S(2)}) collective-permute-start(bf16[2,8,64,256]{3,2,1,0:T(8,128)(2,1)S(1)} %get-tuple-element.83), channel_id=1, source_target_pairs={{0,24},{1,7},{2,26},{3,1},{4,28},{5,3},{6,30},{7,5},{8,0},{9,15},{... | collective-permute-start | bytes 1572872 | tf_op jit(solution)/shard_map/ppermute | solution.py:42
  66.8 2.0 %shard_map.79 = (bf16[1,8,64,256]{3,2,1,0:T(8,128)(2,1)S(1)}, bf16[1,8,64,256]{3,2,1,0:T(8,128)(2,1)S(1)}, bf16[1,8,64,256]{3,2,1,0:T(8,128)(2,1)S(1)}, f32[1,8,64,256]{3,2,1,0:T(8,128)S(1)}) custom-call(s32[1]{0:T(128)} %bitcast.1.sc, bf16[8,256,512]{2,1,0:T(8,128)(2,1)S(1)} %get-tuple-element.48.t_own, bf16[8,256,512]{2,1,0:T(8,128)(2,1)S(1)} %get-tuple-element.49.t_oth, ...), custom_call_target="tpu_custom_call" | custom-call | flops 1000 | bytes 1000 | tf_op jit(solution)/shard_map/pallas_call | solution.py:174
  68.9 3.9 %collective-permute-start.27 = (bf16[1,8,64,256]{3,2,1,0:T(8,128)(2,1)S(1)}, bf16[1,8,64,256]{3,2,1,0:T(8,128)(2,1)S(1)}, u32[]{:S(2)}, u32[]{:S(2)}) collective-permute-start(bf16[1,8,64,256]{3,2,1,0:T(8,128)(2,1)S(1)} %get-tuple-element.86), channel_id=1, source_target_pairs={{0,16},{1,5},{2,18},{3,7},{4,20},{5,1},{6,22},{7,3},{8,24},{9,13},... | collective-permute-start | bytes 786440 | tf_op jit(solution)/shard_map/ppermute | solution.py:42
  73.5 2.0 %collective-permute-start.29 = (bf16[1,8,64,256]{3,2,1,0:T(8,128)(2,1)S(1)}, bf16[1,8,64,256]{3,2,1,0:T(8,128)(2,1)S(1)}, u32[]{:S(2)}, u32[]{:S(2)}) collective-permute-start(bf16[1,8,64,256]{3,2,1,0:T(8,128)(2,1)S(1)} %get-tuple-element.88), channel_id=1, source_target_pairs={{0,24},{1,7},{2,26},{3,1},{4,28},{5,3},{6,30},{7,5},{8,0},{9,15},{... | collective-permute-start | bytes 786440 | tf_op jit(solution)/shard_map/ppermute | solution.py:42
  76.9 2.3 %collective-permute-done.27 = bf16[1,8,64,256]{3,2,1,0:T(8,128)(2,1)S(1)} collective-permute-done((bf16[1,8,64,256]{3,2,1,0:T(8,128)(2,1)S(1)}, bf16[1,8,64,256]{3,2,1,0:T(8,128)(2,1)S(1)}, u32[]{:S(2)}, u32[]{:S(2)}) %collective-permute-start.27) | collective-permute-done | bytes 262176 | tf_op jit(solution)/shard_map/ppermute | solution.py:42
  79.2 2.7 %collective-permute-done.28 = bf16[1,8,64,256]{3,2,1,0:T(8,128)(2,1)S(1)} collective-permute-done((bf16[1,8,64,256]{3,2,1,0:T(8,128)(2,1)S(1)}, bf16[1,8,64,256]{3,2,1,0:T(8,128)(2,1)S(1)}, u32[]{:S(2)}, u32[]{:S(2)}) %collective-permute-start.28) | collective-permute-done | bytes 262176 | tf_op jit(solution)/shard_map/ppermute | solution.py:42
  82.1 2.1 %collective-permute-start.30 = (bf16[4,8,16,256]{3,2,1,0:T(8,128)(2,1)S(1)}, bf16[4,8,16,256]{3,2,1,0:T(8,128)(2,1)}, u32[]{:S(2)}, u32[]{:S(2)}) collective-permute-start(bf16[4,8,16,256]{3,2,1,0:T(8,128)(2,1)S(1)} %pad_maximum_fusion.2), channel_id=1, source_target_pairs={{0,4},{1,17},{2,6},{3,19},{4,0},{5,21},{6,2},{7,23},{8,12},{9,25},... | collective-permute-start | bytes 786440 | tf_op jit(solution)/shard_map/ppermute | solution.py:42
  85.4 1.6 %collective-permute-start.32 = (bf16[4,8,16,256]{3,2,1,0:T(8,128)(2,1)S(1)}, bf16[4,8,16,256]{3,2,1,0:T(8,128)(2,1)}, u32[]{:S(2)}, u32[]{:S(2)}) collective-permute-start(bf16[4,8,16,256]{3,2,1,0:T(8,128)(2,1)S(1)} %pad_maximum_fusion.4), channel_id=1, source_target_pairs={{0,6},{1,25},{2,0},{3,27},{4,2},{5,29},{6,4},{7,31},{8,14},{9,1},{... | collective-permute-start | bytes 786440 | tf_op jit(solution)/shard_map/ppermute | solution.py:42
  87.1 2.2 %collective-permute-done.30 = bf16[4,8,16,256]{3,2,1,0:T(8,128)(2,1)} collective-permute-done((bf16[4,8,16,256]{3,2,1,0:T(8,128)(2,1)S(1)}, bf16[4,8,16,256]{3,2,1,0:T(8,128)(2,1)}, u32[]{:S(2)}, u32[]{:S(2)}) %collective-permute-start.30) | collective-permute-done | bytes 262176 | tf_op jit(solution)/shard_map/ppermute | solution.py:42
  89.3 2.8 %collective-permute-done.31 = bf16[4,8,16,256]{3,2,1,0:T(8,128)(2,1)} collective-permute-done((bf16[4,8,16,256]{3,2,1,0:T(8,128)(2,1)S(1)}, bf16[4,8,16,256]{3,2,1,0:T(8,128)(2,1)}, u32[]{:S(2)}, u32[]{:S(2)}) %collective-permute-start.31) | collective-permute-done | bytes 262176 | tf_op jit(solution)/shard_map/ppermute | solution.py:42
  93.6 2.8 %collective-permute-start.33 = (bf16[8,16,256]{2,1,0:T(8,128)(2,1)S(1)}, bf16[8,16,256]{2,1,0:T(8,128)(2,1)S(1)}, u32[]{:S(2)}, u32[]{:S(2)}) collective-permute-start(bf16[8,16,256]{2,1,0:T(8,128)(2,1)S(1)} %get-tuple-element.103), channel_id=1, source_target_pairs={{0,64},{1,65},{2,66},{3,67},{4,68},{5,69},{6,70},{7,71},{8,72},{9,... | collective-permute-start | bytes 196616 | tf_op jit(solution)/shard_map/ppermute | solution.py:42
  100.9 4.9 %collective-permute-start.36 = (bf16[4,8,16,128]{3,2,1,0:T(8,128)(2,1)S(1)}, bf16[4,8,16,128]{3,2,1,0:T(8,128)(2,1)S(1)}, u32[]{:S(2)}, u32[]{:S(2)}) collective-permute-start(bf16[4,8,16,128]{3,2,1,0:T(8,128)(2,1)S(1)} %get-tuple-element.99), channel_id=1, source_target_pairs={{0,1},{1,0},{2,3},{3,2},{4,5},{5,4},{6,7},{7,6},{8,9},{9,8},{10,11... | collective-permute-start | bytes 393224 | tf_op jit(solution)/shard_map/ppermute | solution.py:42
  107.6 15.3 %all_to_all.5.pieces = bf16[32,3,16,128]{3,2,1,0:T(8,128)(2,1)S(1)} all-to-all(bf16[32,3,16,128]{3,2,1,0:T(8,128)(2,1)S(1)} %bitcast.44), channel_id=1, replica_groups=mesh['grp'=4,'sub'=32] {'sub'}, dimensions={0} | all-to-all | bytes 786432 | tf_op jit(solution)/shard_map/all_to_all | solution.py:320
  (84 shorter events, 31.0 us)
Async XLA Ops:
  4.0 33.8 %collective-permute-start.1 = (bf16[16,256,512]{2,1,0:T(8,128)(2,1)}, bf16[16,256,512]{2,1,0:T(8,128)(2,1)}, u32[]{:S(2)}, u32[]{:S(2)}) collective-permute-start(bf16[16,256,512]{2,1,0:T(8,128)(2,1)} %own.1), channel_id=1, source_target_pairs={{0,1},{1,0},{2,3},{3,2},{4,5},{5,4},{6,7},{7,6},{8,9},{9,8},{10,11... | collective-permute-start | bytes 12582920 | tf_op jit(solution)/shard_map/ppermute | solution.py:42
  5.1 6.1 %collective-permute-start.3 = (bf16[2,128,256]{2,1,0:T(8,128)(2,1)S(1)}, bf16[2,128,256]{2,1,0:T(8,128)(2,1)S(1)}, u32[]{:S(2)}, u32[]{:S(2)}) collective-permute-start(bf16[2,128,256]{2,1,0:T(8,128)(2,1)S(1)} %maximum_select_fusion), channel_id=1, source_target_pairs={{0,8},{1,3},{2,10},{3,5},{4,12},{5,7},{6,14},{7,1},{8,16},{9,11},{... | collective-permute-start | bytes 393224 | tf_op jit(solution)/shard_map/ppermute | solution.py:42
  6.6 6.7 %collective-permute-start.4 = (bf16[2,128,256]{2,1,0:T(8,128)(2,1)S(1)}, bf16[2,128,256]{2,1,0:T(8,128)(2,1)S(1)}, u32[]{:S(2)}, u32[]{:S(2)}) collective-permute-start(bf16[2,128,256]{2,1,0:T(8,128)(2,1)S(1)} %maximum_select_fusion), channel_id=1, source_target_pairs={{0,16},{1,5},{2,18},{3,7},{4,20},{5,1},{6,22},{7,3},{8,24},{9,13},... | collective-permute-start | bytes 393224 | tf_op jit(solution)/shard_map/ppermute | solution.py:42
  9.2 4.1 %collective-permute-start.5 = (bf16[2,128,256]{2,1,0:T(8,128)(2,1)S(1)}, bf16[2,128,256]{2,1,0:T(8,128)(2,1)S(1)}, u32[]{:S(2)}, u32[]{:S(2)}) collective-permute-start(bf16[2,128,256]{2,1,0:T(8,128)(2,1)S(1)} %maximum_select_fusion), channel_id=1, source_target_pairs={{0,24},{1,7},{2,26},{3,1},{4,28},{5,3},{6,30},{7,5},{8,0},{9,15},{... | collective-permute-start | bytes 393224 | tf_op jit(solution)/shard_map/ppermute | solution.py:42
  13.4 10.5 %collective-permute-start.7 = (bf16[8,128,256]{2,1,0:T(8,128)(2,1)S(1)}, bf16[8,128,256]{2,1,0:T(8,128)(2,1)S(1)}, u32[]{:S(2)}, u32[]{:S(2)}) collective-permute-start(bf16[8,128,256]{2,1,0:T(8,128)(2,1)S(1)} %pad_maximum_fusion.set0), channel_id=1, source_target_pairs={{0,2},{1,9},{2,4},{3,11},{4,6},{5,13},{6,0},{7,15},{8,10},{9,17},{... | collective-permute-start | bytes 1572872 | tf_op jit(solution)/shard_map/ppermute | solution.py:42
  14.7 12.1 %collective-permute-start.8 = (bf16[8,128,256]{2,1,0:T(8,128)(2,1)S(1)}, bf16[8,128,256]{2,1,0:T(8,128)(2,1)S(1)}, u32[]{:S(2)}, u32[]{:S(2)}) collective-permute-start(bf16[8,128,256]{2,1,0:T(8,128)(2,1)S(1)} %pad_maximum_fusion.set0), channel_id=1, source_target_pairs={{0,6},{1,25},{2,0},{3,27},{4,2},{5,29},{6,4},{7,31},{8,14},{9,1},{... | collective-permute-start | bytes 1572872 | tf_op jit(solution)/shard_map/ppermute | solution.py:42
  16.1 13.5 %collective-permute-start.9 = (bf16[8,128,256]{2,1,0:T(8,128)(2,1)S(1)}, bf16[8,128,256]{2,1,0:T(8,128)(2,1)S(1)}, u32[]{:S(2)}, u32[]{:S(2)}) collective-permute-start(bf16[8,128,256]{2,1,0:T(8,128)(2,1)S(1)} %pad_maximum_fusion.set0), channel_id=1, source_target_pairs={{0,4},{1,17},{2,6},{3,19},{4,0},{5,21},{6,2},{7,23},{8,12},{9,25},... | collective-permute-start | bytes 1572872 | tf_op jit(solution)/shard_map/ppermute | solution.py:42
  22.3 8.4 %collective-permute-start.10 = (bf16[256,256]{1,0:T(8,128)(2,1)S(1)}, bf16[256,256]{1,0:T(8,128)(2,1)S(1)}, u32[]{:S(2)}, u32[]{:S(2)}) collective-permute-start(bf16[256,256]{1,0:T(8,128)(2,1)S(1)} %broadcast_multiply_fusion), channel_id=1, source_target_pairs={{0,32},{1,33},{2,34},{3,35},{4,36},{5,37},{6,38},{7,39},{8,40},{9,... | collective-permute-start | bytes 393224 | tf_op jit(solution)/shard_map/ppermute | solution.py:42
  23.9 6.8 %collective-permute-start.11 = (bf16[256,256]{1,0:T(8,128)(2,1)S(1)}, bf16[256,256]{1,0:T(8,128)(2,1)S(1)}, u32[]{:S(2)}, u32[]{:S(2)}) collective-permute-start(bf16[256,256]{1,0:T(8,128)(2,1)S(1)} %broadcast_multiply_fusion), channel_id=1, source_target_pairs={{0,96},{1,97},{2,98},{3,99},{4,100},{5,101},{6,102},{7,103},{8,104... | collective-permute-start | bytes 393224 | tf_op jit(solution)/shard_map/ppermute | solution.py:42
  26.7 5.6 %collective-permute-start.12 = (bf16[256,256]{1,0:T(8,128)(2,1)S(1)}, bf16[256,256]{1,0:T(8,128)(2,1)S(1)}, u32[]{:S(2)}, u32[]{:S(2)}) collective-permute-start(bf16[256,256]{1,0:T(8,128)(2,1)S(1)} %broadcast_multiply_fusion), channel_id=1, source_target_pairs={{0,64},{1,65},{2,66},{3,67},{4,68},{5,69},{6,70},{7,71},{8,72},{9,... | collective-permute-start | bytes 393224 | tf_op jit(solution)/shard_map/ppermute | solution.py:42
  32.4 7.7 %collective-permute-start.13 = (bf16[4,128,256]{2,1,0:T(8,128)(2,1)S(1)}, bf16[4,128,256]{2,1,0:T(8,128)(2,1)S(1)}, u32[]{:S(2)}, u32[]{:S(2)}) collective-permute-start(bf16[4,128,256]{2,1,0:T(8,128)(2,1)S(1)} %shard_map.75.refs_0_), channel_id=1, source_target_pairs={{0,1},{1,0},{2,3},{3,2},{4,5},{5,4},{6,7},{7,6},{8,9},{9,8},{10,11... | collective-permute-start | bytes 786440 | tf_op jit(solution)/shard_map/ppermute | solution.py:42
  35.7 7.9 %collective-permute-start.14 = (bf16[4,128,256]{2,1,0:T(8,128)(2,1)S(1)}, bf16[4,128,256]{2,1,0:T(8,128)(2,1)S(1)}, u32[]{:S(2)}, u32[]{:S(2)}) collective-permute-start(bf16[4,128,256]{2,1,0:T(8,128)(2,1)S(1)} %shard_map.75.refs_0_), channel_id=1, source_target_pairs={{0,96},{1,97},{2,98},{3,99},{4,100},{5,101},{6,102},{7,103},{8,104... | collective-permute-start | bytes 786440 | tf_op jit(solution)/shard_map/ppermute | solution.py:42
  37.0 8.8 %collective-permute-start.15 = (bf16[4,128,256]{2,1,0:T(8,128)(2,1)S(1)}, bf16[4,128,256]{2,1,0:T(8,128)(2,1)S(1)}, u32[]{:S(2)}, u32[]{:S(2)}) collective-permute-start(bf16[4,128,256]{2,1,0:T(8,128)(2,1)S(1)} %shard_map.75.refs_0_), channel_id=1, source_target_pairs={{0,32},{1,33},{2,34},{3,35},{4,36},{5,37},{6,38},{7,39},{8,40},{9,... | collective-permute-start | bytes 786440 | tf_op jit(solution)/shard_map/ppermute | solution.py:42
  37.2 16.6 %collective-permute-start.19 = (bf16[3,256,256]{2,1,0:T(8,128)(2,1)S(1)}, bf16[3,256,256]{2,1,0:T(8,128)(2,1)S(1)}, u32[]{:S(2)}, u32[]{:S(2)}) collective-permute-start(bf16[3,256,256]{2,1,0:T(8,128)(2,1)S(1)} %pad_maximum_fusion.1.own), channel_id=1, source_target_pairs={{0,1},{1,0},{2,3},{3,2},{4,5},{5,4},{6,7},{7,6},{8,9},{9,8},{10,11... | collective-permute-start | bytes 1179656 | tf_op jit(solution)/shard_map/ppermute | solution.py:42
  45.7 8.7 %collective-permute-start.20 = (bf16[4,128,256]{2,1,0:T(8,128)(2,1)S(1)}, bf16[4,128,256]{2,1,0:T(8,128)(2,1)S(1)}, u32[]{:S(2)}, u32[]{:S(2)}) collective-permute-start(bf16[4,128,256]{2,1,0:T(8,128)(2,1)S(1)} %collective-permute-done.15.refs_0_), channel_id=1, source_target_pairs={{0,1},{1,0},{2,3},{3,2},{4,5},{5,4},{6,7},{7,6},{8,9},{9,8},{10,11... | collective-permute-start | bytes 786440 | tf_op jit(solution)/shard_map/ppermute | solution.py:42
  46.9 10.1 %collective-permute-start.21 = (bf16[4,128,256]{2,1,0:T(8,128)(2,1)S(1)}, bf16[4,128,256]{2,1,0:T(8,128)(2,1)S(1)}, u32[]{:S(2)}, u32[]{:S(2)}) collective-permute-start(bf16[4,128,256]{2,1,0:T(8,128)(2,1)S(1)} %collective-permute-done.14.refs_2_), channel_id=1, source_target_pairs={{0,1},{1,0},{2,3},{3,2},{4,5},{5,4},{6,7},{7,6},{8,9},{9,8},{10,11... | collective-permute-start | bytes 786440 | tf_op jit(solution)/shard_map/ppermute | solution.py:42
  46.9 14.0 %collective-permute-start.22 = (bf16[4,128,256]{2,1,0:T(8,128)(2,1)S(1)}, bf16[4,128,256]{2,1,0:T(8,128)(2,1)S(1)}, u32[]{:S(2)}, u32[]{:S(2)}) collective-permute-start(bf16[4,128,256]{2,1,0:T(8,128)(2,1)S(1)} %shard_map.75.refs_0_), channel_id=1, source_target_pairs={{0,64},{1,65},{2,66},{3,67},{4,68},{5,69},{6,70},{7,71},{8,72},{9,... | collective-permute-start | bytes 786440 | tf_op jit(solution)/shard_map/ppermute | solution.py:42
  46.9 16.4 %collective-permute-start.16 = (bf16[1,8,64,256]{3,2,1,0:T(8,128)(2,1)S(1)}, bf16[1,8,64,256]{3,2,1,0:T(8,128)(2,1)S(1)}, u32[]{:S(2)}, u32[]{:S(2)}) collective-permute-start(bf16[1,8,64,256]{3,2,1,0:T(8,128)(2,1)S(1)} %get-tuple-element.64), channel_id=1, source_target_pairs={{0,16},{1,5},{2,18},{3,7},{4,20},{5,1},{6,22},{7,3},{8,24},{9,13},... | collective-permute-start | bytes 786440 | tf_op jit(solution)/shard_map/ppermute | solution.py:42
  53.8 11.5 %collective-permute-start.17 = (bf16[1,8,64,256]{3,2,1,0:T(8,128)(2,1)S(1)}, bf16[1,8,64,256]{3,2,1,0:T(8,128)(2,1)S(1)}, u32[]{:S(2)}, u32[]{:S(2)}) collective-permute-start(bf16[1,8,64,256]{3,2,1,0:T(8,128)(2,1)S(1)} %get-tuple-element.65), channel_id=1, source_target_pairs={{0,8},{1,3},{2,10},{3,5},{4,12},{5,7},{6,14},{7,1},{8,16},{9,11},{... | collective-permute-start | bytes 786440 | tf_op jit(solution)/shard_map/ppermute | solution.py:42
  54.5 10.8 %collective-permute-start.18 = (bf16[1,8,64,256]{3,2,1,0:T(8,128)(2,1)S(1)}, bf16[1,8,64,256]{3,2,1,0:T(8,128)(2,1)S(1)}, u32[]{:S(2)}, u32[]{:S(2)}) collective-permute-start(bf16[1,8,64,256]{3,2,1,0:T(8,128)(2,1)S(1)} %get-tuple-element.66), channel_id=1, source_target_pairs={{0,24},{1,7},{2,26},{3,1},{4,28},{5,3},{6,30},{7,5},{8,0},{9,15},{... | collective-permute-start | bytes 786440 | tf_op jit(solution)/shard_map/ppermute | solution.py:42
  61.0 12.6 %collective-permute-start.23 = (bf16[2,8,64,256]{3,2,1,0:T(8,128)(2,1)S(1)}, bf16[2,8,64,256]{3,2,1,0:T(8,128)(2,1)S(1)}, u32[]{:S(2)}, u32[]{:S(2)}) collective-permute-start(bf16[2,8,64,256]{3,2,1,0:T(8,128)(2,1)S(1)} %get-tuple-element.81), channel_id=1, source_target_pairs={{0,16},{1,5},{2,18},{3,7},{4,20},{5,1},{6,22},{7,3},{8,24},{9,13},... | collective-permute-start | bytes 1572872 | tf_op jit(solution)/shard_map/ppermute | solution.py:42
  62.6 13.9 %collective-permute-start.24 = (bf16[2,8,64,256]{3,2,1,0:T(8,128)(2,1)S(1)}, bf16[2,8,64,256]{3,2,1,0:T(8,128)(2,1)S(1)}, u32[]{:S(2)}, u32[]{:S(2)}) collective-permute-start(bf16[2,8,64,256]{3,2,1,0:T(8,128)(2,1)S(1)} %get-tuple-element.82), channel_id=1, source_target_pairs={{0,8},{1,3},{2,10},{3,5},{4,12},{5,7},{6,14},{7,1},{8,16},{9,11},{... | collective-permute-start | bytes 1572872 | tf_op jit(solution)/shard_map/ppermute | solution.py:42
  63.3 13.2 %collective-permute-start.25 = (bf16[2,8,64,256]{3,2,1,0:T(8,128)(2,1)S(1)}, bf16[2,8,64,256]{3,2,1,0:T(8,128)(2,1)S(1)}, u32[]{:S(2)}, u32[]{:S(2)}) collective-permute-start(bf16[2,8,64,256]{3,2,1,0:T(8,128)(2,1)S(1)} %get-tuple-element.83), channel_id=1, source_target_pairs={{0,24},{1,7},{2,26},{3,1},{4,28},{5,3},{6,30},{7,5},{8,0},{9,15},{... | collective-permute-start | bytes 1572872 | tf_op jit(solution)/shard_map/ppermute | solution.py:42
  68.9 10.3 %collective-permute-start.27 = (bf16[1,8,64,256]{3,2,1,0:T(8,128)(2,1)S(1)}, bf16[1,8,64,256]{3,2,1,0:T(8,128)(2,1)S(1)}, u32[]{:S(2)}, u32[]{:S(2)}) collective-permute-start(bf16[1,8,64,256]{3,2,1,0:T(8,128)(2,1)S(1)} %get-tuple-element.86), channel_id=1, source_target_pairs={{0,16},{1,5},{2,18},{3,7},{4,20},{5,1},{6,22},{7,3},{8,24},{9,13},... | collective-permute-start | bytes 786440 | tf_op jit(solution)/shard_map/ppermute | solution.py:42
  72.8 9.0 %collective-permute-start.28 = (bf16[1,8,64,256]{3,2,1,0:T(8,128)(2,1)S(1)}, bf16[1,8,64,256]{3,2,1,0:T(8,128)(2,1)S(1)}, u32[]{:S(2)}, u32[]{:S(2)}) collective-permute-start(bf16[1,8,64,256]{3,2,1,0:T(8,128)(2,1)S(1)} %get-tuple-element.87), channel_id=1, source_target_pairs={{0,8},{1,3},{2,10},{3,5},{4,12},{5,7},{6,14},{7,1},{8,16},{9,11},{... | collective-permute-start | bytes 786440 | tf_op jit(solution)/shard_map/ppermute | solution.py:42
  73.5 8.3 %collective-permute-start.29 = (bf16[1,8,64,256]{3,2,1,0:T(8,128)(2,1)S(1)}, bf16[1,8,64,256]{3,2,1,0:T(8,128)(2,1)S(1)}, u32[]{:S(2)}, u32[]{:S(2)}) collective-permute-start(bf16[1,8,64,256]{3,2,1,0:T(8,128)(2,1)S(1)} %get-tuple-element.88), channel_id=1, source_target_pairs={{0,24},{1,7},{2,26},{3,1},{4,28},{5,3},{6,30},{7,5},{8,0},{9,15},{... | collective-permute-start | bytes 786440 | tf_op jit(solution)/shard_map/ppermute | solution.py:42
  82.1 7.2 %collective-permute-start.30 = (bf16[4,8,16,256]{3,2,1,0:T(8,128)(2,1)S(1)}, bf16[4,8,16,256]{3,2,1,0:T(8,128)(2,1)}, u32[]{:S(2)}, u32[]{:S(2)}) collective-permute-start(bf16[4,8,16,256]{3,2,1,0:T(8,128)(2,1)S(1)} %pad_maximum_fusion.2), channel_id=1, source_target_pairs={{0,4},{1,17},{2,6},{3,19},{4,0},{5,21},{6,2},{7,23},{8,12},{9,25},... | collective-permute-start | bytes 786440 | tf_op jit(solution)/shard_map/ppermute | solution.py:42
  84.2 7.9 %collective-permute-start.31 = (bf16[4,8,16,256]{3,2,1,0:T(8,128)(2,1)S(1)}, bf16[4,8,16,256]{3,2,1,0:T(8,128)(2,1)}, u32[]{:S(2)}, u32[]{:S(2)}) collective-permute-start(bf16[4,8,16,256]{3,2,1,0:T(8,128)(2,1)S(1)} %pad_maximum_fusion.3), channel_id=1, source_target_pairs={{0,2},{1,9},{2,4},{3,11},{4,6},{5,13},{6,0},{7,15},{8,10},{9,17},{... | collective-permute-start | bytes 786440 | tf_op jit(solution)/shard_map/ppermute | solution.py:42
  85.4 6.8 %collective-permute-start.32 = (bf16[4,8,16,256]{3,2,1,0:T(8,128)(2,1)S(1)}, bf16[4,8,16,256]{3,2,1,0:T(8,128)(2,1)}, u32[]{:S(2)}, u32[]{:S(2)}) collective-permute-start(bf16[4,8,16,256]{3,2,1,0:T(8,128)(2,1)S(1)} %pad_maximum_fusion.4), channel_id=1, source_target_pairs={{0,6},{1,25},{2,0},{3,27},{4,2},{5,29},{6,4},{7,31},{8,14},{9,1},{... | collective-permute-start | bytes 786440 | tf_op jit(solution)/shard_map/ppermute | solution.py:42
  93.6 4.7 %collective-permute-start.33 = (bf16[8,16,256]{2,1,0:T(8,128)(2,1)S(1)}, bf16[8,16,256]{2,1,0:T(8,128)(2,1)S(1)}, u32[]{:S(2)}, u32[]{:S(2)}) collective-permute-start(bf16[8,16,256]{2,1,0:T(8,128)(2,1)S(1)} %get-tuple-element.103), channel_id=1, source_target_pairs={{0,64},{1,65},{2,66},{3,67},{4,68},{5,69},{6,70},{7,71},{8,72},{9,... | collective-permute-start | bytes 196616 | tf_op jit(solution)/shard_map/ppermute | solution.py:42
  96.5 4.3 %collective-permute-start.35 = (bf16[8,16,256]{2,1,0:T(8,128)(2,1)S(1)}, bf16[8,16,256]{2,1,0:T(8,128)(2,1)S(1)}, u32[]{:S(2)}, u32[]{:S(2)}) collective-permute-start(bf16[8,16,256]{2,1,0:T(8,128)(2,1)S(1)} %get-tuple-element.101), channel_id=1, source_target_pairs={{0,32},{1,33},{2,34},{3,35},{4,36},{5,37},{6,38},{7,39},{8,40},{9,... | collective-permute-start | bytes 196616 | tf_op jit(solution)/shard_map/ppermute | solution.py:42
  100.9 5.9 %collective-permute-start.36 = (bf16[4,8,16,128]{3,2,1,0:T(8,128)(2,1)S(1)}, bf16[4,8,16,128]{3,2,1,0:T(8,128)(2,1)S(1)}, u32[]{:S(2)}, u32[]{:S(2)}) collective-permute-start(bf16[4,8,16,128]{3,2,1,0:T(8,128)(2,1)S(1)} %get-tuple-element.99), channel_id=1, source_target_pairs={{0,1},{1,0},{2,3},{3,2},{4,5},{5,4},{6,7},{7,6},{8,9},{9,8},{10,11... | collective-permute-start | bytes 393224 | tf_op jit(solution)/shard_map/ppermute | solution.py:42
  (6 other events, 32.7 us)

commit v6 on v5

--- a/solution.py
+++ b/solution.py
@@ -291,13 +291,17 @@
     def strip(e):
         return jnp.concatenate([t[:, :, e * 16 : (e + 1) * 16] for t in sums])
 
-    total = strip(0)
-    for e in (2, 1, 3):
-        total = total + move(strip(e).astype(BF), SECOND[e]).astype(F32)
-    total = total.astype(BF)
+    parts = [t[n] for t in sums for n in range(t.shape[0])]
+    arrived = [move(strip(e).astype(BF), SECOND[e]) for e in (2, 1, 3)]
+
+    def total(group):
+        added = parts[group][:, 0:16]
+        for part in arrived:
+            added = added + part[group].astype(F32)
+        return added.astype(BF)
 
     rows = jnp.stack(
-        [total[0]] + [move(total[at], DEPTH[4 - r]) for at, r in ((3, 2), (1, 1), (2, 3))]
+        [total(0)] + [move(total(at), DEPTH[4 - r]) for at, r in ((3, 2), (1, 1), (2, 3))]
     )
     mine = lax.dynamic_slice_in_dim(rows, c * 128, 128, 3)
     other = move(lax.dynamic_slice_in_dim(rows, (1 - c) * 128, 128, 3), CORE)

time: 124 us -> 127 us (1.024)
  starting transfers between devices: 60.2 us -> 55.3 us
  local copies, waits for them, and re-layouts: 0.45 us -> 4.7 us
  Pallas kernels: 14 us -> 15.5 us
  other arithmetic: 5.21 us -> 6.65 us
  waiting for transfers between devices: 27.1 us -> 28.5 us
    ppermute x37, starting transfers between devices: 60.2 us -> 55.3 us  [move(): return lax.ppermute(value, AXES, permutation)]
    unnamed x2 -> x14, local copies, waits for them, and re-layouts: 0.01 us -> 4.23 us
    pallas_call x3, Pallas kernels: 7.96 us -> 9.42 us  [products_of(): pl.pallas_call(products_body, grid_spec=pltpu.PrefetchScalarGridSpec(num_...]
    squeeze x0 -> x2, other arithmetic: none -> 1.44 us  [per_device(): parts = [t[n] for t in sums for n in range(t.shape[0])]]
    ppermute x37, waiting for transfers between devices: 27.1 us -> 28.5 us  [move(): return lax.ppermute(value, AXES, permutation)]
  transfers between devices with their start and end apart: 37 -> 37, of which waited for: 20 -> 17; matrix products, arithmetic and copies ran while one was open for 2% -> 4% of each run, Pallas kernels for 10% -> 11%
where the time goes in v6:
time: 127 us; the launch traced here: 126 us
  starting transfers between devices  55.3 us (44%)
  waiting for transfers between devices  28.5 us (22%)
  Pallas kernels  15.5 us (12%)
  blocking collectives  14.2 us (11%)
  other arithmetic  6.65 us (5%)
  local copies, waits for them, and re-layouts  4.7 us (4%)
  between operations  1.63 us (1%)
    ppermute x37, starting transfers between devices, move(): return lax.ppermute(value, AXES, permutation)  55.3 us
    ppermute x37, waiting for transfers between devices, move(): return lax.ppermute(value, AXES, permutation)  28.5 us
    all_to_all x1, blocking collectives, per_device(): lax.all_to_all(outgoing.reshape(32, CAP, 16, 128), 'sub', split_axis=0, c...  14.2 us
    pallas_call x3, Pallas kernels, products_of(): pl.pallas_call(products_body, grid_spec=pltpu.PrefetchScalarGridSpec(num_...  9.42 us
    unnamed x14, local copies, waits for them, and re-layouts  4.23 us
  transfers between devices with their start and end apart: 37, of which 17 were waited for; matrix products, arithmetic and copies ran while one was open for 4% of the time, Pallas kernels for 11%

profile of v6, /device:TPU:1, one launch (start us, length us, event | category | flops | bytes accessed | tf_op | source)
XLA Modules:
  0.0 126.4 jit_solution(9081605500411636755)
XLA Ops:
  1.6 1.5 %collective-permute-start = (bf16[128,256]{1,0:T(8,128)(2,1)S(1)}, bf16[128,256]{1,0:T(8,128)(2,1)S(1)}, u32[]{:S(2)}, u32[]{:S(2)}) collective-permute-start(bf16[128,256]{1,0:T(8,128)(2,1)S(1)} %get-tuple-element.113), channel_id=1, source_target_pairs={{0,1},{1,0},{2,3},{3,2},{4,5},{5,4},{6,7},{7,6},{8,9},{9,8},{10,11... | collective-permute-start | bytes 196616 | tf_op jit(solution)/shard_map/ppermute | solution.py:42
  5.1 2.9 %collective-permute-start.5 = (bf16[2,128,256]{2,1,0:T(8,128)(2,1)S(1)}, bf16[2,128,256]{2,1,0:T(8,128)(2,1)S(1)}, u32[]{:S(2)}, u32[]{:S(2)}) collective-permute-start(bf16[2,128,256]{2,1,0:T(8,128)(2,1)S(1)} %maximum_select_fusion), channel_id=1, source_target_pairs={{0,24},{1,7},{2,26},{3,1},{4,28},{5,3},{6,30},{7,5},{8,0},{9,15},{... | collective-permute-start | bytes 393224 | tf_op jit(solution)/shard_map/ppermute | solution.py:42
  10.0 1.4 %collective-permute-done.5 = bf16[2,128,256]{2,1,0:T(8,128)(2,1)S(1)} collective-permute-done((bf16[2,128,256]{2,1,0:T(8,128)(2,1)S(1)}, bf16[2,128,256]{2,1,0:T(8,128)(2,1)S(1)}, u32[]{:S(2)}, u32[]{:S(2)}) %collective-permute-start.5) | collective-permute-done | bytes 131104 | tf_op jit(solution)/shard_map/ppermute | solution.py:42
  11.3 2.3 %collective-permute-done.4 = bf16[2,128,256]{2,1,0:T(8,128)(2,1)S(1)} collective-permute-done((bf16[2,128,256]{2,1,0:T(8,128)(2,1)S(1)}, bf16[2,128,256]{2,1,0:T(8,128)(2,1)S(1)}, u32[]{:S(2)}, u32[]{:S(2)}) %collective-permute-start.4) | collective-permute-done | bytes 131104 | tf_op jit(solution)/shard_map/ppermute | solution.py:42
  13.6 1.4 %collective-permute-done.3 = bf16[2,128,256]{2,1,0:T(8,128)(2,1)S(1)} collective-permute-done((bf16[2,128,256]{2,1,0:T(8,128)(2,1)S(1)}, bf16[2,128,256]{2,1,0:T(8,128)(2,1)S(1)}, u32[]{:S(2)}, u32[]{:S(2)}) %collective-permute-start.3) | collective-permute-done | bytes 131104 | tf_op jit(solution)/shard_map/ppermute | solution.py:42
  16.1 1.8 %collective-permute-start.8 = (bf16[8,128,256]{2,1,0:T(8,128)(2,1)S(1)}, bf16[8,128,256]{2,1,0:T(8,128)(2,1)S(1)}, u32[]{:S(2)}, u32[]{:S(2)}) collective-permute-start(bf16[8,128,256]{2,1,0:T(8,128)(2,1)S(1)} %pad_maximum_fusion.set0), channel_id=1, source_target_pairs={{0,6},{1,25},{2,0},{3,27},{4,2},{5,29},{6,4},{7,31},{8,14},{9,1},{... | collective-permute-start | bytes 1572872 | tf_op jit(solution)/shard_map/ppermute | solution.py:42
  19.1 2.3 %collective-permute-start.2 = (s32[1,2]{1,0:T(1,128)}, s32[1,2]{1,0:T(1,128)S(1)}, u32[]{:S(2)}, u32[]{:S(2)}) collective-permute-start(s32[1,2]{1,0:T(1,128)} %param.8), channel_id=1, source_target_pairs={{0,1},{1,0},{2,3},{3,2},{4,5},{5,4},{6,7},{7,6},{8,9},{9,8},{10,11... | collective-permute-start | bytes 32 | tf_op jit(solution)/shard_map/ppermute | solution.py:42
  23.7 1.6 %collective-permute-start.10 = (bf16[256,256]{1,0:T(8,128)(2,1)S(1)}, bf16[256,256]{1,0:T(8,128)(2,1)S(1)}, u32[]{:S(2)}, u32[]{:S(2)}) collective-permute-start(bf16[256,256]{1,0:T(8,128)(2,1)S(1)} %broadcast_multiply_fusion), channel_id=1, source_target_pairs={{0,32},{1,33},{2,34},{3,35},{4,36},{5,37},{6,38},{7,39},{8,40},{9,... | collective-permute-start | bytes 393224 | tf_op jit(solution)/shard_map/ppermute | solution.py:42
  25.4 3.1 %collective-permute-start.11 = (bf16[256,256]{1,0:T(8,128)(2,1)S(1)}, bf16[256,256]{1,0:T(8,128)(2,1)S(1)}, u32[]{:S(2)}, u32[]{:S(2)}) collective-permute-start(bf16[256,256]{1,0:T(8,128)(2,1)S(1)} %broadcast_multiply_fusion), channel_id=1, source_target_pairs={{0,96},{1,97},{2,98},{3,99},{4,100},{5,101},{6,102},{7,103},{8,104... | collective-permute-start | bytes 393224 | tf_op jit(solution)/shard_map/ppermute | solution.py:42
  29.6 3.6 %collective-permute-start.12 = (bf16[256,256]{1,0:T(8,128)(2,1)S(1)}, bf16[256,256]{1,0:T(8,128)(2,1)S(1)}, u32[]{:S(2)}, u32[]{:S(2)}) collective-permute-start(bf16[256,256]{1,0:T(8,128)(2,1)S(1)} %broadcast_multiply_fusion), channel_id=1, source_target_pairs={{0,64},{1,65},{2,66},{3,67},{4,68},{5,69},{6,70},{7,71},{8,72},{9,... | collective-permute-start | bytes 393224 | tf_op jit(solution)/shard_map/ppermute | solution.py:42
  39.8 2.2 %shard_map.73 = (bf16[8,256,512]{2,1,0:T(8,128)(2,1)S(1)}, bf16[8,256,512]{2,1,0:T(8,128)(2,1)S(1)}) custom-call(s32[1]{0:T(128)} %bitcast.1.sc, bf16[16,256,512]{2,1,0:T(8,128)(2,1)} %own.1, bf16[16,256,512]{2,1,0:T(8,128)(2,1)} %collective-permute-done.1.oth), custom_call_target="tpu_custom_call" | custom-call | bytes 1000 | tf_op jit(solution)/shard_map/pallas_call | solution.py:127
  42.1 2.7 %shard_map.76 = (bf16[1,8,64,256]{3,2,1,0:T(8,128)(2,1)}, bf16[1,8,64,256]{3,2,1,0:T(8,128)(2,1)S(1)}, bf16[1,8,64,256]{3,2,1,0:T(8,128)(2,1)}, f32[1,8,64,256]{3,2,1,0:T(8,128)S(1)}) custom-call(s32[1]{0:T(128)} %bitcast.1.sc, bf16[8,256,512]{2,1,0:T(8,128)(2,1)S(1)} %get-tuple-element.48.t_own, bf16[8,256,512]{2,1,0:T(8,128)(2,1)S(1)} %get-tuple-element.49.t_oth, ...), custom_call_target="tpu_custom_call" | custom-call | flops 1000 | bytes 1000 | tf_op jit(solution)/shard_map/pallas_call | solution.py:174
  46.9 1.7 %collective-permute-start.20 = (bf16[4,128,256]{2,1,0:T(8,128)(2,1)S(1)}, bf16[4,128,256]{2,1,0:T(8,128)(2,1)S(1)}, u32[]{:S(2)}, u32[]{:S(2)}) collective-permute-start(bf16[4,128,256]{2,1,0:T(8,128)(2,1)S(1)} %collective-permute-done.15.refs_0_), channel_id=1, source_target_pairs={{0,1},{1,0},{2,3},{3,2},{4,5},{5,4},{6,7},{7,6},{8,9},{9,8},{10,11... | collective-permute-start | bytes 786440 | tf_op jit(solution)/shard_map/ppermute | solution.py:42
  48.6 6.6 %collective-permute-start.16 = (bf16[1,8,64,256]{3,2,1,0:T(8,128)(2,1)S(1)}, bf16[1,8,64,256]{3,2,1,0:T(8,128)(2,1)}, u32[]{:S(2)}, u32[]{:S(2)}) collective-permute-start(bf16[1,8,64,256]{3,2,1,0:T(8,128)(2,1)S(1)} %get-tuple-element.64), channel_id=1, source_target_pairs={{0,16},{1,5},{2,18},{3,7},{4,20},{5,1},{6,22},{7,3},{8,24},{9,13},... | collective-permute-start | bytes 786440 | tf_op jit(solution)/shard_map/ppermute | solution.py:42
  55.9 2.0 %collective-permute-start.18 = (bf16[1,8,64,256]{3,2,1,0:T(8,128)(2,1)}, bf16[1,8,64,256]{3,2,1,0:T(8,128)(2,1)}, u32[]{:S(2)}, u32[]{:S(2)}) collective-permute-start(bf16[1,8,64,256]{3,2,1,0:T(8,128)(2,1)} %get-tuple-element.66), channel_id=1, source_target_pairs={{0,24},{1,7},{2,26},{3,1},{4,28},{5,3},{6,30},{7,5},{8,0},{9,15},{... | collective-permute-start | bytes 786440 | tf_op jit(solution)/shard_map/ppermute | solution.py:42
  58.5 4.7 %shard_map.78 = (bf16[2,8,64,256]{3,2,1,0:T(8,128)(2,1)}, bf16[2,8,64,256]{3,2,1,0:T(8,128)(2,1)}, bf16[2,8,64,256]{3,2,1,0:T(8,128)(2,1)}, f32[2,8,64,256]{3,2,1,0:T(8,128)S(1)}) custom-call(s32[1]{0:T(128)} %bitcast.1.sc, bf16[8,256,512]{2,1,0:T(8,128)(2,1)S(1)} %get-tuple-element.48.t_own, bf16[8,256,512]{2,1,0:T(8,128)(2,1)S(1)} %get-tuple-element.49.t_oth, ...), custom_call_target="tpu_custom_call" | custom-call | flops 1000 | bytes 1000 | tf_op jit(solution)/shard_map/pallas_call | solution.py:174
  64.9 1.4 %collective-permute-start.24 = (bf16[2,8,64,256]{3,2,1,0:T(8,128)(2,1)}, bf16[2,8,64,256]{3,2,1,0:T(8,128)(2,1)}, u32[]{:S(2)}, u32[]{:S(2)}) collective-permute-start(bf16[2,8,64,256]{3,2,1,0:T(8,128)(2,1)} %get-tuple-element.82), channel_id=1, source_target_pairs={{0,8},{1,3},{2,10},{3,5},{4,12},{5,7},{6,14},{7,1},{8,16},{9,11},{... | collective-permute-start | bytes 1572872 | tf_op jit(solution)/shard_map/ppermute | solution.py:42
  68.4 1.6 %copy-done.1 = bf16[8,256,512]{2,1,0:T(8,128)(2,1)S(1)} copy-done((bf16[8,256,512]{2,1,0:T(8,128)(2,1)S(1)}, bf16[8,256,512]{2,1,0:T(8,128)(2,1)}, u32[]{:S(2)}) %copy-start.1) | copy-done | bytes 2097176
  70.9 2.0 %shard_map.79 = (bf16[1,8,64,256]{3,2,1,0:T(8,128)(2,1)S(1)}, bf16[1,8,64,256]{3,2,1,0:T(8,128)(2,1)S(1)}, bf16[1,8,64,256]{3,2,1,0:T(8,128)(2,1)S(1)}, f32[1,8,64,256]{3,2,1,0:T(8,128)S(1)}) custom-call(s32[1]{0:T(128)} %bitcast.1.sc, bf16[8,256,512]{2,1,0:T(8,128)(2,1)S(1)} %get-tuple-element.48.t_own, bf16[8,256,512]{2,1,0:T(8,128)(2,1)S(1)} %copy-done.1, ...), custom_call_target="tpu_custom_call" | custom-call | flops 1000 | bytes 1000 | tf_op jit(solution)/shard_map/pallas_call | solution.py:174
  73.0 3.8 %collective-permute-start.29 = (bf16[1,8,64,256]{3,2,1,0:T(8,128)(2,1)S(1)}, bf16[1,8,64,256]{3,2,1,0:T(8,128)(2,1)S(1)}, u32[]{:S(2)}, u32[]{:S(2)}) collective-permute-start(bf16[1,8,64,256]{3,2,1,0:T(8,128)(2,1)S(1)} %get-tuple-element.88), channel_id=1, source_target_pairs={{0,24},{1,7},{2,26},{3,1},{4,28},{5,3},{6,30},{7,5},{8,0},{9,15},{... | collective-permute-start | bytes 786440 | tf_op jit(solution)/shard_map/ppermute | solution.py:42
  76.7 1.4 %collective-permute-start.27 = (bf16[1,8,64,256]{3,2,1,0:T(8,128)(2,1)S(1)}, bf16[1,8,64,256]{3,2,1,0:T(8,128)(2,1)S(1)}, u32[]{:S(2)}, u32[]{:S(2)}) collective-permute-start(bf16[1,8,64,256]{3,2,1,0:T(8,128)(2,1)S(1)} %get-tuple-element.86), channel_id=1, source_target_pairs={{0,16},{1,5},{2,18},{3,7},{4,20},{5,1},{6,22},{7,3},{8,24},{9,13},... | collective-permute-start | bytes 786440 | tf_op jit(solution)/shard_map/ppermute | solution.py:42
  78.1 2.2 %collective-permute-done.24 = bf16[2,8,64,256]{3,2,1,0:T(8,128)(2,1)} collective-permute-done((bf16[2,8,64,256]{3,2,1,0:T(8,128)(2,1)}, bf16[2,8,64,256]{3,2,1,0:T(8,128)(2,1)}, u32[]{:S(2)}, u32[]{:S(2)}) %collective-permute-start.24) | collective-permute-done | bytes 524320 | tf_op jit(solution)/shard_map/ppermute | solution.py:42
  80.3 1.7 %fusion.26 = (bf16[2,8,64,256]{3,2,1,0:T(8,128)(2,1)S(1)}, f32[2,8,64,256]{3,2,1,0:T(8,128)S(1)}) fusion(bf16[2,8,64,256]{3,2,1,0:T(8,128)(2,1)} %collective-permute-done.25, bf16[2,8,64,256]{3,2,1,0:T(8,128)(2,1)} %collective-permute-done.24, f32[2,8,64,256]{3,2,1,0:T(8,128)S(1)} %copy-done.3, bf16[2,8,64,256]{3,2,1,0:T(8,128)(2,1)} %collective-permute-done.23), kind=kLoop, calls=%fused_computation.88 | loop fusion | flops 1835008 | bytes 4194304 | tf_op jit(solution)/shard_map/convert.28
  82.1 3.9 %collective-permute-done.28 = bf16[1,8,64,256]{3,2,1,0:T(8,128)(2,1)S(1)} collective-permute-done((bf16[1,8,64,256]{3,2,1,0:T(8,128)(2,1)S(1)}, bf16[1,8,64,256]{3,2,1,0:T(8,128)(2,1)S(1)}, u32[]{:S(2)}, u32[]{:S(2)}) %collective-permute-start.28) | collective-permute-done | bytes 262176 | tf_op jit(solution)/shard_map/ppermute | solution.py:42
  87.9 1.8 %collective-permute-start.30 = (bf16[4,8,16,256]{3,2,1,0:T(8,128)(2,1)S(1)}, bf16[4,8,16,256]{3,2,1,0:T(8,128)(2,1)S(1)}, u32[]{:S(2)}, u32[]{:S(2)}) collective-permute-start(bf16[4,8,16,256]{3,2,1,0:T(8,128)(2,1)S(1)} %pad_maximum_fusion.2), channel_id=1, source_target_pairs={{0,4},{1,17},{2,6},{3,19},{4,0},{5,21},{6,2},{7,23},{8,12},{9,25},... | collective-permute-start | bytes 786440 | tf_op jit(solution)/shard_map/ppermute | solution.py:42
  89.8 1.7 %collective-permute-done.32 = bf16[4,8,16,256]{3,2,1,0:T(8,128)(2,1)S(1)} collective-permute-done((bf16[4,8,16,256]{3,2,1,0:T(8,128)(2,1)S(1)}, bf16[4,8,16,256]{3,2,1,0:T(8,128)(2,1)S(1)}, u32[]{:S(2)}, u32[]{:S(2)}) %collective-permute-start.32) | collective-permute-done | bytes 262176 | tf_op jit(solution)/shard_map/ppermute | solution.py:42
  91.5 5.3 %collective-permute-done.31 = bf16[4,8,16,256]{3,2,1,0:T(8,128)(2,1)S(1)} collective-permute-done((bf16[4,8,16,256]{3,2,1,0:T(8,128)(2,1)S(1)}, bf16[4,8,16,256]{3,2,1,0:T(8,128)(2,1)S(1)}, u32[]{:S(2)}, u32[]{:S(2)}) %collective-permute-start.31) | collective-permute-done | bytes 262176 | tf_op jit(solution)/shard_map/ppermute | solution.py:42
  97.9 1.8 %collective-permute-start.34 = (bf16[8,16,256]{2,1,0:T(8,128)(2,1)S(1)}, bf16[8,16,256]{2,1,0:T(8,128)(2,1)S(1)}, u32[]{:S(2)}, u32[]{:S(2)}) collective-permute-start(bf16[8,16,256]{2,1,0:T(8,128)(2,1)S(1)} %get-tuple-element.99), channel_id=1, source_target_pairs={{0,96},{1,97},{2,98},{3,99},{4,100},{5,101},{6,102},{7,103},{8,104... | collective-permute-start | bytes 196616 | tf_op jit(solution)/shard_map/ppermute | solution.py:42
  99.7 2.0 %collective-permute-start.33 = (bf16[8,16,256]{2,1,0:T(8,128)(2,1)S(1)}, bf16[8,16,256]{2,1,0:T(8,128)(2,1)S(1)}, u32[]{:S(2)}, u32[]{:S(2)}) collective-permute-start(bf16[8,16,256]{2,1,0:T(8,128)(2,1)S(1)} %get-tuple-element.100), channel_id=1, source_target_pairs={{0,64},{1,65},{2,66},{3,67},{4,68},{5,69},{6,70},{7,71},{8,72},{9,... | collective-permute-start | bytes 196616 | tf_op jit(solution)/shard_map/ppermute | solution.py:42
  101.9 2.4 %collective-permute-done.33 = bf16[8,16,256]{2,1,0:T(8,128)(2,1)S(1)} collective-permute-done((bf16[8,16,256]{2,1,0:T(8,128)(2,1)S(1)}, bf16[8,16,256]{2,1,0:T(8,128)(2,1)S(1)}, u32[]{:S(2)}, u32[]{:S(2)}) %collective-permute-start.33) | collective-permute-done | bytes 65568 | tf_op jit(solution)/shard_map/ppermute | solution.py:42
  104.4 5.1 %collective-permute-start.36 = (bf16[4,8,16,128]{3,2,1,0:T(8,128)(2,1)S(1)}, bf16[4,8,16,128]{3,2,1,0:T(8,128)(2,1)S(1)}, u32[]{:S(2)}, u32[]{:S(2)}) collective-permute-start(bf16[4,8,16,128]{3,2,1,0:T(8,128)(2,1)S(1)} %get-tuple-element.105), channel_id=1, source_target_pairs={{0,1},{1,0},{2,3},{3,2},{4,5},{5,4},{6,7},{7,6},{8,9},{9,8},{10,11... | collective-permute-start | bytes 393224 | tf_op jit(solution)/shard_map/ppermute | solution.py:42
  111.3 14.2 %all_to_all.5.pieces = bf16[32,3,16,128]{3,2,1,0:T(8,128)(2,1)S(1)} all-to-all(bf16[32,3,16,128]{3,2,1,0:T(8,128)(2,1)S(1)} %bitcast.108), channel_id=1, replica_groups=mesh['grp'=4,'sub'=32] {'sub'}, dimensions={0} | all-to-all | bytes 786432 | tf_op jit(solution)/shard_map/all_to_all | solution.py:324
  (93 shorter events, 30.7 us)
Async XLA Ops:
  4.0 35.8 %collective-permute-start.1 = (bf16[16,256,512]{2,1,0:T(8,128)(2,1)}, bf16[16,256,512]{2,1,0:T(8,128)(2,1)}, u32[]{:S(2)}, u32[]{:S(2)}) collective-permute-start(bf16[16,256,512]{2,1,0:T(8,128)(2,1)} %own.1), channel_id=1, source_target_pairs={{0,1},{1,0},{2,3},{3,2},{4,5},{5,4},{6,7},{7,6},{8,9},{9,8},{10,11... | collective-permute-start | bytes 12582920 | tf_op jit(solution)/shard_map/ppermute | solution.py:42
  5.1 6.2 %collective-permute-start.5 = (bf16[2,128,256]{2,1,0:T(8,128)(2,1)S(1)}, bf16[2,128,256]{2,1,0:T(8,128)(2,1)S(1)}, u32[]{:S(2)}, u32[]{:S(2)}) collective-permute-start(bf16[2,128,256]{2,1,0:T(8,128)(2,1)S(1)} %maximum_select_fusion), channel_id=1, source_target_pairs={{0,24},{1,7},{2,26},{3,1},{4,28},{5,3},{6,30},{7,5},{8,0},{9,15},{... | collective-permute-start | bytes 393224 | tf_op jit(solution)/shard_map/ppermute | solution.py:42
  8.0 5.6 %collective-permute-start.4 = (bf16[2,128,256]{2,1,0:T(8,128)(2,1)S(1)}, bf16[2,128,256]{2,1,0:T(8,128)(2,1)S(1)}, u32[]{:S(2)}, u32[]{:S(2)}) collective-permute-start(bf16[2,128,256]{2,1,0:T(8,128)(2,1)S(1)} %maximum_select_fusion), channel_id=1, source_target_pairs={{0,16},{1,5},{2,18},{3,7},{4,20},{5,1},{6,22},{7,3},{8,24},{9,13},... | collective-permute-start | bytes 393224 | tf_op jit(solution)/shard_map/ppermute | solution.py:42
  8.4 6.7 %collective-permute-start.3 = (bf16[2,128,256]{2,1,0:T(8,128)(2,1)S(1)}, bf16[2,128,256]{2,1,0:T(8,128)(2,1)S(1)}, u32[]{:S(2)}, u32[]{:S(2)}) collective-permute-start(bf16[2,128,256]{2,1,0:T(8,128)(2,1)S(1)} %maximum_select_fusion), channel_id=1, source_target_pairs={{0,8},{1,3},{2,10},{3,5},{4,12},{5,7},{6,14},{7,1},{8,16},{9,11},{... | collective-permute-start | bytes 393224 | tf_op jit(solution)/shard_map/ppermute | solution.py:42
  15.1 10.3 %collective-permute-start.7 = (bf16[8,128,256]{2,1,0:T(8,128)(2,1)S(1)}, bf16[8,128,256]{2,1,0:T(8,128)(2,1)S(1)}, u32[]{:S(2)}, u32[]{:S(2)}) collective-permute-start(bf16[8,128,256]{2,1,0:T(8,128)(2,1)S(1)} %pad_maximum_fusion.set0), channel_id=1, source_target_pairs={{0,2},{1,9},{2,4},{3,11},{4,6},{5,13},{6,0},{7,15},{8,10},{9,17},{... | collective-permute-start | bytes 1572872 | tf_op jit(solution)/shard_map/ppermute | solution.py:42
  16.1 13.5 %collective-permute-start.8 = (bf16[8,128,256]{2,1,0:T(8,128)(2,1)S(1)}, bf16[8,128,256]{2,1,0:T(8,128)(2,1)S(1)}, u32[]{:S(2)}, u32[]{:S(2)}) collective-permute-start(bf16[8,128,256]{2,1,0:T(8,128)(2,1)S(1)} %pad_maximum_fusion.set0), channel_id=1, source_target_pairs={{0,6},{1,25},{2,0},{3,27},{4,2},{5,29},{6,4},{7,31},{8,14},{9,1},{... | collective-permute-start | bytes 1572872 | tf_op jit(solution)/shard_map/ppermute | solution.py:42
  17.9 16.8 %collective-permute-start.9 = (bf16[8,128,256]{2,1,0:T(8,128)(2,1)S(1)}, bf16[8,128,256]{2,1,0:T(8,128)(2,1)S(1)}, u32[]{:S(2)}, u32[]{:S(2)}) collective-permute-start(bf16[8,128,256]{2,1,0:T(8,128)(2,1)S(1)} %pad_maximum_fusion.set0), channel_id=1, source_target_pairs={{0,4},{1,17},{2,6},{3,19},{4,0},{5,21},{6,2},{7,23},{8,12},{9,25},... | collective-permute-start | bytes 1572872 | tf_op jit(solution)/shard_map/ppermute | solution.py:42
  23.7 12.0 %collective-permute-start.10 = (bf16[256,256]{1,0:T(8,128)(2,1)S(1)}, bf16[256,256]{1,0:T(8,128)(2,1)S(1)}, u32[]{:S(2)}, u32[]{:S(2)}) collective-permute-start(bf16[256,256]{1,0:T(8,128)(2,1)S(1)} %broadcast_multiply_fusion), channel_id=1, source_target_pairs={{0,32},{1,33},{2,34},{3,35},{4,36},{5,37},{6,38},{7,39},{8,40},{9,... | collective-permute-start | bytes 393224 | tf_op jit(solution)/shard_map/ppermute | solution.py:42
  25.4 10.4 %collective-permute-start.11 = (bf16[256,256]{1,0:T(8,128)(2,1)S(1)}, bf16[256,256]{1,0:T(8,128)(2,1)S(1)}, u32[]{:S(2)}, u32[]{:S(2)}) collective-permute-start(bf16[256,256]{1,0:T(8,128)(2,1)S(1)} %broadcast_multiply_fusion), channel_id=1, source_target_pairs={{0,96},{1,97},{2,98},{3,99},{4,100},{5,101},{6,102},{7,103},{8,104... | collective-permute-start | bytes 393224 | tf_op jit(solution)/shard_map/ppermute | solution.py:42
  29.6 6.8 %collective-permute-start.12 = (bf16[256,256]{1,0:T(8,128)(2,1)S(1)}, bf16[256,256]{1,0:T(8,128)(2,1)S(1)}, u32[]{:S(2)}, u32[]{:S(2)}) collective-permute-start(bf16[256,256]{1,0:T(8,128)(2,1)S(1)} %broadcast_multiply_fusion), channel_id=1, source_target_pairs={{0,64},{1,65},{2,66},{3,67},{4,68},{5,69},{6,70},{7,71},{8,72},{9,... | collective-permute-start | bytes 393224 | tf_op jit(solution)/shard_map/ppermute | solution.py:42
  36.4 5.7 %collective-permute-start.13 = (bf16[4,128,256]{2,1,0:T(8,128)(2,1)S(1)}, bf16[4,128,256]{2,1,0:T(8,128)(2,1)S(1)}, u32[]{:S(2)}, u32[]{:S(2)}) collective-permute-start(bf16[4,128,256]{2,1,0:T(8,128)(2,1)S(1)} %shard_map.75.refs_0_), channel_id=1, source_target_pairs={{0,1},{1,0},{2,3},{3,2},{4,5},{5,4},{6,7},{7,6},{8,9},{9,8},{10,11... | collective-permute-start | bytes 786440 | tf_op jit(solution)/shard_map/ppermute | solution.py:42
  37.6 7.9 %collective-permute-start.14 = (bf16[4,128,256]{2,1,0:T(8,128)(2,1)S(1)}, bf16[4,128,256]{2,1,0:T(8,128)(2,1)S(1)}, u32[]{:S(2)}, u32[]{:S(2)}) collective-permute-start(bf16[4,128,256]{2,1,0:T(8,128)(2,1)S(1)} %shard_map.75.refs_0_), channel_id=1, source_target_pairs={{0,96},{1,97},{2,98},{3,99},{4,100},{5,101},{6,102},{7,103},{8,104... | collective-permute-start | bytes 786440 | tf_op jit(solution)/shard_map/ppermute | solution.py:42
  38.7 8.3 %collective-permute-start.15 = (bf16[4,128,256]{2,1,0:T(8,128)(2,1)S(1)}, bf16[4,128,256]{2,1,0:T(8,128)(2,1)S(1)}, u32[]{:S(2)}, u32[]{:S(2)}) collective-permute-start(bf16[4,128,256]{2,1,0:T(8,128)(2,1)S(1)} %shard_map.75.refs_0_), channel_id=1, source_target_pairs={{0,32},{1,33},{2,34},{3,35},{4,36},{5,37},{6,38},{7,39},{8,40},{9,... | collective-permute-start | bytes 786440 | tf_op jit(solution)/shard_map/ppermute | solution.py:42
  39.2 16.1 %collective-permute-start.19 = (bf16[3,256,256]{2,1,0:T(8,128)(2,1)S(1)}, bf16[3,256,256]{2,1,0:T(8,128)(2,1)S(1)}, u32[]{:S(2)}, u32[]{:S(2)}) collective-permute-start(bf16[3,256,256]{2,1,0:T(8,128)(2,1)S(1)} %pad_maximum_fusion.1.own), channel_id=1, source_target_pairs={{0,1},{1,0},{2,3},{3,2},{4,5},{5,4},{6,7},{7,6},{8,9},{9,8},{10,11... | collective-permute-start | bytes 1179656 | tf_op jit(solution)/shard_map/ppermute | solution.py:42
  46.9 9.0 %collective-permute-start.20 = (bf16[4,128,256]{2,1,0:T(8,128)(2,1)S(1)}, bf16[4,128,256]{2,1,0:T(8,128)(2,1)S(1)}, u32[]{:S(2)}, u32[]{:S(2)}) collective-permute-start(bf16[4,128,256]{2,1,0:T(8,128)(2,1)S(1)} %collective-permute-done.15.refs_0_), channel_id=1, source_target_pairs={{0,1},{1,0},{2,3},{3,2},{4,5},{5,4},{6,7},{7,6},{8,9},{9,8},{10,11... | collective-permute-start | bytes 786440 | tf_op jit(solution)/shard_map/ppermute | solution.py:42
  48.6 9.9 %collective-permute-start.21 = (bf16[4,128,256]{2,1,0:T(8,128)(2,1)S(1)}, bf16[4,128,256]{2,1,0:T(8,128)(2,1)S(1)}, u32[]{:S(2)}, u32[]{:S(2)}) collective-permute-start(bf16[4,128,256]{2,1,0:T(8,128)(2,1)S(1)} %collective-permute-done.14.refs_2_), channel_id=1, source_target_pairs={{0,1},{1,0},{2,3},{3,2},{4,5},{5,4},{6,7},{7,6},{8,9},{9,8},{10,11... | collective-permute-start | bytes 786440 | tf_op jit(solution)/shard_map/ppermute | solution.py:42
  48.6 15.6 %collective-permute-start.22 = (bf16[4,128,256]{2,1,0:T(8,128)(2,1)S(1)}, bf16[4,128,256]{2,1,0:T(8,128)(2,1)S(1)}, u32[]{:S(2)}, u32[]{:S(2)}) collective-permute-start(bf16[4,128,256]{2,1,0:T(8,128)(2,1)S(1)} %shard_map.75.refs_0_), channel_id=1, source_target_pairs={{0,64},{1,65},{2,66},{3,67},{4,68},{5,69},{6,70},{7,71},{8,72},{9,... | collective-permute-start | bytes 786440 | tf_op jit(solution)/shard_map/ppermute | solution.py:42
  48.6 17.7 %collective-permute-start.16 = (bf16[1,8,64,256]{3,2,1,0:T(8,128)(2,1)S(1)}, bf16[1,8,64,256]{3,2,1,0:T(8,128)(2,1)}, u32[]{:S(2)}, u32[]{:S(2)}) collective-permute-start(bf16[1,8,64,256]{3,2,1,0:T(8,128)(2,1)S(1)} %get-tuple-element.64), channel_id=1, source_target_pairs={{0,16},{1,5},{2,18},{3,7},{4,20},{5,1},{6,22},{7,3},{8,24},{9,13},... | collective-permute-start | bytes 786440 | tf_op jit(solution)/shard_map/ppermute | solution.py:42
  55.2 11.1 %collective-permute-start.17 = (bf16[1,8,64,256]{3,2,1,0:T(8,128)(2,1)}, bf16[1,8,64,256]{3,2,1,0:T(8,128)(2,1)}, u32[]{:S(2)}, u32[]{:S(2)}) collective-permute-start(bf16[1,8,64,256]{3,2,1,0:T(8,128)(2,1)} %get-tuple-element.65), channel_id=1, source_target_pairs={{0,8},{1,3},{2,10},{3,5},{4,12},{5,7},{6,14},{7,1},{8,16},{9,11},{... | collective-permute-start | bytes 786440 | tf_op jit(solution)/shard_map/ppermute | solution.py:42
  55.9 10.4 %collective-permute-start.18 = (bf16[1,8,64,256]{3,2,1,0:T(8,128)(2,1)}, bf16[1,8,64,256]{3,2,1,0:T(8,128)(2,1)}, u32[]{:S(2)}, u32[]{:S(2)}) collective-permute-start(bf16[1,8,64,256]{3,2,1,0:T(8,128)(2,1)} %get-tuple-element.66), channel_id=1, source_target_pairs={{0,24},{1,7},{2,26},{3,1},{4,28},{5,3},{6,30},{7,5},{8,0},{9,15},{... | collective-permute-start | bytes 786440 | tf_op jit(solution)/shard_map/ppermute | solution.py:42
  64.9 11.8 %collective-permute-start.25 = (bf16[2,8,64,256]{3,2,1,0:T(8,128)(2,1)}, bf16[2,8,64,256]{3,2,1,0:T(8,128)(2,1)}, u32[]{:S(2)}, u32[]{:S(2)}) collective-permute-start(bf16[2,8,64,256]{3,2,1,0:T(8,128)(2,1)} %get-tuple-element.83), channel_id=1, source_target_pairs={{0,24},{1,7},{2,26},{3,1},{4,28},{5,3},{6,30},{7,5},{8,0},{9,15},{... | collective-permute-start | bytes 1572872 | tf_op jit(solution)/shard_map/ppermute | solution.py:42
  64.9 15.4 %collective-permute-start.24 = (bf16[2,8,64,256]{3,2,1,0:T(8,128)(2,1)}, bf16[2,8,64,256]{3,2,1,0:T(8,128)(2,1)}, u32[]{:S(2)}, u32[]{:S(2)}) collective-permute-start(bf16[2,8,64,256]{3,2,1,0:T(8,128)(2,1)} %get-tuple-element.82), channel_id=1, source_target_pairs={{0,8},{1,3},{2,10},{3,5},{4,12},{5,7},{6,14},{7,1},{8,16},{9,11},{... | collective-permute-start | bytes 1572872 | tf_op jit(solution)/shard_map/ppermute | solution.py:42
  66.3 13.9 %collective-permute-start.23 = (bf16[2,8,64,256]{3,2,1,0:T(8,128)(2,1)}, bf16[2,8,64,256]{3,2,1,0:T(8,128)(2,1)}, u32[]{:S(2)}, u32[]{:S(2)}) collective-permute-start(bf16[2,8,64,256]{3,2,1,0:T(8,128)(2,1)} %get-tuple-element.81), channel_id=1, source_target_pairs={{0,16},{1,5},{2,18},{3,7},{4,20},{5,1},{6,22},{7,3},{8,24},{9,13},... | collective-permute-start | bytes 1572872 | tf_op jit(solution)/shard_map/ppermute | solution.py:42
  73.0 9.1 %collective-permute-start.29 = (bf16[1,8,64,256]{3,2,1,0:T(8,128)(2,1)S(1)}, bf16[1,8,64,256]{3,2,1,0:T(8,128)(2,1)S(1)}, u32[]{:S(2)}, u32[]{:S(2)}) collective-permute-start(bf16[1,8,64,256]{3,2,1,0:T(8,128)(2,1)S(1)} %get-tuple-element.88), channel_id=1, source_target_pairs={{0,24},{1,7},{2,26},{3,1},{4,28},{5,3},{6,30},{7,5},{8,0},{9,15},{... | collective-permute-start | bytes 786440 | tf_op jit(solution)/shard_map/ppermute | solution.py:42
  76.7 9.2 %collective-permute-start.28 = (bf16[1,8,64,256]{3,2,1,0:T(8,128)(2,1)S(1)}, bf16[1,8,64,256]{3,2,1,0:T(8,128)(2,1)S(1)}, u32[]{:S(2)}, u32[]{:S(2)}) collective-permute-start(bf16[1,8,64,256]{3,2,1,0:T(8,128)(2,1)S(1)} %get-tuple-element.87), channel_id=1, source_target_pairs={{0,8},{1,3},{2,10},{3,5},{4,12},{5,7},{6,14},{7,1},{8,16},{9,11},{... | collective-permute-start | bytes 786440 | tf_op jit(solution)/shard_map/ppermute | solution.py:42
  76.7 9.2 %collective-permute-start.27 = (bf16[1,8,64,256]{3,2,1,0:T(8,128)(2,1)S(1)}, bf16[1,8,64,256]{3,2,1,0:T(8,128)(2,1)S(1)}, u32[]{:S(2)}, u32[]{:S(2)}) collective-permute-start(bf16[1,8,64,256]{3,2,1,0:T(8,128)(2,1)S(1)} %get-tuple-element.86), channel_id=1, source_target_pairs={{0,16},{1,5},{2,18},{3,7},{4,20},{5,1},{6,22},{7,3},{8,24},{9,13},... | collective-permute-start | bytes 786440 | tf_op jit(solution)/shard_map/ppermute | solution.py:42
  86.2 5.3 %collective-permute-start.32 = (bf16[4,8,16,256]{3,2,1,0:T(8,128)(2,1)S(1)}, bf16[4,8,16,256]{3,2,1,0:T(8,128)(2,1)S(1)}, u32[]{:S(2)}, u32[]{:S(2)}) collective-permute-start(bf16[4,8,16,256]{3,2,1,0:T(8,128)(2,1)S(1)} %pad_maximum_fusion.4), channel_id=1, source_target_pairs={{0,6},{1,25},{2,0},{3,27},{4,2},{5,29},{6,4},{7,31},{8,14},{9,1},{... | collective-permute-start | bytes 786440 | tf_op jit(solution)/shard_map/ppermute | solution.py:42
  87.2 9.6 %collective-permute-start.31 = (bf16[4,8,16,256]{3,2,1,0:T(8,128)(2,1)S(1)}, bf16[4,8,16,256]{3,2,1,0:T(8,128)(2,1)S(1)}, u32[]{:S(2)}, u32[]{:S(2)}) collective-permute-start(bf16[4,8,16,256]{3,2,1,0:T(8,128)(2,1)S(1)} %pad_maximum_fusion.3), channel_id=1, source_target_pairs={{0,2},{1,9},{2,4},{3,11},{4,6},{5,13},{6,0},{7,15},{8,10},{9,17},{... | collective-permute-start | bytes 786440 | tf_op jit(solution)/shard_map/ppermute | solution.py:42
  87.9 8.9 %collective-permute-start.30 = (bf16[4,8,16,256]{3,2,1,0:T(8,128)(2,1)S(1)}, bf16[4,8,16,256]{3,2,1,0:T(8,128)(2,1)S(1)}, u32[]{:S(2)}, u32[]{:S(2)}) collective-permute-start(bf16[4,8,16,256]{3,2,1,0:T(8,128)(2,1)S(1)} %pad_maximum_fusion.2), channel_id=1, source_target_pairs={{0,4},{1,17},{2,6},{3,19},{4,0},{5,21},{6,2},{7,23},{8,12},{9,25},... | collective-permute-start | bytes 786440 | tf_op jit(solution)/shard_map/ppermute | solution.py:42
  97.0 5.0 %collective-permute-start.35 = (bf16[8,16,256]{2,1,0:T(8,128)(2,1)S(1)}, bf16[8,16,256]{2,1,0:T(8,128)(2,1)S(1)}, u32[]{:S(2)}, u32[]{:S(2)}) collective-permute-start(bf16[8,16,256]{2,1,0:T(8,128)(2,1)S(1)} %get-tuple-element.98), channel_id=1, source_target_pairs={{0,32},{1,33},{2,34},{3,35},{4,36},{5,37},{6,38},{7,39},{8,40},{9,... | collective-permute-start | bytes 196616 | tf_op jit(solution)/shard_map/ppermute | solution.py:42
  99.7 4.6 %collective-permute-start.33 = (bf16[8,16,256]{2,1,0:T(8,128)(2,1)S(1)}, bf16[8,16,256]{2,1,0:T(8,128)(2,1)S(1)}, u32[]{:S(2)}, u32[]{:S(2)}) collective-permute-start(bf16[8,16,256]{2,1,0:T(8,128)(2,1)S(1)} %get-tuple-element.100), channel_id=1, source_target_pairs={{0,64},{1,65},{2,66},{3,67},{4,68},{5,69},{6,70},{7,71},{8,72},{9,... | collective-permute-start | bytes 196616 | tf_op jit(solution)/shard_map/ppermute | solution.py:42
  104.4 6.1 %collective-permute-start.36 = (bf16[4,8,16,128]{3,2,1,0:T(8,128)(2,1)S(1)}, bf16[4,8,16,128]{3,2,1,0:T(8,128)(2,1)S(1)}, u32[]{:S(2)}, u32[]{:S(2)}) collective-permute-start(bf16[4,8,16,128]{3,2,1,0:T(8,128)(2,1)S(1)} %get-tuple-element.105), channel_id=1, source_target_pairs={{0,1},{1,0},{2,3},{3,2},{4,5},{5,4},{6,7},{7,6},{8,9},{9,8},{10,11... | collective-permute-start | bytes 393224 | tf_op jit(solution)/shard_map/ppermute | solution.py:42
  (12 other events, 72.1 us)

commit v7 on v5

--- a/solution.py
+++ b/solution.py
@@ -240,7 +240,7 @@
         lax.dynamic_slice_in_dim(go, c * 128, 128, 0),
         move(lax.dynamic_slice_in_dim(go, (1 - c) * 128, 128, 0), CORE),
     )
-    go, theirs = tie(go, three_centre)
+    go, theirs, pair_oth = tie(go, three_centre, move(pair_blocks, CORE))
     t_oth = move(theirs, CORE)
 
     go1, go3, go2 = [move(go, FIRST[d]) for d in (1, 3, 2)]
@@ -258,7 +258,7 @@
     ).astype(jnp.int32)
     gv = order_rows(strips, gv, move(gv, CORE))
 
-    partners = by_core(pair_blocks[0], move(pair_blocks, CORE)[0]).reshape(4)
+    partners = by_core(pair_blocks[0], pair_oth[0]).reshape(4)
     places = jnp.concatenate([jnp.stack([c, q1, q2]), partners]).astype(jnp.int32)
     places, gv, set1, set3, set2 = tie(places, gv, set1, set3, set2)
     picked = pick(places, near, set1, set2, set3)
@@ -270,11 +270,11 @@
     core = c.reshape(1).astype(jnp.int32)
     given = (core, *keep_half(core, three_centre, t_oth))
     sends0 = products_of(*given, gv, (picked, move(picked, CORE)), 1, 0, 0)
-    *sends0, side3, side1 = tie(*sends0, *side)
+    *_, side3, side1 = tie(*sends0, *side)
     got0 = [move(sends0[d - 1], FIRST[d]) for d in (2, 1, 3)]
     halves = [h for a in (side1, side3) for h in (a, move(a, CORE))]
     sends1 = products_of(*given, gv_rest, halves, 2, 0, 0)
-    *sends1, far = tie(*sends1, far)
+    *_, far = tie(*sends1, far)
     *got0, far = tie(*got0, far)
     sends2 = products_of(*given, gv_rest, (far, move(far, CORE)), 1, 0, 2)
 

time: 124 us -> 124 us (level)
  no operation moved by 1% of the time
where the time goes in v7:
time: 124 us
  starting transfers between devices  59.5 us (48%)
  waiting for transfers between devices  28 us (23%)
  blocking collectives  15.3 us (12%)
  Pallas kernels  14 us (11%)
  other arithmetic  5.21 us (4%)
  between operations  1.62 us (1%)
    ppermute x37, starting transfers between devices, move(): return lax.ppermute(value, AXES, permutation)  59.5 us
    ppermute x37, waiting for transfers between devices, move(): return lax.ppermute(value, AXES, permutation)  28 us
    all_to_all x1, blocking collectives, per_device(): lax.all_to_all(outgoing.reshape(32, CAP, 16, 128), 'sub', split_axis=0, c...  15.3 us
    pallas_call x3, Pallas kernels, products_of(): pl.pallas_call(products_body, grid_spec=pltpu.PrefetchScalarGridSpec(num_...  7.96 us
  transfers between devices with their start and end apart: 37, of which 20 were waited for; matrix products, arithmetic and copies ran while one was open for 2% of the time, Pallas kernels for 10%

profile of v7, /device:TPU:1, one launch (start us, length us, event | category | flops | bytes accessed | tf_op | source)
XLA Modules:
  0.0 124.1 jit_solution(12081877042209911142)
XLA Ops:
  1.6 1.5 %collective-permute-start = (bf16[128,256]{1,0:T(8,128)(2,1)S(1)}, bf16[128,256]{1,0:T(8,128)(2,1)S(1)}, u32[]{:S(2)}, u32[]{:S(2)}) collective-permute-start(bf16[128,256]{1,0:T(8,128)(2,1)S(1)} %get-tuple-element.97), channel_id=1, source_target_pairs={{0,1},{1,0},{2,3},{3,2},{4,5},{5,4},{6,7},{7,6},{8,9},{9,8},{10,11... | collective-permute-start | bytes 196616 | tf_op jit(solution)/shard_map/ppermute | solution.py:42
  6.7 2.6 %collective-permute-start.4 = (bf16[2,128,256]{2,1,0:T(8,128)(2,1)S(1)}, bf16[2,128,256]{2,1,0:T(8,128)(2,1)S(1)}, u32[]{:S(2)}, u32[]{:S(2)}) collective-permute-start(bf16[2,128,256]{2,1,0:T(8,128)(2,1)S(1)} %maximum_select_fusion), channel_id=1, source_target_pairs={{0,16},{1,5},{2,18},{3,7},{4,20},{5,1},{6,22},{7,3},{8,24},{9,13},... | collective-permute-start | bytes 393224 | tf_op jit(solution)/shard_map/ppermute | solution.py:42
  11.3 2.1 %collective-permute-done.4 = bf16[2,128,256]{2,1,0:T(8,128)(2,1)S(1)} collective-permute-done((bf16[2,128,256]{2,1,0:T(8,128)(2,1)S(1)}, bf16[2,128,256]{2,1,0:T(8,128)(2,1)S(1)}, u32[]{:S(2)}, u32[]{:S(2)}) %collective-permute-start.4) | collective-permute-done | bytes 131104 | tf_op jit(solution)/shard_map/ppermute | solution.py:42
  14.8 1.5 %collective-permute-start.8 = (bf16[8,128,256]{2,1,0:T(8,128)(2,1)S(1)}, bf16[8,128,256]{2,1,0:T(8,128)(2,1)S(1)}, u32[]{:S(2)}, u32[]{:S(2)}) collective-permute-start(bf16[8,128,256]{2,1,0:T(8,128)(2,1)S(1)} %pad_maximum_fusion.set0), channel_id=1, source_target_pairs={{0,6},{1,25},{2,0},{3,27},{4,2},{5,29},{6,4},{7,31},{8,14},{9,1},{... | collective-permute-start | bytes 1572872 | tf_op jit(solution)/shard_map/ppermute | solution.py:42
  16.2 1.5 %collective-permute-start.9 = (bf16[8,128,256]{2,1,0:T(8,128)(2,1)S(1)}, bf16[8,128,256]{2,1,0:T(8,128)(2,1)S(1)}, u32[]{:S(2)}, u32[]{:S(2)}) collective-permute-start(bf16[8,128,256]{2,1,0:T(8,128)(2,1)S(1)} %pad_maximum_fusion.set0), channel_id=1, source_target_pairs={{0,4},{1,17},{2,6},{3,19},{4,0},{5,21},{6,2},{7,23},{8,12},{9,25},... | collective-permute-start | bytes 1572872 | tf_op jit(solution)/shard_map/ppermute | solution.py:42
  17.8 2.5 %collective-permute-start.6 = (bf16[1,256,256]{2,1,0:T(8,128)(2,1)S(1)}, bf16[1,256,256]{2,1,0:T(8,128)(2,1)S(1)}, u32[]{:S(2)}, u32[]{:S(2)}) collective-permute-start(bf16[1,256,256]{2,1,0:T(8,128)(2,1)S(1)} %bitcast.45), channel_id=1, source_target_pairs={{0,1},{1,0},{2,3},{3,2},{4,5},{5,4},{6,7},{7,6},{8,9},{9,8},{10,11... | collective-permute-start | bytes 393224 | tf_op jit(solution)/shard_map/ppermute | solution.py:42
  21.2 1.6 %collective-permute-start.10 = (bf16[256,256]{1,0:T(8,128)(2,1)S(1)}, bf16[256,256]{1,0:T(8,128)(2,1)S(1)}, u32[]{:S(2)}, u32[]{:S(2)}) collective-permute-start(bf16[256,256]{1,0:T(8,128)(2,1)S(1)} %broadcast_multiply_fusion), channel_id=1, source_target_pairs={{0,32},{1,33},{2,34},{3,35},{4,36},{5,37},{6,38},{7,39},{8,40},{9,... | collective-permute-start | bytes 393224 | tf_op jit(solution)/shard_map/ppermute | solution.py:42
  23.1 3.8 %collective-permute-start.11 = (bf16[256,256]{1,0:T(8,128)(2,1)S(1)}, bf16[256,256]{1,0:T(8,128)(2,1)S(1)}, u32[]{:S(2)}, u32[]{:S(2)}) collective-permute-start(bf16[256,256]{1,0:T(8,128)(2,1)S(1)} %broadcast_multiply_fusion), channel_id=1, source_target_pairs={{0,96},{1,97},{2,98},{3,99},{4,100},{5,101},{6,102},{7,103},{8,104... | collective-permute-start | bytes 393224 | tf_op jit(solution)/shard_map/ppermute | solution.py:42
  32.2 3.7 %collective-permute-start.13 = (bf16[4,128,256]{2,1,0:T(8,128)(2,1)S(1)}, bf16[4,128,256]{2,1,0:T(8,128)(2,1)S(1)}, u32[]{:S(2)}, u32[]{:S(2)}) collective-permute-start(bf16[4,128,256]{2,1,0:T(8,128)(2,1)S(1)} %shard_map.75.refs_0_), channel_id=1, source_target_pairs={{0,1},{1,0},{2,3},{3,2},{4,5},{5,4},{6,7},{7,6},{8,9},{9,8},{10,11... | collective-permute-start | bytes 786440 | tf_op jit(solution)/shard_map/ppermute | solution.py:42
  38.1 2.2 %shard_map.73 = (bf16[8,256,512]{2,1,0:T(8,128)(2,1)S(1)}, bf16[8,256,512]{2,1,0:T(8,128)(2,1)S(1)}) custom-call(s32[1]{0:T(128)} %bitcast.1.sc, bf16[16,256,512]{2,1,0:T(8,128)(2,1)} %own.1, bf16[16,256,512]{2,1,0:T(8,128)(2,1)} %collective-permute-done.2.oth), custom_call_target="tpu_custom_call" | custom-call | bytes 1000 | tf_op jit(solution)/shard_map/pallas_call | solution.py:127
  40.3 2.0 %shard_map.76 = (bf16[1,8,64,256]{3,2,1,0:T(8,128)(2,1)S(1)}, bf16[1,8,64,256]{3,2,1,0:T(8,128)(2,1)S(1)}, bf16[1,8,64,256]{3,2,1,0:T(8,128)(2,1)S(1)}, f32[1,8,64,256]{3,2,1,0:T(8,128)S(1)}) custom-call(s32[1]{0:T(128)} %bitcast.1.sc, bf16[8,256,512]{2,1,0:T(8,128)(2,1)S(1)} %get-tuple-element.41.t_own, bf16[8,256,512]{2,1,0:T(8,128)(2,1)S(1)} %get-tuple-element.42.t_oth, ...), custom_call_target="tpu_custom_call" | custom-call | flops 1000 | bytes 1000 | tf_op jit(solution)/shard_map/pallas_call | solution.py:174
  42.4 1.5 %collective-permute-done.18.refs_2_ = bf16[4,128,256]{2,1,0:T(8,128)(2,1)S(1)} collective-permute-done((bf16[4,128,256]{2,1,0:T(8,128)(2,1)S(1)}, bf16[4,128,256]{2,1,0:T(8,128)(2,1)S(1)}, u32[]{:S(2)}, u32[]{:S(2)}) %collective-permute-start.18) | collective-permute-done | bytes 262176 | tf_op jit(solution)/shard_map/ppermute | solution.py:42
  43.9 2.1 %collective-permute-done.19.refs_0_ = bf16[4,128,256]{2,1,0:T(8,128)(2,1)S(1)} collective-permute-done((bf16[4,128,256]{2,1,0:T(8,128)(2,1)S(1)}, bf16[4,128,256]{2,1,0:T(8,128)(2,1)S(1)}, u32[]{:S(2)}, u32[]{:S(2)}) %collective-permute-start.19) | collective-permute-done | bytes 262176 | tf_op jit(solution)/shard_map/ppermute | solution.py:42
  47.2 6.8 %collective-permute-start.14 = (bf16[1,8,64,256]{3,2,1,0:T(8,128)(2,1)S(1)}, bf16[1,8,64,256]{3,2,1,0:T(8,128)(2,1)S(1)}, u32[]{:S(2)}, u32[]{:S(2)}) collective-permute-start(bf16[1,8,64,256]{3,2,1,0:T(8,128)(2,1)S(1)} %get-tuple-element.54), channel_id=1, source_target_pairs={{0,16},{1,5},{2,18},{3,7},{4,20},{5,1},{6,22},{7,3},{8,24},{9,13},... | collective-permute-start | bytes 786440 | tf_op jit(solution)/shard_map/ppermute | solution.py:42
  54.7 2.0 %collective-permute-start.16 = (bf16[1,8,64,256]{3,2,1,0:T(8,128)(2,1)S(1)}, bf16[1,8,64,256]{3,2,1,0:T(8,128)(2,1)S(1)}, u32[]{:S(2)}, u32[]{:S(2)}) collective-permute-start(bf16[1,8,64,256]{3,2,1,0:T(8,128)(2,1)S(1)} %get-tuple-element.56), channel_id=1, source_target_pairs={{0,24},{1,7},{2,26},{3,1},{4,28},{5,3},{6,30},{7,5},{8,0},{9,15},{... | collective-permute-start | bytes 786440 | tf_op jit(solution)/shard_map/ppermute | solution.py:42
  57.3 3.9 %shard_map.78 = (bf16[2,8,64,256]{3,2,1,0:T(8,128)(2,1)S(1)}, bf16[2,8,64,256]{3,2,1,0:T(8,128)(2,1)S(1)}, bf16[2,8,64,256]{3,2,1,0:T(8,128)(2,1)S(1)}, f32[2,8,64,256]{3,2,1,0:T(8,128)S(1)}) custom-call(s32[1]{0:T(128)} %bitcast.1.sc, bf16[8,256,512]{2,1,0:T(8,128)(2,1)S(1)} %get-tuple-element.41.t_own, bf16[8,256,512]{2,1,0:T(8,128)(2,1)S(1)} %get-tuple-element.42.t_oth, ...), custom_call_target="tpu_custom_call" | custom-call | flops 1000 | bytes 1000 | tf_op jit(solution)/shard_map/pallas_call | solution.py:174
  61.9 2.2 %collective-permute-start.25 = (bf16[2,8,64,256]{3,2,1,0:T(8,128)(2,1)S(1)}, bf16[2,8,64,256]{3,2,1,0:T(8,128)(2,1)S(1)}, u32[]{:S(2)}, u32[]{:S(2)}) collective-permute-start(bf16[2,8,64,256]{3,2,1,0:T(8,128)(2,1)S(1)} %get-tuple-element.64), channel_id=1, source_target_pairs={{0,24},{1,7},{2,26},{3,1},{4,28},{5,3},{6,30},{7,5},{8,0},{9,15},{... | collective-permute-start | bytes 1572872 | tf_op jit(solution)/shard_map/ppermute | solution.py:42
  65.6 2.0 %shard_map.79 = (bf16[1,8,64,256]{3,2,1,0:T(8,128)(2,1)S(1)}, bf16[1,8,64,256]{3,2,1,0:T(8,128)(2,1)S(1)}, bf16[1,8,64,256]{3,2,1,0:T(8,128)(2,1)S(1)}, f32[1,8,64,256]{3,2,1,0:T(8,128)S(1)}) custom-call(s32[1]{0:T(128)} %bitcast.1.sc, bf16[8,256,512]{2,1,0:T(8,128)(2,1)S(1)} %get-tuple-element.41.t_own, bf16[8,256,512]{2,1,0:T(8,128)(2,1)S(1)} %get-tuple-element.42.t_oth, ...), custom_call_target="tpu_custom_call" | custom-call | flops 1000 | bytes 1000 | tf_op jit(solution)/shard_map/pallas_call | solution.py:174
  67.6 3.9 %collective-permute-start.27 = (bf16[1,8,64,256]{3,2,1,0:T(8,128)(2,1)S(1)}, bf16[1,8,64,256]{3,2,1,0:T(8,128)(2,1)S(1)}, u32[]{:S(2)}, u32[]{:S(2)}) collective-permute-start(bf16[1,8,64,256]{3,2,1,0:T(8,128)(2,1)S(1)} %get-tuple-element.72), channel_id=1, source_target_pairs={{0,16},{1,5},{2,18},{3,7},{4,20},{5,1},{6,22},{7,3},{8,24},{9,13},... | collective-permute-start | bytes 786440 | tf_op jit(solution)/shard_map/ppermute | solution.py:42
  72.0 2.2 %collective-permute-start.29 = (bf16[1,8,64,256]{3,2,1,0:T(8,128)(2,1)S(1)}, bf16[1,8,64,256]{3,2,1,0:T(8,128)(2,1)S(1)}, u32[]{:S(2)}, u32[]{:S(2)}) collective-permute-start(bf16[1,8,64,256]{3,2,1,0:T(8,128)(2,1)S(1)} %get-tuple-element.74), channel_id=1, source_target_pairs={{0,24},{1,7},{2,26},{3,1},{4,28},{5,3},{6,30},{7,5},{8,0},{9,15},{... | collective-permute-start | bytes 786440 | tf_op jit(solution)/shard_map/ppermute | solution.py:42
  74.2 2.3 %collective-permute-done.24 = bf16[2,8,64,256]{3,2,1,0:T(8,128)(2,1)S(1)} collective-permute-done((bf16[2,8,64,256]{3,2,1,0:T(8,128)(2,1)S(1)}, bf16[2,8,64,256]{3,2,1,0:T(8,128)(2,1)S(1)}, u32[]{:S(2)}, u32[]{:S(2)}) %collective-permute-start.24) | collective-permute-done | bytes 524320 | tf_op jit(solution)/shard_map/ppermute | solution.py:42
  76.9 2.5 %collective-permute-done.27 = bf16[1,8,64,256]{3,2,1,0:T(8,128)(2,1)S(1)} collective-permute-done((bf16[1,8,64,256]{3,2,1,0:T(8,128)(2,1)S(1)}, bf16[1,8,64,256]{3,2,1,0:T(8,128)(2,1)S(1)}, u32[]{:S(2)}, u32[]{:S(2)}) %collective-permute-start.27) | collective-permute-done | bytes 262176 | tf_op jit(solution)/shard_map/ppermute | solution.py:42
  79.4 2.5 %collective-permute-done.28 = bf16[1,8,64,256]{3,2,1,0:T(8,128)(2,1)S(1)} collective-permute-done((bf16[1,8,64,256]{3,2,1,0:T(8,128)(2,1)S(1)}, bf16[1,8,64,256]{3,2,1,0:T(8,128)(2,1)S(1)}, u32[]{:S(2)}, u32[]{:S(2)}) %collective-permute-start.28) | collective-permute-done | bytes 262176 | tf_op jit(solution)/shard_map/ppermute | solution.py:42
  82.1 2.1 %collective-permute-start.30 = (bf16[4,8,16,256]{3,2,1,0:T(8,128)(2,1)S(1)}, bf16[4,8,16,256]{3,2,1,0:T(8,128)(2,1)}, u32[]{:S(2)}, u32[]{:S(2)}) collective-permute-start(bf16[4,8,16,256]{3,2,1,0:T(8,128)(2,1)S(1)} %pad_maximum_fusion.2), channel_id=1, source_target_pairs={{0,4},{1,17},{2,6},{3,19},{4,0},{5,21},{6,2},{7,23},{8,12},{9,25},... | collective-permute-start | bytes 786440 | tf_op jit(solution)/shard_map/ppermute | solution.py:42
  85.5 1.6 %collective-permute-start.32 = (bf16[4,8,16,256]{3,2,1,0:T(8,128)(2,1)S(1)}, bf16[4,8,16,256]{3,2,1,0:T(8,128)(2,1)}, u32[]{:S(2)}, u32[]{:S(2)}) collective-permute-start(bf16[4,8,16,256]{3,2,1,0:T(8,128)(2,1)S(1)} %pad_maximum_fusion.4), channel_id=1, source_target_pairs={{0,6},{1,25},{2,0},{3,27},{4,2},{5,29},{6,4},{7,31},{8,14},{9,1},{... | collective-permute-start | bytes 786440 | tf_op jit(solution)/shard_map/ppermute | solution.py:42
  87.2 2.1 %collective-permute-done.30 = bf16[4,8,16,256]{3,2,1,0:T(8,128)(2,1)} collective-permute-done((bf16[4,8,16,256]{3,2,1,0:T(8,128)(2,1)S(1)}, bf16[4,8,16,256]{3,2,1,0:T(8,128)(2,1)}, u32[]{:S(2)}, u32[]{:S(2)}) %collective-permute-start.30) | collective-permute-done | bytes 262176 | tf_op jit(solution)/shard_map/ppermute | solution.py:42
  89.3 2.8 %collective-permute-done.31 = bf16[4,8,16,256]{3,2,1,0:T(8,128)(2,1)} collective-permute-done((bf16[4,8,16,256]{3,2,1,0:T(8,128)(2,1)S(1)}, bf16[4,8,16,256]{3,2,1,0:T(8,128)(2,1)}, u32[]{:S(2)}, u32[]{:S(2)}) %collective-permute-start.31) | collective-permute-done | bytes 262176 | tf_op jit(solution)/shard_map/ppermute | solution.py:42
  93.6 3.0 %collective-permute-start.33 = (bf16[8,16,256]{2,1,0:T(8,128)(2,1)S(1)}, bf16[8,16,256]{2,1,0:T(8,128)(2,1)S(1)}, u32[]{:S(2)}, u32[]{:S(2)}) collective-permute-start(bf16[8,16,256]{2,1,0:T(8,128)(2,1)S(1)} %get-tuple-element.89), channel_id=1, source_target_pairs={{0,64},{1,65},{2,66},{3,67},{4,68},{5,69},{6,70},{7,71},{8,72},{9,... | collective-permute-start | bytes 196616 | tf_op jit(solution)/shard_map/ppermute | solution.py:42
  96.6 1.5 %collective-permute-start.35 = (bf16[8,16,256]{2,1,0:T(8,128)(2,1)S(1)}, bf16[8,16,256]{2,1,0:T(8,128)(2,1)S(1)}, u32[]{:S(2)}, u32[]{:S(2)}) collective-permute-start(bf16[8,16,256]{2,1,0:T(8,128)(2,1)S(1)} %get-tuple-element.87), channel_id=1, source_target_pairs={{0,32},{1,33},{2,34},{3,35},{4,36},{5,37},{6,38},{7,39},{8,40},{9,... | collective-permute-start | bytes 196616 | tf_op jit(solution)/shard_map/ppermute | solution.py:42
  98.3 1.5 %collective-permute-done.34 = bf16[8,16,256]{2,1,0:T(8,128)(2,1)S(1)} collective-permute-done((bf16[8,16,256]{2,1,0:T(8,128)(2,1)S(1)}, bf16[8,16,256]{2,1,0:T(8,128)(2,1)S(1)}, u32[]{:S(2)}, u32[]{:S(2)}) %collective-permute-start.34) | collective-permute-done | bytes 65568 | tf_op jit(solution)/shard_map/ppermute | solution.py:42
  101.1 5.0 %collective-permute-start.36 = (bf16[4,8,16,128]{3,2,1,0:T(8,128)(2,1)S(1)}, bf16[4,8,16,128]{3,2,1,0:T(8,128)(2,1)S(1)}, u32[]{:S(2)}, u32[]{:S(2)}) collective-permute-start(bf16[4,8,16,128]{3,2,1,0:T(8,128)(2,1)S(1)} %get-tuple-element.85), channel_id=1, source_target_pairs={{0,1},{1,0},{2,3},{3,2},{4,5},{5,4},{6,7},{7,6},{8,9},{9,8},{10,11... | collective-permute-start | bytes 393224 | tf_op jit(solution)/shard_map/ppermute | solution.py:42
  107.8 15.3 %all_to_all.5.pieces = bf16[32,3,16,128]{3,2,1,0:T(8,128)(2,1)S(1)} all-to-all(bf16[32,3,16,128]{3,2,1,0:T(8,128)(2,1)S(1)} %bitcast.44), channel_id=1, replica_groups=mesh['grp'=4,'sub'=32] {'sub'}, dimensions={0} | all-to-all | bytes 786432 | tf_op jit(solution)/shard_map/all_to_all | solution.py:320
  (84 shorter events, 28.6 us)
Async XLA Ops:
  4.4 33.7 %collective-permute-start.2 = (bf16[16,256,512]{2,1,0:T(8,128)(2,1)}, bf16[16,256,512]{2,1,0:T(8,128)(2,1)}, u32[]{:S(2)}, u32[]{:S(2)}) collective-permute-start(bf16[16,256,512]{2,1,0:T(8,128)(2,1)} %own.1), channel_id=1, source_target_pairs={{0,1},{1,0},{2,3},{3,2},{4,5},{5,4},{6,7},{7,6},{8,9},{9,8},{10,11... | collective-permute-start | bytes 12582920 | tf_op jit(solution)/shard_map/ppermute | solution.py:42
  5.2 6.1 %collective-permute-start.3 = (bf16[2,128,256]{2,1,0:T(8,128)(2,1)S(1)}, bf16[2,128,256]{2,1,0:T(8,128)(2,1)S(1)}, u32[]{:S(2)}, u32[]{:S(2)}) collective-permute-start(bf16[2,128,256]{2,1,0:T(8,128)(2,1)S(1)} %maximum_select_fusion), channel_id=1, source_target_pairs={{0,8},{1,3},{2,10},{3,5},{4,12},{5,7},{6,14},{7,1},{8,16},{9,11},{... | collective-permute-start | bytes 393224 | tf_op jit(solution)/shard_map/ppermute | solution.py:42
  6.7 6.7 %collective-permute-start.4 = (bf16[2,128,256]{2,1,0:T(8,128)(2,1)S(1)}, bf16[2,128,256]{2,1,0:T(8,128)(2,1)S(1)}, u32[]{:S(2)}, u32[]{:S(2)}) collective-permute-start(bf16[2,128,256]{2,1,0:T(8,128)(2,1)S(1)} %maximum_select_fusion), channel_id=1, source_target_pairs={{0,16},{1,5},{2,18},{3,7},{4,20},{5,1},{6,22},{7,3},{8,24},{9,13},... | collective-permute-start | bytes 393224 | tf_op jit(solution)/shard_map/ppermute | solution.py:42
  9.3 4.1 %collective-permute-start.5 = (bf16[2,128,256]{2,1,0:T(8,128)(2,1)S(1)}, bf16[2,128,256]{2,1,0:T(8,128)(2,1)S(1)}, u32[]{:S(2)}, u32[]{:S(2)}) collective-permute-start(bf16[2,128,256]{2,1,0:T(8,128)(2,1)S(1)} %maximum_select_fusion), channel_id=1, source_target_pairs={{0,24},{1,7},{2,26},{3,1},{4,28},{5,3},{6,30},{7,5},{8,0},{9,15},{... | collective-permute-start | bytes 393224 | tf_op jit(solution)/shard_map/ppermute | solution.py:42
  13.5 9.6 %collective-permute-start.7 = (bf16[8,128,256]{2,1,0:T(8,128)(2,1)S(1)}, bf16[8,128,256]{2,1,0:T(8,128)(2,1)S(1)}, u32[]{:S(2)}, u32[]{:S(2)}) collective-permute-start(bf16[8,128,256]{2,1,0:T(8,128)(2,1)S(1)} %pad_maximum_fusion.set0), channel_id=1, source_target_pairs={{0,2},{1,9},{2,4},{3,11},{4,6},{5,13},{6,0},{7,15},{8,10},{9,17},{... | collective-permute-start | bytes 1572872 | tf_op jit(solution)/shard_map/ppermute | solution.py:42
  14.8 12.1 %collective-permute-start.8 = (bf16[8,128,256]{2,1,0:T(8,128)(2,1)S(1)}, bf16[8,128,256]{2,1,0:T(8,128)(2,1)S(1)}, u32[]{:S(2)}, u32[]{:S(2)}) collective-permute-start(bf16[8,128,256]{2,1,0:T(8,128)(2,1)S(1)} %pad_maximum_fusion.set0), channel_id=1, source_target_pairs={{0,6},{1,25},{2,0},{3,27},{4,2},{5,29},{6,4},{7,31},{8,14},{9,1},{... | collective-permute-start | bytes 1572872 | tf_op jit(solution)/shard_map/ppermute | solution.py:42
  16.2 13.5 %collective-permute-start.9 = (bf16[8,128,256]{2,1,0:T(8,128)(2,1)S(1)}, bf16[8,128,256]{2,1,0:T(8,128)(2,1)S(1)}, u32[]{:S(2)}, u32[]{:S(2)}) collective-permute-start(bf16[8,128,256]{2,1,0:T(8,128)(2,1)S(1)} %pad_maximum_fusion.set0), channel_id=1, source_target_pairs={{0,4},{1,17},{2,6},{3,19},{4,0},{5,21},{6,2},{7,23},{8,12},{9,25},... | collective-permute-start | bytes 1572872 | tf_op jit(solution)/shard_map/ppermute | solution.py:42
  21.2 9.6 %collective-permute-start.10 = (bf16[256,256]{1,0:T(8,128)(2,1)S(1)}, bf16[256,256]{1,0:T(8,128)(2,1)S(1)}, u32[]{:S(2)}, u32[]{:S(2)}) collective-permute-start(bf16[256,256]{1,0:T(8,128)(2,1)S(1)} %broadcast_multiply_fusion), channel_id=1, source_target_pairs={{0,32},{1,33},{2,34},{3,35},{4,36},{5,37},{6,38},{7,39},{8,40},{9,... | collective-permute-start | bytes 393224 | tf_op jit(solution)/shard_map/ppermute | solution.py:42
  23.1 7.7 %collective-permute-start.11 = (bf16[256,256]{1,0:T(8,128)(2,1)S(1)}, bf16[256,256]{1,0:T(8,128)(2,1)S(1)}, u32[]{:S(2)}, u32[]{:S(2)}) collective-permute-start(bf16[256,256]{1,0:T(8,128)(2,1)S(1)} %broadcast_multiply_fusion), channel_id=1, source_target_pairs={{0,96},{1,97},{2,98},{3,99},{4,100},{5,101},{6,102},{7,103},{8,104... | collective-permute-start | bytes 393224 | tf_op jit(solution)/shard_map/ppermute | solution.py:42
  26.9 5.3 %collective-permute-start.12 = (bf16[256,256]{1,0:T(8,128)(2,1)S(1)}, bf16[256,256]{1,0:T(8,128)(2,1)S(1)}, u32[]{:S(2)}, u32[]{:S(2)}) collective-permute-start(bf16[256,256]{1,0:T(8,128)(2,1)S(1)} %broadcast_multiply_fusion), channel_id=1, source_target_pairs={{0,64},{1,65},{2,66},{3,67},{4,68},{5,69},{6,70},{7,71},{8,72},{9,... | collective-permute-start | bytes 393224 | tf_op jit(solution)/shard_map/ppermute | solution.py:42
  32.2 8.2 %collective-permute-start.13 = (bf16[4,128,256]{2,1,0:T(8,128)(2,1)S(1)}, bf16[4,128,256]{2,1,0:T(8,128)(2,1)S(1)}, u32[]{:S(2)}, u32[]{:S(2)}) collective-permute-start(bf16[4,128,256]{2,1,0:T(8,128)(2,1)S(1)} %shard_map.75.refs_0_), channel_id=1, source_target_pairs={{0,1},{1,0},{2,3},{3,2},{4,5},{5,4},{6,7},{7,6},{8,9},{9,8},{10,11... | collective-permute-start | bytes 786440 | tf_op jit(solution)/shard_map/ppermute | solution.py:42
  35.9 7.9 %collective-permute-start.18 = (bf16[4,128,256]{2,1,0:T(8,128)(2,1)S(1)}, bf16[4,128,256]{2,1,0:T(8,128)(2,1)S(1)}, u32[]{:S(2)}, u32[]{:S(2)}) collective-permute-start(bf16[4,128,256]{2,1,0:T(8,128)(2,1)S(1)} %shard_map.75.refs_0_), channel_id=1, source_target_pairs={{0,96},{1,97},{2,98},{3,99},{4,100},{5,101},{6,102},{7,103},{8,104... | collective-permute-start | bytes 786440 | tf_op jit(solution)/shard_map/ppermute | solution.py:42
  37.2 8.8 %collective-permute-start.19 = (bf16[4,128,256]{2,1,0:T(8,128)(2,1)S(1)}, bf16[4,128,256]{2,1,0:T(8,128)(2,1)S(1)}, u32[]{:S(2)}, u32[]{:S(2)}) collective-permute-start(bf16[4,128,256]{2,1,0:T(8,128)(2,1)S(1)} %shard_map.75.refs_0_), channel_id=1, source_target_pairs={{0,32},{1,33},{2,34},{3,35},{4,36},{5,37},{6,38},{7,39},{8,40},{9,... | collective-permute-start | bytes 786440 | tf_op jit(solution)/shard_map/ppermute | solution.py:42
  37.4 16.6 %collective-permute-start.17 = (bf16[3,256,256]{2,1,0:T(8,128)(2,1)S(1)}, bf16[3,256,256]{2,1,0:T(8,128)(2,1)S(1)}, u32[]{:S(2)}, u32[]{:S(2)}) collective-permute-start(bf16[3,256,256]{2,1,0:T(8,128)(2,1)S(1)} %pad_maximum_fusion.1.own), channel_id=1, source_target_pairs={{0,1},{1,0},{2,3},{3,2},{4,5},{5,4},{6,7},{7,6},{8,9},{9,8},{10,11... | collective-permute-start | bytes 1179656 | tf_op jit(solution)/shard_map/ppermute | solution.py:42
  46.0 8.7 %collective-permute-start.20 = (bf16[4,128,256]{2,1,0:T(8,128)(2,1)S(1)}, bf16[4,128,256]{2,1,0:T(8,128)(2,1)S(1)}, u32[]{:S(2)}, u32[]{:S(2)}) collective-permute-start(bf16[4,128,256]{2,1,0:T(8,128)(2,1)S(1)} %collective-permute-done.19.refs_0_), channel_id=1, source_target_pairs={{0,1},{1,0},{2,3},{3,2},{4,5},{5,4},{6,7},{7,6},{8,9},{9,8},{10,11... | collective-permute-start | bytes 786440 | tf_op jit(solution)/shard_map/ppermute | solution.py:42
  47.2 10.1 %collective-permute-start.21 = (bf16[4,128,256]{2,1,0:T(8,128)(2,1)S(1)}, bf16[4,128,256]{2,1,0:T(8,128)(2,1)S(1)}, u32[]{:S(2)}, u32[]{:S(2)}) collective-permute-start(bf16[4,128,256]{2,1,0:T(8,128)(2,1)S(1)} %collective-permute-done.18.refs_2_), channel_id=1, source_target_pairs={{0,1},{1,0},{2,3},{3,2},{4,5},{5,4},{6,7},{7,6},{8,9},{9,8},{10,11... | collective-permute-start | bytes 786440 | tf_op jit(solution)/shard_map/ppermute | solution.py:42
  47.2 14.1 %collective-permute-start.22 = (bf16[4,128,256]{2,1,0:T(8,128)(2,1)S(1)}, bf16[4,128,256]{2,1,0:T(8,128)(2,1)S(1)}, u32[]{:S(2)}, u32[]{:S(2)}) collective-permute-start(bf16[4,128,256]{2,1,0:T(8,128)(2,1)S(1)} %shard_map.75.refs_0_), channel_id=1, source_target_pairs={{0,64},{1,65},{2,66},{3,67},{4,68},{5,69},{6,70},{7,71},{8,72},{9,... | collective-permute-start | bytes 786440 | tf_op jit(solution)/shard_map/ppermute | solution.py:42
  47.2 14.7 %collective-permute-start.14 = (bf16[1,8,64,256]{3,2,1,0:T(8,128)(2,1)S(1)}, bf16[1,8,64,256]{3,2,1,0:T(8,128)(2,1)S(1)}, u32[]{:S(2)}, u32[]{:S(2)}) collective-permute-start(bf16[1,8,64,256]{3,2,1,0:T(8,128)(2,1)S(1)} %get-tuple-element.54), channel_id=1, source_target_pairs={{0,16},{1,5},{2,18},{3,7},{4,20},{5,1},{6,22},{7,3},{8,24},{9,13},... | collective-permute-start | bytes 786440 | tf_op jit(solution)/shard_map/ppermute | solution.py:42
  54.0 10.1 %collective-permute-start.15 = (bf16[1,8,64,256]{3,2,1,0:T(8,128)(2,1)S(1)}, bf16[1,8,64,256]{3,2,1,0:T(8,128)(2,1)S(1)}, u32[]{:S(2)}, u32[]{:S(2)}) collective-permute-start(bf16[1,8,64,256]{3,2,1,0:T(8,128)(2,1)S(1)} %get-tuple-element.55), channel_id=1, source_target_pairs={{0,8},{1,3},{2,10},{3,5},{4,12},{5,7},{6,14},{7,1},{8,16},{9,11},{... | collective-permute-start | bytes 786440 | tf_op jit(solution)/shard_map/ppermute | solution.py:42
  54.7 9.3 %collective-permute-start.16 = (bf16[1,8,64,256]{3,2,1,0:T(8,128)(2,1)S(1)}, bf16[1,8,64,256]{3,2,1,0:T(8,128)(2,1)S(1)}, u32[]{:S(2)}, u32[]{:S(2)}) collective-permute-start(bf16[1,8,64,256]{3,2,1,0:T(8,128)(2,1)S(1)} %get-tuple-element.56), channel_id=1, source_target_pairs={{0,24},{1,7},{2,26},{3,1},{4,28},{5,3},{6,30},{7,5},{8,0},{9,15},{... | collective-permute-start | bytes 786440 | tf_op jit(solution)/shard_map/ppermute | solution.py:42
  61.2 10.8 %collective-permute-start.23 = (bf16[2,8,64,256]{3,2,1,0:T(8,128)(2,1)S(1)}, bf16[2,8,64,256]{3,2,1,0:T(8,128)(2,1)S(1)}, u32[]{:S(2)}, u32[]{:S(2)}) collective-permute-start(bf16[2,8,64,256]{3,2,1,0:T(8,128)(2,1)S(1)} %get-tuple-element.63), channel_id=1, source_target_pairs={{0,16},{1,5},{2,18},{3,7},{4,20},{5,1},{6,22},{7,3},{8,24},{9,13},... | collective-permute-start | bytes 1572872 | tf_op jit(solution)/shard_map/ppermute | solution.py:42
  61.3 15.2 %collective-permute-start.24 = (bf16[2,8,64,256]{3,2,1,0:T(8,128)(2,1)S(1)}, bf16[2,8,64,256]{3,2,1,0:T(8,128)(2,1)S(1)}, u32[]{:S(2)}, u32[]{:S(2)}) collective-permute-start(bf16[2,8,64,256]{3,2,1,0:T(8,128)(2,1)S(1)} %get-tuple-element.62), channel_id=1, source_target_pairs={{0,8},{1,3},{2,10},{3,5},{4,12},{5,7},{6,14},{7,1},{8,16},{9,11},{... | collective-permute-start | bytes 1572872 | tf_op jit(solution)/shard_map/ppermute | solution.py:42
  61.9 14.7 %collective-permute-start.25 = (bf16[2,8,64,256]{3,2,1,0:T(8,128)(2,1)S(1)}, bf16[2,8,64,256]{3,2,1,0:T(8,128)(2,1)S(1)}, u32[]{:S(2)}, u32[]{:S(2)}) collective-permute-start(bf16[2,8,64,256]{3,2,1,0:T(8,128)(2,1)S(1)} %get-tuple-element.64), channel_id=1, source_target_pairs={{0,24},{1,7},{2,26},{3,1},{4,28},{5,3},{6,30},{7,5},{8,0},{9,15},{... | collective-permute-start | bytes 1572872 | tf_op jit(solution)/shard_map/ppermute | solution.py:42
  67.6 11.8 %collective-permute-start.27 = (bf16[1,8,64,256]{3,2,1,0:T(8,128)(2,1)S(1)}, bf16[1,8,64,256]{3,2,1,0:T(8,128)(2,1)S(1)}, u32[]{:S(2)}, u32[]{:S(2)}) collective-permute-start(bf16[1,8,64,256]{3,2,1,0:T(8,128)(2,1)S(1)} %get-tuple-element.72), channel_id=1, source_target_pairs={{0,16},{1,5},{2,18},{3,7},{4,20},{5,1},{6,22},{7,3},{8,24},{9,13},... | collective-permute-start | bytes 786440 | tf_op jit(solution)/shard_map/ppermute | solution.py:42
  71.5 10.3 %collective-permute-start.28 = (bf16[1,8,64,256]{3,2,1,0:T(8,128)(2,1)S(1)}, bf16[1,8,64,256]{3,2,1,0:T(8,128)(2,1)S(1)}, u32[]{:S(2)}, u32[]{:S(2)}) collective-permute-start(bf16[1,8,64,256]{3,2,1,0:T(8,128)(2,1)S(1)} %get-tuple-element.73), channel_id=1, source_target_pairs={{0,8},{1,3},{2,10},{3,5},{4,12},{5,7},{6,14},{7,1},{8,16},{9,11},{... | collective-permute-start | bytes 786440 | tf_op jit(solution)/shard_map/ppermute | solution.py:42
  72.0 9.8 %collective-permute-start.29 = (bf16[1,8,64,256]{3,2,1,0:T(8,128)(2,1)S(1)}, bf16[1,8,64,256]{3,2,1,0:T(8,128)(2,1)S(1)}, u32[]{:S(2)}, u32[]{:S(2)}) collective-permute-start(bf16[1,8,64,256]{3,2,1,0:T(8,128)(2,1)S(1)} %get-tuple-element.74), channel_id=1, source_target_pairs={{0,24},{1,7},{2,26},{3,1},{4,28},{5,3},{6,30},{7,5},{8,0},{9,15},{... | collective-permute-start | bytes 786440 | tf_op jit(solution)/shard_map/ppermute | solution.py:42
  82.1 7.2 %collective-permute-start.30 = (bf16[4,8,16,256]{3,2,1,0:T(8,128)(2,1)S(1)}, bf16[4,8,16,256]{3,2,1,0:T(8,128)(2,1)}, u32[]{:S(2)}, u32[]{:S(2)}) collective-permute-start(bf16[4,8,16,256]{3,2,1,0:T(8,128)(2,1)S(1)} %pad_maximum_fusion.2), channel_id=1, source_target_pairs={{0,4},{1,17},{2,6},{3,19},{4,0},{5,21},{6,2},{7,23},{8,12},{9,25},... | collective-permute-start | bytes 786440 | tf_op jit(solution)/shard_map/ppermute | solution.py:42
  84.2 7.9 %collective-permute-start.31 = (bf16[4,8,16,256]{3,2,1,0:T(8,128)(2,1)S(1)}, bf16[4,8,16,256]{3,2,1,0:T(8,128)(2,1)}, u32[]{:S(2)}, u32[]{:S(2)}) collective-permute-start(bf16[4,8,16,256]{3,2,1,0:T(8,128)(2,1)S(1)} %pad_maximum_fusion.3), channel_id=1, source_target_pairs={{0,2},{1,9},{2,4},{3,11},{4,6},{5,13},{6,0},{7,15},{8,10},{9,17},{... | collective-permute-start | bytes 786440 | tf_op jit(solution)/shard_map/ppermute | solution.py:42
  85.5 6.8 %collective-permute-start.32 = (bf16[4,8,16,256]{3,2,1,0:T(8,128)(2,1)S(1)}, bf16[4,8,16,256]{3,2,1,0:T(8,128)(2,1)}, u32[]{:S(2)}, u32[]{:S(2)}) collective-permute-start(bf16[4,8,16,256]{3,2,1,0:T(8,128)(2,1)S(1)} %pad_maximum_fusion.4), channel_id=1, source_target_pairs={{0,6},{1,25},{2,0},{3,27},{4,2},{5,29},{6,4},{7,31},{8,14},{9,1},{... | collective-permute-start | bytes 786440 | tf_op jit(solution)/shard_map/ppermute | solution.py:42
  93.6 4.7 %collective-permute-start.33 = (bf16[8,16,256]{2,1,0:T(8,128)(2,1)S(1)}, bf16[8,16,256]{2,1,0:T(8,128)(2,1)S(1)}, u32[]{:S(2)}, u32[]{:S(2)}) collective-permute-start(bf16[8,16,256]{2,1,0:T(8,128)(2,1)S(1)} %get-tuple-element.89), channel_id=1, source_target_pairs={{0,64},{1,65},{2,66},{3,67},{4,68},{5,69},{6,70},{7,71},{8,72},{9,... | collective-permute-start | bytes 196616 | tf_op jit(solution)/shard_map/ppermute | solution.py:42
  96.6 4.3 %collective-permute-start.35 = (bf16[8,16,256]{2,1,0:T(8,128)(2,1)S(1)}, bf16[8,16,256]{2,1,0:T(8,128)(2,1)S(1)}, u32[]{:S(2)}, u32[]{:S(2)}) collective-permute-start(bf16[8,16,256]{2,1,0:T(8,128)(2,1)S(1)} %get-tuple-element.87), channel_id=1, source_target_pairs={{0,32},{1,33},{2,34},{3,35},{4,36},{5,37},{6,38},{7,39},{8,40},{9,... | collective-permute-start | bytes 196616 | tf_op jit(solution)/shard_map/ppermute | solution.py:42
  101.1 6.0 %collective-permute-start.36 = (bf16[4,8,16,128]{3,2,1,0:T(8,128)(2,1)S(1)}, bf16[4,8,16,128]{3,2,1,0:T(8,128)(2,1)S(1)}, u32[]{:S(2)}, u32[]{:S(2)}) collective-permute-start(bf16[4,8,16,128]{3,2,1,0:T(8,128)(2,1)S(1)} %get-tuple-element.85), channel_id=1, source_target_pairs={{0,1},{1,0},{2,3},{3,2},{4,5},{5,4},{6,7},{7,6},{8,9},{9,8},{10,11... | collective-permute-start | bytes 393224 | tf_op jit(solution)/shard_map/ppermute | solution.py:42
  (6 other events, 33.0 us)
